TPU v7x, 32 devices: a whole 2x2x4 slice. The times are simulated.
32 devices in a mesh: row: 8 (over y, x, core), col: 4 (over z).
Axes of the slice: x: 2, y: 2, z: 4, core: 2. Of those that a mesh axis runs over, the one named last changes fastest.
Arguments:
- activations: bfloat16 [256, 16384], P('col', 'row'), may hold values from -6 to 6
- grad_out: bfloat16 [256, 16384], P('col', 'row'), may hold values from -1.5 to 1.5
- first_blocks: bfloat16 [8, 4, 384, 128, 128], P('row', 'col'), may hold values from -0.125 to 0.125
- first_coords: int32 [8, 4, 384, 2], P('row', 'col'), may hold values from -1 to 511, as said below
- second_blocks: bfloat16 [4, 8, 384, 128, 128], P('col', 'row'), may hold values from -0.0625 to 0.0625
- second_coords: int32 [4, 8, 384, 2], P('col', 'row'), may hold values from -1 to 511, as said below
Outputs:
- output: float32 [256, 16384], P('col', 'row')
- grad_input: float32 [256, 16384], P('col', 'row')
- grad_first: bfloat16 [8, 4, 384, 128, 128], P('row', 'col')
- grad_second: bfloat16 [4, 8, 384, 128, 128], P('col', 'row')
Inputs may be any that keep to these rules, and one draw needn't show every extreme that they name: `first_coords`: tile [a, b] lists, once each, exactly the nonzero blocks of W1 whose block row lies in a * 16 to a * 16 + 15 and whose block column lies in b * 128 to b * 128 + 127, in increasing order of block row and then block column; the remaining of its 384 slots hold -1 in both coordinates. Some tile fills all 384 slots. `second_coords`: tile [a, b] lists, once each, exactly the nonzero blocks of W2 whose block row lies in a * 128 to a * 128 + 127 and whose block column lies in b * 16 to b * 16 + 15, in increasing order of block row and then block column; the remaining of its 384 slots hold -1 in both coordinates. Some tile fills all 384 slots.
All inputs are finite; a program needn't handle non-finite values.
Results may differ from a plain program's by a relative error of at most 0.005.
Values may be sent and summed in bfloat16 or wider, within the bound.
A program may use at most 320 MiB of HBM per device.

v0:
```python
import functools
import math

import jax
import jax.numpy as jnp
from jax import lax
from jax.experimental import pallas as pl
from jax.experimental.pallas import tpu as pltpu
from jax.sharding import PartitionSpec as P

FF = 65536
CHUNK = 32
VMEM_LIMIT = 58 * 1024 * 1024


def gelu_tanh(values):
    return jax.nn.gelu(values, approximate=True)


def contract(left, right, left_dim, right_dim):
    return lax.dot_general(
        left, right, (((left_dim,), (right_dim,)), ((), ())), preferred_element_type=jnp.float32
    )


def lanes(ref, index, width):
    return ref[:, pl.ds(pl.multiple_of(index * width, width), width)]


def to_hidden_kernel(flipped, source, target, panel, weights, keep, send, totals):
    step = pl.program_id(0)
    segments = totals.shape[0] - 1
    half = segments // 2
    width = weights.shape[-1]

    @pl.when(step == 0)
    def _():
        def clear(index, carry):
            totals[index] = jnp.zeros(totals.shape[1:], jnp.float32)
            return carry

        lax.fori_loop(0, segments, clear, 0)

    for slot in range(CHUNK):
        k = step * CHUNK + slot
        term = contract(
            lanes(panel, source[k], width), weights[slot], 1, 1 if flipped else 0
        )
        totals[target[k]] += term

    @pl.when(step == pl.num_programs(0) - 1)
    def _():
        def write(index, carry):
            keep[index] = totals[index]
            send[index] = totals[half + index].astype(jnp.bfloat16)
            return carry

        lax.fori_loop(0, half, write, 0)


def to_hidden(panel, weights, source, target, segments, flipped):
    tokens = panel.shape[0]
    slots, width, _ = weights.shape
    half = segments // 2
    return pl.pallas_call(
        functools.partial(to_hidden_kernel, flipped),
        grid_spec=pltpu.PrefetchScalarGridSpec(
            num_scalar_prefetch=2,
            grid=(slots // CHUNK,),
            in_specs=[
                pl.BlockSpec(panel.shape, lambda s, a, b: (0, 0)),
                pl.BlockSpec((CHUNK, width, width), lambda s, a, b: (s, 0, 0)),
            ],
            out_specs=[pl.BlockSpec((half, tokens, width), lambda s, a, b: (0, 0, 0))] * 2,
            scratch_shapes=[pltpu.VMEM((segments + 1, tokens, width), jnp.float32)],
        ),
        out_shape=[
            jax.ShapeDtypeStruct((half, tokens, width), jnp.float32),
            jax.ShapeDtypeStruct((half, tokens, width), jnp.bfloat16),
        ],
        compiler_params=pltpu.CompilerParams(vmem_limit_bytes=VMEM_LIMIT),
        cost_estimate=pl.CostEstimate(
            flops=8 * slots * tokens * width * width,
            bytes_accessed=2 * weights.size + 6 * half * tokens * width,
            transcendentals=0,
        ),
    )(source, target, panel, weights)


def fetch(parts, hidden, sems):
    copies = []
    start = 0
    for number, part in enumerate(parts):
        count = part.shape[0]
        copies.append(pltpu.make_async_copy(part, hidden.at[pl.ds(start, count)], sems.at[number]))
        copies[-1].start()
        start += count
    for copy in copies:
        copy.wait()


def to_model_kernel(transposed, pieces, with_sums, with_grads, model_at, hidden_at, live, *refs):
    refs = list(refs)
    panel = refs.pop(0) if with_grads else None
    weights = refs.pop(0) if with_sums else None
    hidden_parts = [refs.pop(0) for _ in range(pieces)]
    grads = refs.pop(0) if with_grads else None
    own, send, totals = [refs.pop(0) for _ in range(3)] if with_sums else (None, None, None)
    hidden, sems = refs
    step = pl.program_id(0)
    width = hidden.shape[-1]

    @pl.when(step == 0)
    def _():
        if with_sums:
            totals[...] = jnp.zeros(totals.shape, jnp.float32)
        fetch(hidden_parts, hidden, sems)

    for slot in range(CHUNK):
        k = step * CHUNK + slot
        model = model_at[k]
        values = hidden[hidden_at[k]]
        is_live = live[k] > 0
        if with_sums:
            term = contract(values, weights[slot], 1, 1 if transposed else 0)
            totals[jnp.where(is_live, model, totals.shape[0] - 1)] += term
        if with_grads:
            other = lanes(panel, model, width)
            if transposed:
                grad = contract(other, values, 0, 0)
            else:
                grad = contract(values, other, 0, 0)
            grads[slot] = jnp.where(is_live, grad, 0.0).astype(jnp.bfloat16)

    if with_sums:

        @pl.when(step == pl.num_programs(0) - 1)
        def _():
            share = own.shape[0]
            for segment in range(totals.shape[0] - 1):
                columns = pl.ds(segment * width, width)
                own[:, columns] = totals[segment, pl.ds(0, share), :]
                for number, piece in enumerate(send):
                    rows = pl.ds((number + 1) * share, share)
                    piece[:, columns] = totals[segment, rows, :].astype(jnp.bfloat16)


def to_model(
    panel, hidden_parts, weights, places, members, transposed, with_sums=True, with_grads=True
):
    tokens, columns = panel.shape
    slots, width, _ = weights.shape
    segments = columns // width
    share = tokens // members
    hidden_count = sum(part.shape[0] for part in hidden_parts)
    pieces = len(hidden_parts)
    chunk_spec = pl.BlockSpec((CHUNK, width, width), lambda s, a, b, c: (s, 0, 0))
    share_spec = pl.BlockSpec((share, columns), lambda s, a, b, c: (0, 0))
    operands, in_specs, out_specs, out_shape, scratch = [], [], [], [], []
    if with_grads:
        operands.append(panel)
        in_specs.append(pl.BlockSpec(panel.shape, lambda s, a, b, c: (0, 0)))
        out_specs.append(chunk_spec)
        out_shape.append(jax.ShapeDtypeStruct(weights.shape, jnp.bfloat16))
    if with_sums:
        operands.append(weights)
        in_specs.append(chunk_spec)
        out_specs += [share_spec, [share_spec] * (members - 1)]
        out_shape += [
            jax.ShapeDtypeStruct((share, columns), jnp.float32),
            [jax.ShapeDtypeStruct((share, columns), jnp.bfloat16)] * (members - 1),
        ]
        scratch.append(pltpu.VMEM((segments + 1, tokens, width), jnp.float32))
    scratch += [
        pltpu.VMEM((hidden_count, tokens, width), jnp.bfloat16),
        pltpu.SemaphoreType.DMA((pieces,)),
    ]

    def kernel(*refs):
        flat = list(refs)
        if with_sums:
            start = 3 + len(operands) + pieces + (1 if with_grads else 0) + 1
            if not isinstance(flat[start], (list, tuple)):
                flat[start : start + members - 1] = [flat[start : start + members - 1]]
        to_model_kernel(transposed, pieces, with_sums, with_grads, *flat)

    return pl.pallas_call(
        kernel,
        grid_spec=pltpu.PrefetchScalarGridSpec(
            num_scalar_prefetch=3,
            grid=(slots // CHUNK,),
            in_specs=in_specs + [pl.BlockSpec(memory_space=pl.ANY)] * pieces,
            out_specs=out_specs,
            scratch_shapes=scratch,
        ),
        out_shape=out_shape,
        compiler_params=pltpu.CompilerParams(vmem_limit_bytes=VMEM_LIMIT),
        cost_estimate=pl.CostEstimate(
            flops=8 * slots * tokens * width * width * (with_sums + with_grads),
            bytes_accessed=4 * weights.size + 2 * hidden_count * tokens * width,
            transcendentals=0,
        ),
    )(*places, *operands, *hidden_parts)


def swap(values, bit):
    count = lax.axis_size("row")
    return lax.ppermute(values, "row", [(s, s ^ (1 << bit)) for s in range(count)])


def swap_orders():
    rest = list(range(1, int(math.log2(lax.axis_size("row")))))
    return [rest, rest[::-1]]


def hidden_position(index, segments):
    level = int(math.log2(segments))
    row = lax.axis_index("row")
    masks = []
    for order in swap_orders():
        mask = (row & 1) << (level - 1)
        for number, bit in enumerate(order):
            mask = mask | (((row >> bit) & 1) << (level - 3 - number))
        masks.append(mask)
    is_late = ((index >> (level - 2)) & 1) > 0
    return index ^ jnp.where(is_late, masks[1], masks[0])


def after(values, *earlier):
    return lax.optimization_barrier((values, earlier))[0]


def added(terms, start, count):
    total = None
    for array, base in terms:
        piece = array[base + start : base + start + count].astype(jnp.float32)
        total = piece if total is None else total + piece
    return total


def scatter_begin(keep, send, *earlier):
    arrived = swap(send, 0)
    quarter = keep.shape[0] // 2
    half = quarter // 2
    parts = [[(keep, n * quarter), (arrived, n * quarter)] for n in range(2)]
    sent = [added(terms, half, half).astype(jnp.bfloat16) for terms in parts]
    outgoing = after(sent, *earlier) if earlier else sent
    return parts, sent, [swap(v, order[0]) for v, order in zip(outgoing, swap_orders())]


def scatter_end(parts, arrived):
    results = []
    for terms, first, order in zip(parts, arrived, swap_orders()):
        terms = terms + [(first, 0)]
        half = first.shape[0]
        for bit in order[1:]:
            half = half // 2
            terms.append((swap(added(terms, half, half).astype(jnp.bfloat16), bit), 0))
        results.append(added(terms, 0, half))
    return results


def gather_near(parts):
    pairs = []
    for part, order in zip(parts, swap_orders()):
        stages = order[::-1]
        for bit in stages[:-1]:
            part = jnp.concatenate([part, swap(part, bit)], axis=0)
        pairs.append((part, swap(part, stages[-1])))
    return pairs


def gather_far(pairs, *earlier):
    far = []
    for first, second in pairs:
        late = after(second, *earlier) if earlier else second
        far += [swap(first, 0), swap(late, 0)]
    return [piece for pair in pairs for piece in pair] + far


def shift(values, distance):
    count = lax.axis_size("col")
    return lax.ppermute(values, "col", [(s, (s + distance) % count) for s in range(count)])


def gather_tokens(values):
    count = lax.axis_size("col")
    return jnp.concatenate([values] + [shift(values, -d) for d in range(1, count)], axis=0)


def scatter_tokens(own, send):
    total = own
    for number, piece in enumerate(send):
        total = total + shift(piece, number + 1).astype(jnp.float32)
    return total


def body(activations, grad_out, first_blocks, first_coords, second_blocks, second_coords):
    width = first_blocks.shape[-1]
    members = lax.axis_size("col")
    row_tiles = activations.shape[1] // width
    col_tiles = FF // width // members
    row_base = lax.axis_index("row") * row_tiles
    col_base = lax.axis_index("col") * col_tiles

    def fields(model, hidden):
        is_live = model >= 0
        model_at = jnp.where(is_live, model - row_base, 0)
        hidden_at = jnp.where(is_live, hidden_position(hidden - col_base, col_tiles), 0)
        target = jnp.where(is_live, hidden_at, col_tiles)
        return model_at, hidden_at, target, is_live.astype(jnp.int32)

    model_one, hidden_one, target_one, live_one = fields(
        first_coords[0, 0, :, 0], first_coords[0, 0, :, 1]
    )
    model_two, hidden_two, target_two, live_two = fields(
        second_coords[0, 0, :, 1], second_coords[0, 0, :, 0]
    )
    weights_one = first_blocks[0, 0]
    weights_two = second_blocks[0, 0]

    inputs_all = gather_tokens(activations)
    cotangent_all = gather_tokens(after(grad_out, inputs_all))
    pre_keep, pre_send = to_hidden(
        inputs_all, weights_one, model_one, target_one, col_tiles, False
    )
    pre_terms, pre_sent, pre_arrived = scatter_begin(pre_keep, after(pre_send, cotangent_all))
    back_keep, back_send = to_hidden(
        after(cotangent_all, *pre_sent), weights_two, model_two, target_two, col_tiles, True
    )
    pre_parts = scatter_end(pre_terms, pre_arrived)
    back_terms, _, back_arrived = scatter_begin(
        back_keep, after(back_send, *pre_arrived), *pre_parts
    )
    hidden_own, gelu_backs = [], []
    for pre in pre_parts:
        hidden_full, gelu_back = jax.vjp(gelu_tanh, pre)
        hidden_own.append(hidden_full.astype(jnp.bfloat16))
        gelu_backs.append(gelu_back)
    hidden_near = gather_near(hidden_own)
    back_parts = scatter_end(back_terms, after(back_arrived, *[pair[0] for pair in hidden_near]))
    grad_pre_own = [
        gelu_back(back)[0].astype(jnp.bfloat16) for gelu_back, back in zip(gelu_backs, back_parts)
    ]
    hidden_parts = gather_far(hidden_near)
    grad_pre_near = gather_near(after(grad_pre_own, *hidden_near))
    grad_second, own_out, send_out = to_model(
        cotangent_all, hidden_parts, weights_two, (model_two, hidden_two, live_two), members, False
    )
    grad_pre_parts = gather_far(grad_pre_near, own_out)
    output = scatter_tokens(own_out, after(send_out, *grad_pre_parts))
    places_one = (model_one, hidden_one, live_one)
    own_in, send_in = to_model(
        inputs_all,
        grad_pre_parts,
        weights_one,
        places_one,
        members,
        True,
        with_grads=False,
    )
    grad_input = scatter_tokens(own_in, send_in)
    (grad_first,) = to_model(
        inputs_all,
        after(grad_pre_parts, own_in, output),
        weights_one,
        places_one,
        members,
        True,
        with_sums=False,
    )
    return (output, grad_input, grad_first[None, None], grad_second[None, None])


def solution(mesh):
    return jax.shard_map(
        body,
        mesh=mesh,
        in_specs=(
            P("col", "row"),
            P("col", "row"),
            P("row", "col", None, None, None),
            P("row", "col", None, None),
            P("col", "row", None, None, None),
            P("col", "row", None, None),
        ),
        out_specs=(
            P("col", "row"),
            P("col", "row"),
            P("row", "col", None, None, None),
            P("col", "row", None, None, None),
        ),
        check_vma=False,
    )
```

profile of v0, /device:TPU:12, one launch (start us, length us, event | category | flops | bytes accessed | tf_op | source)
XLA Modules:
  0.0 306.8 jit_solution(6321635159410261474)
XLA Ops:
  0.6 0.5 collective-permute-start
  1.1 2.6 collective-permute-start.1
  3.7 2.5 collective-permute-start.2
  6.2 1.0 constant_dynamic-update-slice_fusion.3
  7.2 0.8 subtract_reduce_fusion
  8.0 0.7 compare_reduce_fusion
  8.7 0.6 broadcast_select_fusion.1
  9.3 12.0 %collective-permute-done = bf16[64,2048]{1,0:T(8,128)(2,1)S(1)} collective-permute-done((bf16[64,2048]{1,0:T(8,128)(2,1)}, bf16[64,2048]{1,0:T(8,128)(2,1)S(1)}, u32[]{:S(2)}, u32[]{:S(2)}) %collective-permute-start) | collective-permute-done | bytes 262176 | tf_op jit(solution)/shard_map/ppermute | solution.py:283
  21.5 4.7 %collective-permute-done.2 = bf16[64,2048]{1,0:T(8,128)(2,1)S(1)} collective-permute-done((bf16[64,2048]{1,0:T(8,128)(2,1)}, bf16[64,2048]{1,0:T(8,128)(2,1)S(1)}, u32[]{:S(2)}, u32[]{:S(2)}) %collective-permute-start.2) | collective-permute-done | bytes 262176 | tf_op jit(solution)/shard_map/ppermute | solution.py:283
  26.2 1.1 collective-permute-start.3
  27.4 2.8 collective-permute-start.4
  30.2 22.4 %shard_map.93 = (f32[64,256,128]{2,1,0:T(8,128)}, bf16[64,256,128]{2,1,0:T(8,128)(2,1)}) custom-call(s32[384]{0:T(512)} %get-tuple-element.95.source.refs_0_, s32[384]{0:T(512)} %get-tuple-element.86.target, bf16[256,2048]{1,0:T(8,128)(2,1)} %copy-done.8, bf16[384,128,128]{2,1,0:T(8,128)(2,1)} %bitcast.6), custom_call_target="tpu_custom_call" | custom-call | flops 12884901888 | bytes 25165824 | tf_op jit(solution)/shard_map/pallas_call | solution.py:65
  52.8 0.7 broadcast_select_fusion
  53.5 6.6 %collective-permute-done.6 = bf16[64,256,128]{2,1,0:T(8,128)(2,1)S(1)} collective-permute-done((bf16[64,256,128]{2,1,0:T(8,128)(2,1)}, bf16[64,256,128]{2,1,0:T(8,128)(2,1)S(1)}, u32[]{:S(2)}, u32[]{:S(2)}) %collective-permute-start.6) | collective-permute-done | bytes 4194336 | tf_op jit(solution)/shard_map/ppermute | solution.py:208
  60.1 4.3 %add_convert_fusion.2 = (bf16[16,256,128]{2,1,0:T(8,128)(2,1)}, bf16[16,256,128]{2,1,0:T(8,128)(2,1)}) fusion(f32[64,256,128]{2,1,0:T(8,128)} %get-tuple-element.41, bf16[64,256,128]{2,1,0:T(8,128)(2,1)S(1)} %collective-permute-done.6), kind=kLoop, calls=%fused_computation.2 | loop fusion | flops 3145728 | bytes 8388608 | tf_op jit(solution)/shard_map/convert_element_type | solution.py:246
  64.7 1.7 collective-permute-start.7
  66.4 22.1 %shard_map.95 = (f32[64,256,128]{2,1,0:T(8,128)}, bf16[64,256,128]{2,1,0:T(8,128)(2,1)}) custom-call(s32[384]{0:T(512)} %get-tuple-element.96.refs_0_.source, s32[384]{0:T(512)} %get-tuple-element.80.target, bf16[256,2048]{1,0:T(8,128)(2,1)} %copy-done.9, bf16[384,128,128]{2,1,0:T(8,128)(2,1)} %bitcast.4), custom_call_target="tpu_custom_call" | custom-call | flops 12884901888 | bytes 25165824 | tf_op jit(solution)/shard_map/pallas_call | solution.py:65
  88.5 1.4 collective-permute-done.11
  90.0 1.4 add_convert_fusion.6
  91.4 1.7 collective-permute-start.12
  93.1 12.7 %collective-permute-done.12 = bf16[8,256,128]{2,1,0:T(8,128)(2,1)S(1)} collective-permute-done((bf16[8,256,128]{2,1,0:T(8,128)(2,1)S(1)}, bf16[8,256,128]{2,1,0:T(8,128)(2,1)S(1)}, u32[]{:S(2)}, u32[]{:S(2)}) %collective-permute-start.12) | collective-permute-done | bytes 524320 | tf_op jit(solution)/shard_map/ppermute | solution.py:208
  105.8 2.4 multiply_convert_fusion
  108.2 1.8 collective-permute-start.8
  110.0 11.9 %collective-permute-done.8 = bf16[8,256,128]{2,1,0:T(8,128)(2,1)S(1)} collective-permute-done((bf16[8,256,128]{2,1,0:T(8,128)(2,1)S(1)}, bf16[8,256,128]{2,1,0:T(8,128)(2,1)S(1)}, u32[]{:S(2)}, u32[]{:S(2)}) %collective-permute-start.8) | collective-permute-done | bytes 524320 | tf_op jit(solution)/shard_map/ppermute | solution.py:208
  121.8 1.9 multiply_convert_fusion.1
  123.8 0.6 add_convert_fusion
  124.5 1.7 collective-permute-start.20
  126.2 1.4 collective-permute-start.21
  127.6 0.7 collective-permute-start.13
  128.6 31.1 %collective-permute-done.13 = bf16[8,256,128]{2,1,0:T(8,128)(2,1)S(1)} collective-permute-done((bf16[8,256,128]{2,1,0:T(8,128)(2,1)S(1)}, bf16[8,256,128]{2,1,0:T(8,128)(2,1)S(1)}, u32[]{:S(2)}, u32[]{:S(2)}) %collective-permute-start.13) | collective-permute-done | bytes 524320 | tf_op jit(solution)/shard_map/ppermute | solution.py:208
  159.8 1.3 collective-permute-done.9
  161.8 1.6 collective-permute-start.14
  163.5 1.3 collective-permute-start.10
  164.8 11.5 %collective-permute-done.23 = bf16[8,256,128]{2,1,0:T(8,128)(2,1)S(1)} collective-permute-done((bf16[8,256,128]{2,1,0:T(8,128)(2,1)S(1)}, bf16[8,256,128]{2,1,0:T(8,128)(2,1)S(1)}, u32[]{:S(2)}, u32[]{:S(2)}) %collective-permute-start.23) | collective-permute-done | bytes 524320 | tf_op jit(solution)/shard_map/ppermute | solution.py:208
  176.3 1.1 fusion.13
  177.4 1.4 collective-permute-start.22
  178.8 16.9 %collective-permute-done.22 = bf16[8,256,128]{2,1,0:T(8,128)(2,1)S(1)} collective-permute-done((bf16[8,256,128]{2,1,0:T(8,128)(2,1)S(1)}, bf16[8,256,128]{2,1,0:T(8,128)(2,1)S(1)}, u32[]{:S(2)}, u32[]{:S(2)}) %collective-permute-start.22) | collective-permute-done | bytes 524320 | tf_op jit(solution)/shard_map/ppermute | solution.py:208
  195.8 0.9 fusion.6
  196.8 1.4 collective-permute-start.26
  198.2 0.5 collective-permute-start.15
  199.2 8.2 %collective-permute-done.26 = bf16[8,256,128]{2,1,0:T(8,128)(2,1)S(1)} collective-permute-done((bf16[8,256,128]{2,1,0:T(8,128)(2,1)S(1)}, bf16[8,256,128]{2,1,0:T(8,128)(2,1)S(1)}, u32[]{:S(2)}, u32[]{:S(2)}) %collective-permute-start.26) | collective-permute-done | bytes 524320 | tf_op jit(solution)/shard_map/ppermute | solution.py:208
  207.4 1.1 collective-permute-start.24
  208.4 0.6 convert_element_type.132.refs_2_
  209.2 10.2 %collective-permute-done.24 = bf16[8,256,128]{2,1,0:T(8,128)(2,1)S(1)} collective-permute-done((bf16[8,256,128]{2,1,0:T(8,128)(2,1)S(1)}, bf16[8,256,128]{2,1,0:T(8,128)(2,1)S(1)}, u32[]{:S(2)}, u32[]{:S(2)}) %collective-permute-start.24) | collective-permute-done | bytes 524320 | tf_op jit(solution)/shard_map/ppermute | solution.py:208
  219.5 1.1 collective-permute-start.27
  220.6 1.4 collective-permute-start.25
  222.1 1.0 copy-done.20
  223.4 1.0 copy-done.22
  224.3 24.9 %shard_map.94 = (bf16[384,128,128]{2,1,0:T(8,128)(2,1)}, f32[64,2048]{1,0:T(8,128)}, bf16[64,2048]{1,0:T(8,128)(2,1)}, bf16[64,2048]{1,0:T(8,128)(2,1)}, bf16[64,2048]{1,0:T(8,128)(2,1)}) custom-call(s32[384]{0:T(512)} %get-tuple-element.96.refs_0_.source, s32[384]{0:T(512)} %get-tuple-element.81.refs_1_, s32[384]{0:T(512)} %convert_element_type.132.refs_2_, ...), custom_call_target="tpu_custom_call" | custom-call | flops 25769803776 | bytes 33554432 | tf_op jit(solution)/shard_map/pallas_call | solution.py:187
  250.3 0.8 convert_element_type.172.refs_2_
  251.1 0.8 collective-permute-done.30.refs_10_
  252.0 1.5 collective-permute-done.28.refs_8_
  253.5 1.5 collective-permute-done.31.refs_11_
  255.0 1.5 collective-permute-done.29.refs_9_
  256.5 1.1 collective-permute-start.32
  257.6 3.3 %collective-permute-start.33 = (bf16[64,2048]{1,0:T(8,128)(2,1)}, bf16[64,2048]{1,0:T(8,128)(2,1)S(1)}, u32[]{:S(2)}, u32[]{:S(2)}) collective-permute-start(bf16[64,2048]{1,0:T(8,128)(2,1)} %get-tuple-element.61), channel_id=1, source_target_pairs={{0,2},{1,3},{2,0},{3,1},{4,6},{5,7},{6,4},{7,5},{8,10},{9,11},{10,... | collective-permute-start | bytes 786440 | tf_op jit(solution)/shard_map/ppermute | solution.py:283
  260.9 18.7 %shard_map.96 = (f32[64,2048]{1,0:T(8,128)}, bf16[64,2048]{1,0:T(8,128)(2,1)}, bf16[64,2048]{1,0:T(8,128)(2,1)}, bf16[64,2048]{1,0:T(8,128)(2,1)}) custom-call(s32[384]{0:T(512)} %get-tuple-element.95.source.refs_0_, s32[384]{0:T(512)} %get-tuple-element.87.refs_1_, s32[384]{0:T(512)} %convert_element_type.172.refs_2_, bf16[384,128,128]{2,1,0:T(8,128)(2,1)} %bitcast.7, ...), custom_call_target="tpu_custom_call" | custom-call | flops 12884901888 | bytes 33554432 | tf_op jit(solution)/shard_map/pallas_call | solution.py:187
  279.6 2.0 collective-permute-start.35
  281.6 1.8 collective-permute-start.36
  283.5 0.9 convert_add_fusion.3
  284.4 17.9 %shard_map.97 = bf16[384,128,128]{2,1,0:T(8,128)(2,1)} custom-call(s32[384]{0:T(512)} %get-tuple-element.95.source.refs_0_, s32[384]{0:T(512)} %get-tuple-element.87.refs_1_, s32[384]{0:T(512)} %convert_element_type.172.refs_2_, bf16[256,2048]{1,0:T(8,128)(2,1)} %copy-done.8, bf16[16,256,128]{2,1,0:T(8,128)(2,1)} %copy-done.5, ...), custom_call_target="tpu_custom_call" | custom-call | flops 12884901888 | bytes 33554432 | tf_op jit(solution)/shard_map/pallas_call | solution.py:187
  302.3 1.5 collective-permute-done.36
  303.9 2.1 collective-permute-done.37
  305.9 0.9 convert_add_fusion.2
  (94 shorter events, 4.4 us)
Async XLA Ops:
  0.6 20.7 %collective-permute-start = (bf16[64,2048]{1,0:T(8,128)(2,1)}, bf16[64,2048]{1,0:T(8,128)(2,1)S(1)}, u32[]{:S(2)}, u32[]{:S(2)}) collective-permute-start(bf16[64,2048]{1,0:T(8,128)(2,1)} %param.6), channel_id=1, source_target_pairs={{0,3},{1,0},{2,1},{3,2},{4,7},{5,4},{6,5},{7,6},{8,11},{9,8},{10,9... | collective-permute-start | bytes 786440 | tf_op jit(solution)/shard_map/ppermute | solution.py:283
  1.1 20.3 %collective-permute-start.1 = (bf16[64,2048]{1,0:T(8,128)(2,1)}, bf16[64,2048]{1,0:T(8,128)(2,1)S(1)}, u32[]{:S(2)}, u32[]{:S(2)}) collective-permute-start(bf16[64,2048]{1,0:T(8,128)(2,1)} %param.6), channel_id=1, source_target_pairs={{0,2},{1,3},{2,0},{3,1},{4,6},{5,7},{6,4},{7,5},{8,10},{9,11},{10,... | collective-permute-start | bytes 786440 | tf_op jit(solution)/shard_map/ppermute | solution.py:283
  3.7 22.5 %collective-permute-start.2 = (bf16[64,2048]{1,0:T(8,128)(2,1)}, bf16[64,2048]{1,0:T(8,128)(2,1)S(1)}, u32[]{:S(2)}, u32[]{:S(2)}) collective-permute-start(bf16[64,2048]{1,0:T(8,128)(2,1)} %param.6), channel_id=1, source_target_pairs={{0,1},{1,2},{2,3},{3,0},{4,5},{5,6},{6,7},{7,4},{8,9},{9,10},{10,1... | collective-permute-start | bytes 786440 | tf_op jit(solution)/shard_map/ppermute | solution.py:283
  26.2 3.9 %copy-start.8 = (bf16[256,2048]{1,0:T(8,128)(2,1)}, bf16[256,2048]{1,0:T(8,128)(2,1)S(1)}, u32[]{:S(2)}) copy-start(bf16[256,2048]{1,0:T(8,128)(2,1)S(1)} %constant_dynamic-update-slice_fusion.panel.refs_3_) | copy-start | bytes 3145732
  26.2 26.3 %collective-permute-start.3 = (bf16[64,2048]{1,0:T(8,128)(2,1)}, bf16[64,2048]{1,0:T(8,128)(2,1)S(1)}, u32[]{:S(2)}, u32[]{:S(2)}) collective-permute-start(bf16[64,2048]{1,0:T(8,128)(2,1)} %param.7), channel_id=1, source_target_pairs={{0,3},{1,0},{2,1},{3,2},{4,7},{5,4},{6,5},{7,6},{8,11},{9,8},{10,9... | collective-permute-start | bytes 786440 | tf_op jit(solution)/shard_map/ppermute | solution.py:283
  27.4 25.2 %collective-permute-start.4 = (bf16[64,2048]{1,0:T(8,128)(2,1)}, bf16[64,2048]{1,0:T(8,128)(2,1)S(1)}, u32[]{:S(2)}, u32[]{:S(2)}) collective-permute-start(bf16[64,2048]{1,0:T(8,128)(2,1)} %param.7), channel_id=1, source_target_pairs={{0,2},{1,3},{2,0},{3,1},{4,6},{5,7},{6,4},{7,5},{8,10},{9,11},{10,... | collective-permute-start | bytes 786440 | tf_op jit(solution)/shard_map/ppermute | solution.py:283
  30.1 22.5 %collective-permute-start.5 = (bf16[64,2048]{1,0:T(8,128)(2,1)}, bf16[64,2048]{1,0:T(8,128)(2,1)S(1)}, u32[]{:S(2)}, u32[]{:S(2)}) collective-permute-start(bf16[64,2048]{1,0:T(8,128)(2,1)} %param.7), channel_id=1, source_target_pairs={{0,1},{1,2},{2,3},{3,0},{4,5},{5,6},{6,7},{7,4},{8,9},{9,10},{10,1... | collective-permute-start | bytes 786440 | tf_op jit(solution)/shard_map/ppermute | solution.py:283
  30.1 22.4 %copy-start.7 = (bf16[64,2048]{1,0:T(8,128)(2,1)S(1)}, bf16[64,2048]{1,0:T(8,128)(2,1)}, u32[]{:S(2)}) copy-start(bf16[64,2048]{1,0:T(8,128)(2,1)} %param.7) | copy-start | bytes 786436
  30.1 22.6 %copy-start.10 = (s32[1,1,384,2]{2,3,1,0:T(2,128)S(1)}, s32[1,1,384,2]{2,3,1,0:T(2,128)}, u32[]{:S(2)}) copy-start(s32[1,1,384,2]{2,3,1,0:T(2,128)} %param.11) | copy-start | bytes 9220
  52.7 7.4 %copy-start.9 = (bf16[256,2048]{1,0:T(8,128)(2,1)}, bf16[256,2048]{1,0:T(8,128)(2,1)S(1)}, u32[]{:S(2)}) copy-start(bf16[256,2048]{1,0:T(8,128)(2,1)S(1)} %constant_dynamic-update-slice_fusion.4.refs_3_.panel) | copy-start | bytes 3145732
  52.7 7.4 %collective-permute-start.6 = (bf16[64,256,128]{2,1,0:T(8,128)(2,1)}, bf16[64,256,128]{2,1,0:T(8,128)(2,1)S(1)}, u32[]{:S(2)}, u32[]{:S(2)}) collective-permute-start(bf16[64,256,128]{2,1,0:T(8,128)(2,1)} %get-tuple-element.43), channel_id=1, source_target_pairs={{0,4},{4,0},{8,12},{12,8},{16,20},{20,16},{24,28},{28,24},{1,5},{5... | collective-permute-start | bytes 12582920 | tf_op jit(solution)/shard_map/ppermute | solution.py:208
  64.4 25.4 %collective-permute-start.11 = (bf16[16,256,128]{2,1,0:T(8,128)(2,1)}, bf16[16,256,128]{2,1,0:T(8,128)(2,1)S(1)}, u32[]{:S(2)}, u32[]{:S(2)}) collective-permute-start(bf16[16,256,128]{2,1,0:T(8,128)(2,1)} %get-tuple-element.93), channel_id=1, source_target_pairs={{0,16},{4,20},{8,24},{12,28},{16,0},{20,4},{24,8},{28,12},{1,17},{... | collective-permute-start | bytes 3145736 | tf_op jit(solution)/shard_map/ppermute | solution.py:208
  64.7 25.2 %collective-permute-start.7 = (bf16[16,256,128]{2,1,0:T(8,128)(2,1)}, bf16[16,256,128]{2,1,0:T(8,128)(2,1)}, u32[]{:S(2)}, u32[]{:S(2)}) collective-permute-start(bf16[16,256,128]{2,1,0:T(8,128)(2,1)} %get-tuple-element.94), channel_id=1, source_target_pairs={{0,8},{4,12},{8,0},{12,4},{16,24},{20,28},{24,16},{28,20},{1,9},{5... | collective-permute-start | bytes 3145736 | tf_op jit(solution)/shard_map/ppermute | solution.py:208
  90.0 33.8 %collective-permute-start.19 = (bf16[64,256,128]{2,1,0:T(8,128)(2,1)}, bf16[64,256,128]{2,1,0:T(8,128)(2,1)S(1)}, u32[]{:S(2)}, u32[]{:S(2)}) collective-permute-start(bf16[64,256,128]{2,1,0:T(8,128)(2,1)} %get-tuple-element.51), channel_id=1, source_target_pairs={{0,4},{4,0},{8,12},{12,8},{16,20},{20,16},{24,28},{28,24},{1,5},{5... | collective-permute-start | bytes 12582920 | tf_op jit(solution)/shard_map/ppermute | solution.py:208
  91.4 32.4 %copy-start = (f32[64,256,128]{2,1,0:T(8,128)S(1)}, f32[64,256,128]{2,1,0:T(8,128)}, u32[]{:S(2)}) copy-start(f32[64,256,128]{2,1,0:T(8,128)} %get-tuple-element.49) | copy-start | bytes 25165828
  91.4 14.4 %collective-permute-start.12 = (bf16[8,256,128]{2,1,0:T(8,128)(2,1)S(1)}, bf16[8,256,128]{2,1,0:T(8,128)(2,1)S(1)}, u32[]{:S(2)}, u32[]{:S(2)}) collective-permute-start(bf16[8,256,128]{2,1,0:T(8,128)(2,1)S(1)} %add_convert_fusion.6), channel_id=1, source_target_pairs={{0,8},{4,12},{8,0},{12,4},{16,24},{20,28},{24,16},{28,20},{1,9},{5... | collective-permute-start | bytes 1572872 | tf_op jit(solution)/shard_map/ppermute | solution.py:208
  108.2 13.6 %collective-permute-start.8 = (bf16[8,256,128]{2,1,0:T(8,128)(2,1)S(1)}, bf16[8,256,128]{2,1,0:T(8,128)(2,1)S(1)}, u32[]{:S(2)}, u32[]{:S(2)}) collective-permute-start(bf16[8,256,128]{2,1,0:T(8,128)(2,1)S(1)} %get-tuple-element.92), channel_id=1, source_target_pairs={{0,16},{4,20},{8,24},{12,28},{16,0},{20,4},{24,8},{28,12},{1,17},{... | collective-permute-start | bytes 1572872 | tf_op jit(solution)/shard_map/ppermute | solution.py:208
  124.5 36.7 %collective-permute-start.20 = (bf16[16,256,128]{2,1,0:T(8,128)(2,1)S(1)}, bf16[16,256,128]{2,1,0:T(8,128)(2,1)S(1)}, u32[]{:S(2)}, u32[]{:S(2)}) collective-permute-start(bf16[16,256,128]{2,1,0:T(8,128)(2,1)S(1)} %get-tuple-element.52), channel_id=1, source_target_pairs={{0,8},{4,12},{8,0},{12,4},{16,24},{20,28},{24,16},{28,20},{1,9},{5... | collective-permute-start | bytes 3145736 | tf_op jit(solution)/shard_map/ppermute | solution.py:208
  126.2 35.0 %collective-permute-start.21 = (bf16[16,256,128]{2,1,0:T(8,128)(2,1)S(1)}, bf16[16,256,128]{2,1,0:T(8,128)(2,1)S(1)}, u32[]{:S(2)}, u32[]{:S(2)}) collective-permute-start(bf16[16,256,128]{2,1,0:T(8,128)(2,1)S(1)} %get-tuple-element.53), channel_id=1, source_target_pairs={{0,16},{4,20},{8,24},{12,28},{16,0},{20,4},{24,8},{28,12},{1,17},{... | collective-permute-start | bytes 3145736 | tf_op jit(solution)/shard_map/ppermute | solution.py:208
  127.6 32.1 %collective-permute-start.13 = (bf16[8,256,128]{2,1,0:T(8,128)(2,1)S(1)}, bf16[8,256,128]{2,1,0:T(8,128)(2,1)S(1)}, u32[]{:S(2)}, u32[]{:S(2)}) collective-permute-start(bf16[8,256,128]{2,1,0:T(8,128)(2,1)S(1)} %get-tuple-element.82), channel_id=1, source_target_pairs={{0,8},{4,12},{8,0},{12,4},{16,24},{20,28},{24,16},{28,20},{1,9},{5... | collective-permute-start | bytes 1572872 | tf_op jit(solution)/shard_map/ppermute | solution.py:208
  128.2 32.8 %collective-permute-start.9 = (bf16[8,256,128]{2,1,0:T(8,128)(2,1)S(1)}, bf16[8,256,128]{2,1,0:T(8,128)(2,1)S(1)}, u32[]{:S(2)}, u32[]{:S(2)}) collective-permute-start(bf16[8,256,128]{2,1,0:T(8,128)(2,1)S(1)} %get-tuple-element.84), channel_id=1, source_target_pairs={{0,16},{4,20},{8,24},{12,28},{16,0},{20,4},{24,8},{28,12},{1,17},{... | collective-permute-start | bytes 1572872 | tf_op jit(solution)/shard_map/ppermute | solution.py:208
  159.8 38.4 %copy-start.1 = (bf16[16,256,128]{2,1,0:T(8,128)(2,1)}, bf16[16,256,128]{2,1,0:T(8,128)(2,1)S(1)}, u32[]{:S(2)}) copy-start(bf16[16,256,128]{2,1,0:T(8,128)(2,1)S(1)} %pad_maximum_fusion.1.refs_7_) | copy-start | bytes 3145732
  161.1 37.0 %copy-start.2 = (bf16[16,256,128]{2,1,0:T(8,128)(2,1)}, bf16[16,256,128]{2,1,0:T(8,128)(2,1)S(1)}, u32[]{:S(2)}) copy-start(bf16[16,256,128]{2,1,0:T(8,128)(2,1)S(1)} %pad_maximum_fusion.refs_5_) | copy-start | bytes 3145732
  161.4 14.9 %collective-permute-start.23 = (bf16[8,256,128]{2,1,0:T(8,128)(2,1)S(1)}, bf16[8,256,128]{2,1,0:T(8,128)(2,1)S(1)}, u32[]{:S(2)}, u32[]{:S(2)}) collective-permute-start(bf16[8,256,128]{2,1,0:T(8,128)(2,1)S(1)} %add_convert_fusion.4), channel_id=1, source_target_pairs={{0,8},{4,12},{8,0},{12,4},{16,24},{20,28},{24,16},{28,20},{1,9},{5... | collective-permute-start | bytes 1572872 | tf_op jit(solution)/shard_map/ppermute | solution.py:208
  161.8 34.9 %collective-permute-start.14 = (bf16[16,256,128]{2,1,0:T(8,128)(2,1)S(1)}, bf16[16,256,128]{2,1,0:T(8,128)(2,1)S(1)}, u32[]{:S(2)}, u32[]{:S(2)}) collective-permute-start(bf16[16,256,128]{2,1,0:T(8,128)(2,1)S(1)} %pad_maximum_fusion.1.refs_7_), channel_id=1, source_target_pairs={{0,16},{4,20},{8,24},{12,28},{16,0},{20,4},{24,8},{28,12},{1,17},{... | collective-permute-start | bytes 3145736 | tf_op jit(solution)/shard_map/ppermute | solution.py:208
  163.5 33.2 %collective-permute-start.10 = (bf16[16,256,128]{2,1,0:T(8,128)(2,1)S(1)}, bf16[16,256,128]{2,1,0:T(8,128)(2,1)S(1)}, u32[]{:S(2)}, u32[]{:S(2)}) collective-permute-start(bf16[16,256,128]{2,1,0:T(8,128)(2,1)S(1)} %pad_maximum_fusion.refs_5_), channel_id=1, source_target_pairs={{0,8},{4,12},{8,0},{12,4},{16,24},{20,28},{24,16},{28,20},{1,9},{5... | collective-permute-start | bytes 3145736 | tf_op jit(solution)/shard_map/ppermute | solution.py:208
  177.4 18.4 %collective-permute-start.22 = (bf16[8,256,128]{2,1,0:T(8,128)(2,1)S(1)}, bf16[8,256,128]{2,1,0:T(8,128)(2,1)S(1)}, u32[]{:S(2)}, u32[]{:S(2)}) collective-permute-start(bf16[8,256,128]{2,1,0:T(8,128)(2,1)S(1)} %get-tuple-element.89), channel_id=1, source_target_pairs={{0,16},{4,20},{8,24},{12,28},{16,0},{20,4},{24,8},{28,12},{1,17},{... | collective-permute-start | bytes 1572872 | tf_op jit(solution)/shard_map/ppermute | solution.py:208
  196.7 25.3 %copy-start.13 = (bf16[16,256,128]{2,1,0:T(8,128)(2,1)}, bf16[16,256,128]{2,1,0:T(8,128)(2,1)S(1)}, u32[]{:S(2)}) copy-start(bf16[16,256,128]{2,1,0:T(8,128)(2,1)S(1)} %collective-permute-done.14.refs_8_) | copy-start | bytes 3145732
  196.7 25.3 %copy-start.14 = (bf16[16,256,128]{2,1,0:T(8,128)(2,1)}, bf16[16,256,128]{2,1,0:T(8,128)(2,1)S(1)}, u32[]{:S(2)}) copy-start(bf16[16,256,128]{2,1,0:T(8,128)(2,1)S(1)} %collective-permute-done.10.refs_6_) | copy-start | bytes 3145732
  196.8 10.6 %collective-permute-start.26 = (bf16[8,256,128]{2,1,0:T(8,128)(2,1)S(1)}, bf16[8,256,128]{2,1,0:T(8,128)(2,1)S(1)}, u32[]{:S(2)}, u32[]{:S(2)}) collective-permute-start(bf16[8,256,128]{2,1,0:T(8,128)(2,1)S(1)} %get-tuple-element.57), channel_id=1, source_target_pairs={{0,8},{4,12},{8,0},{12,4},{16,24},{20,28},{24,16},{28,20},{1,9},{5... | collective-permute-start | bytes 1572872 | tf_op jit(solution)/shard_map/ppermute | solution.py:208
  198.2 22.5 %collective-permute-start.17 = (bf16[16,256,128]{2,1,0:T(8,128)(2,1)S(1)}, bf16[16,256,128]{2,1,0:T(8,128)(2,1)S(1)}, u32[]{:S(2)}, u32[]{:S(2)}) collective-permute-start(bf16[16,256,128]{2,1,0:T(8,128)(2,1)S(1)} %pad_maximum_fusion.1.refs_7_), channel_id=1, source_target_pairs={{0,4},{4,0},{8,12},{12,8},{16,20},{20,16},{24,28},{28,24},{1,5},{5... | collective-permute-start | bytes 3145736 | tf_op jit(solution)/shard_map/ppermute | solution.py:208
  198.2 23.9 %collective-permute-start.15 = (bf16[16,256,128]{2,1,0:T(8,128)(2,1)S(1)}, bf16[16,256,128]{2,1,0:T(8,128)(2,1)S(1)}, u32[]{:S(2)}, u32[]{:S(2)}) collective-permute-start(bf16[16,256,128]{2,1,0:T(8,128)(2,1)S(1)} %pad_maximum_fusion.refs_5_), channel_id=1, source_target_pairs={{0,4},{4,0},{8,12},{12,8},{16,20},{20,16},{24,28},{28,24},{1,5},{5... | collective-permute-start | bytes 3145736 | tf_op jit(solution)/shard_map/ppermute | solution.py:208
  198.7 23.4 %collective-permute-start.18 = (bf16[16,256,128]{2,1,0:T(8,128)(2,1)S(1)}, bf16[16,256,128]{2,1,0:T(8,128)(2,1)S(1)}, u32[]{:S(2)}, u32[]{:S(2)}) collective-permute-start(bf16[16,256,128]{2,1,0:T(8,128)(2,1)S(1)} %collective-permute-done.14.refs_8_), channel_id=1, source_target_pairs={{0,4},{4,0},{8,12},{12,8},{16,20},{20,16},{24,28},{28,24},{1,5},{5... | collective-permute-start | bytes 3145736 | tf_op jit(solution)/shard_map/ppermute | solution.py:208
  198.7 23.3 %collective-permute-start.16 = (bf16[16,256,128]{2,1,0:T(8,128)(2,1)S(1)}, bf16[16,256,128]{2,1,0:T(8,128)(2,1)S(1)}, u32[]{:S(2)}, u32[]{:S(2)}) collective-permute-start(bf16[16,256,128]{2,1,0:T(8,128)(2,1)S(1)} %collective-permute-done.10.refs_6_), channel_id=1, source_target_pairs={{0,4},{4,0},{8,12},{12,8},{16,20},{20,16},{24,28},{28,24},{1,5},{5... | collective-permute-start | bytes 3145736 | tf_op jit(solution)/shard_map/ppermute | solution.py:208
  207.4 12.1 %collective-permute-start.24 = (bf16[8,256,128]{2,1,0:T(8,128)(2,1)S(1)}, bf16[8,256,128]{2,1,0:T(8,128)(2,1)S(1)}, u32[]{:S(2)}, u32[]{:S(2)}) collective-permute-start(bf16[8,256,128]{2,1,0:T(8,128)(2,1)S(1)} %fusion.6), channel_id=1, source_target_pairs={{0,16},{4,20},{8,24},{12,28},{16,0},{20,4},{24,8},{28,12},{1,17},{... | collective-permute-start | bytes 1572872 | tf_op jit(solution)/shard_map/ppermute | solution.py:208
  209.2 40.0 %copy-start.6 = (bf16[16,256,128]{2,1,0:T(8,128)(2,1)}, bf16[16,256,128]{2,1,0:T(8,128)(2,1)S(1)}, u32[]{:S(2)}) copy-start(bf16[16,256,128]{2,1,0:T(8,128)(2,1)S(1)} %constant_dynamic-update-slice_fusion.10.refs_6_) | copy-start | bytes 3145732
  219.5 30.4 %collective-permute-start.27 = (bf16[16,256,128]{2,1,0:T(8,128)(2,1)S(1)}, bf16[16,256,128]{2,1,0:T(8,128)(2,1)S(1)}, u32[]{:S(2)}, u32[]{:S(2)}) collective-permute-start(bf16[16,256,128]{2,1,0:T(8,128)(2,1)S(1)} %constant_dynamic-update-slice_fusion.10.refs_6_), channel_id=1, source_target_pairs={{0,16},{4,20},{8,24},{12,28},{16,0},{20,4},{24,8},{28,12},{1,17},{... | collective-permute-start | bytes 3145736 | tf_op jit(solution)/shard_map/ppermute | solution.py:208
  220.6 28.7 %copy-start.5 = (bf16[16,256,128]{2,1,0:T(8,128)(2,1)}, bf16[16,256,128]{2,1,0:T(8,128)(2,1)S(1)}, u32[]{:S(2)}) copy-start(bf16[16,256,128]{2,1,0:T(8,128)(2,1)S(1)} %constant_dynamic-update-slice_fusion.8.refs_4_) | copy-start | bytes 3145732
  220.6 1.5 copy-start.19
  220.6 29.3 %collective-permute-start.25 = (bf16[16,256,128]{2,1,0:T(8,128)(2,1)S(1)}, bf16[16,256,128]{2,1,0:T(8,128)(2,1)S(1)}, u32[]{:S(2)}, u32[]{:S(2)}) collective-permute-start(bf16[16,256,128]{2,1,0:T(8,128)(2,1)S(1)} %constant_dynamic-update-slice_fusion.8.refs_4_), channel_id=1, source_target_pairs={{0,8},{4,12},{8,0},{12,4},{16,24},{20,28},{24,16},{28,20},{1,9},{5... | collective-permute-start | bytes 3145736 | tf_op jit(solution)/shard_map/ppermute | solution.py:208
  222.1 1.0 copy-start.20
  222.1 1.3 copy-start.21
  223.4 1.0 copy-start.22
  249.2 2.7 collective-permute-start.30
  249.3 4.1 %collective-permute-start.28 = (bf16[16,256,128]{2,1,0:T(8,128)(2,1)S(1)}, bf16[16,256,128]{2,1,0:T(8,128)(2,1)S(1)}, u32[]{:S(2)}, u32[]{:S(2)}) collective-permute-start(bf16[16,256,128]{2,1,0:T(8,128)(2,1)S(1)} %constant_dynamic-update-slice_fusion.8.refs_4_), channel_id=1, source_target_pairs={{0,4},{4,0},{8,12},{12,8},{16,20},{20,16},{24,28},{28,24},{1,5},{5... | collective-permute-start | bytes 3145736 | tf_op jit(solution)/shard_map/ppermute | solution.py:208
  249.8 11.1 %copy-start.11 = (bf16[16,256,128]{2,1,0:T(8,128)(2,1)}, bf16[16,256,128]{2,1,0:T(8,128)(2,1)S(1)}, u32[]{:S(2)}) copy-start(bf16[16,256,128]{2,1,0:T(8,128)(2,1)S(1)} %collective-permute-done.27.refs_7_) | copy-start | bytes 3145732
  249.8 5.1 %collective-permute-start.31 = (bf16[16,256,128]{2,1,0:T(8,128)(2,1)S(1)}, bf16[16,256,128]{2,1,0:T(8,128)(2,1)S(1)}, u32[]{:S(2)}, u32[]{:S(2)}) collective-permute-start(bf16[16,256,128]{2,1,0:T(8,128)(2,1)S(1)} %collective-permute-done.27.refs_7_), channel_id=1, source_target_pairs={{0,4},{4,0},{8,12},{12,8},{16,20},{20,16},{24,28},{28,24},{1,5},{5... | collective-permute-start | bytes 3145736 | tf_op jit(solution)/shard_map/ppermute | solution.py:208
  249.9 11.0 %copy-start.12 = (bf16[16,256,128]{2,1,0:T(8,128)(2,1)}, bf16[16,256,128]{2,1,0:T(8,128)(2,1)S(1)}, u32[]{:S(2)}) copy-start(bf16[16,256,128]{2,1,0:T(8,128)(2,1)S(1)} %collective-permute-done.25.refs_5_) | copy-start | bytes 3145732
  249.9 6.5 %collective-permute-start.29 = (bf16[16,256,128]{2,1,0:T(8,128)(2,1)S(1)}, bf16[16,256,128]{2,1,0:T(8,128)(2,1)S(1)}, u32[]{:S(2)}, u32[]{:S(2)}) collective-permute-start(bf16[16,256,128]{2,1,0:T(8,128)(2,1)S(1)} %collective-permute-done.25.refs_5_), channel_id=1, source_target_pairs={{0,4},{4,0},{8,12},{12,8},{16,20},{20,16},{24,28},{28,24},{1,5},{5... | collective-permute-start | bytes 3145736 | tf_op jit(solution)/shard_map/ppermute | solution.py:208
  252.0 4.5 %copy-start.15 = (bf16[16,256,128]{2,1,0:T(8,128)(2,1)}, bf16[16,256,128]{2,1,0:T(8,128)(2,1)S(1)}, u32[]{:S(2)}) copy-start(bf16[16,256,128]{2,1,0:T(8,128)(2,1)S(1)} %collective-permute-done.30.refs_10_) | copy-start | bytes 3145732
  253.5 7.4 %copy-start.16 = (bf16[16,256,128]{2,1,0:T(8,128)(2,1)}, bf16[16,256,128]{2,1,0:T(8,128)(2,1)S(1)}, u32[]{:S(2)}) copy-start(bf16[16,256,128]{2,1,0:T(8,128)(2,1)S(1)} %collective-permute-done.28.refs_8_) | copy-start | bytes 3145732
  255.0 6.0 %copy-start.17 = (bf16[16,256,128]{2,1,0:T(8,128)(2,1)}, bf16[16,256,128]{2,1,0:T(8,128)(2,1)S(1)}, u32[]{:S(2)}) copy-start(bf16[16,256,128]{2,1,0:T(8,128)(2,1)S(1)} %collective-permute-done.31.refs_11_) | copy-start | bytes 3145732
  256.5 4.5 %copy-start.18 = (bf16[16,256,128]{2,1,0:T(8,128)(2,1)}, bf16[16,256,128]{2,1,0:T(8,128)(2,1)S(1)}, u32[]{:S(2)}) copy-start(bf16[16,256,128]{2,1,0:T(8,128)(2,1)S(1)} %collective-permute-done.29.refs_9_) | copy-start | bytes 3145732
  256.5 27.0 %collective-permute-start.32 = (bf16[64,2048]{1,0:T(8,128)(2,1)}, bf16[64,2048]{1,0:T(8,128)(2,1)S(1)}, u32[]{:S(2)}, u32[]{:S(2)}) collective-permute-start(bf16[64,2048]{1,0:T(8,128)(2,1)} %get-tuple-element.60), channel_id=1, source_target_pairs={{0,1},{1,2},{2,3},{3,0},{4,5},{5,6},{6,7},{7,4},{8,9},{9,10},{10,1... | collective-permute-start | bytes 786440 | tf_op jit(solution)/shard_map/ppermute | solution.py:283
  257.6 25.9 %collective-permute-start.33 = (bf16[64,2048]{1,0:T(8,128)(2,1)}, bf16[64,2048]{1,0:T(8,128)(2,1)S(1)}, u32[]{:S(2)}, u32[]{:S(2)}) collective-permute-start(bf16[64,2048]{1,0:T(8,128)(2,1)} %get-tuple-element.61), channel_id=1, source_target_pairs={{0,2},{1,3},{2,0},{3,1},{4,6},{5,7},{6,4},{7,5},{8,10},{9,11},{10,... | collective-permute-start | bytes 786440 | tf_op jit(solution)/shard_map/ppermute | solution.py:283
  260.8 22.7 %collective-permute-start.34 = (bf16[64,2048]{1,0:T(8,128)(2,1)}, bf16[64,2048]{1,0:T(8,128)(2,1)S(1)}, u32[]{:S(2)}, u32[]{:S(2)}) collective-permute-start(bf16[64,2048]{1,0:T(8,128)(2,1)} %get-tuple-element.62), channel_id=1, source_target_pairs={{0,3},{1,0},{2,1},{3,2},{4,7},{5,4},{6,5},{7,6},{8,11},{9,8},{10,9... | collective-permute-start | bytes 786440 | tf_op jit(solution)/shard_map/ppermute | solution.py:283
  260.9 22.6 %copy-start.3 = (f32[64,2048]{1,0:T(8,128)S(1)}, f32[64,2048]{1,0:T(8,128)}, u32[]{:S(2)}) copy-start(f32[64,2048]{1,0:T(8,128)} %get-tuple-element.44) | copy-start | bytes 1572868
  279.6 22.7 %collective-permute-start.35 = (bf16[64,2048]{1,0:T(8,128)(2,1)}, bf16[64,2048]{1,0:T(8,128)(2,1)S(1)}, u32[]{:S(2)}, u32[]{:S(2)}) collective-permute-start(bf16[64,2048]{1,0:T(8,128)(2,1)} %get-tuple-element.64), channel_id=1, source_target_pairs={{0,1},{1,2},{2,3},{3,0},{4,5},{5,6},{6,7},{7,4},{8,9},{9,10},{10,1... | collective-permute-start | bytes 786440 | tf_op jit(solution)/shard_map/ppermute | solution.py:283
  281.6 22.2 %collective-permute-start.36 = (bf16[64,2048]{1,0:T(8,128)(2,1)}, bf16[64,2048]{1,0:T(8,128)(2,1)S(1)}, u32[]{:S(2)}, u32[]{:S(2)}) collective-permute-start(bf16[64,2048]{1,0:T(8,128)(2,1)} %get-tuple-element.65), channel_id=1, source_target_pairs={{0,2},{1,3},{2,0},{3,1},{4,6},{5,7},{6,4},{7,5},{8,10},{9,11},{10,... | collective-permute-start | bytes 786440 | tf_op jit(solution)/shard_map/ppermute | solution.py:283
  283.5 22.5 %collective-permute-start.37 = (bf16[64,2048]{1,0:T(8,128)(2,1)}, bf16[64,2048]{1,0:T(8,128)(2,1)S(1)}, u32[]{:S(2)}, u32[]{:S(2)}) collective-permute-start(bf16[64,2048]{1,0:T(8,128)(2,1)} %get-tuple-element.66), channel_id=1, source_target_pairs={{0,3},{1,0},{2,1},{3,2},{4,7},{5,4},{6,5},{7,6},{8,11},{9,8},{10,9... | collective-permute-start | bytes 786440 | tf_op jit(solution)/shard_map/ppermute | solution.py:283
  284.4 21.5 %copy-start.4 = (f32[64,2048]{1,0:T(8,128)S(1)}, f32[64,2048]{1,0:T(8,128)}, u32[]{:S(2)}) copy-start(f32[64,2048]{1,0:T(8,128)} %get-tuple-element.63) | copy-start | bytes 1572868
where the time goes:
time: 309 us; the launch traced here: 307 us
  waiting for transfers between devices  138 us (45%)
  Pallas kernels  106 us (34%)
  starting transfers between devices  39.3 us (13%)
  other arithmetic  19.1 us (6%)
  local copies, waits for them, and re-layouts  3.65 us (1%)
    ppermute x26, waiting for transfers between devices, swap(): lax.ppermute(values, 'row', [(s, s ^ 1 << bit) for s in range(count)])  117 us
    pallas_call x3, Pallas kernels, to_model(): pl.pallas_call(kernel, grid_spec=pltpu.PrefetchScalarGridSpec(num_scalar_...  61.4 us
    pallas_call x2, Pallas kernels, to_hidden(): pl.pallas_call(functools.partial(to_hidden_kernel, flipped), grid_spec=pl...  44.5 us
    ppermute x26, starting transfers between devices, swap(): lax.ppermute(values, 'row', [(s, s ^ 1 << bit) for s in range(count)])  21.6 us
    ppermute x12, waiting for transfers between devices, shift(): lax.ppermute(values, 'col', [(s, (s + distance) % count) for s in range(c...  20.5 us
    ppermute x12, starting transfers between devices, shift(): lax.ppermute(values, 'col', [(s, (s + distance) % count) for s in range(c...  17.7 us
  transfers between devices with their start and end apart: 38, of which 21 were waited for; matrix products, arithmetic and copies ran while one was open for 5% of the time, Pallas kernels for 35%

commit v1 on v0

--- a/solution.py
+++ b/solution.py
@@ -245,37 +245,406 @@
     parts = [[(keep, n * quarter), (arrived, n * quarter)] for n in range(2)]
     sent = [added(terms, half, half).astype(jnp.bfloat16) for terms in parts]
     outgoing = after(sent, *earlier) if earlier else sent
-    return parts, sent, [swap(v, order[0]) for v, order in zip(outgoing, swap_orders())]
-
-
-def scatter_end(parts, arrived):
-    results = []
-    for terms, first, order in zip(parts, arrived, swap_orders()):
-        terms = terms + [(first, 0)]
-        half = first.shape[0]
-        for bit in order[1:]:
-            half = half // 2
-            terms.append((swap(added(terms, half, half).astype(jnp.bfloat16), bit), 0))
-        results.append(added(terms, 0, half))
-    return results
-
-
-def gather_near(parts):
-    pairs = []
-    for part, order in zip(parts, swap_orders()):
-        stages = order[::-1]
-        for bit in stages[:-1]:
-            part = jnp.concatenate([part, swap(part, bit)], axis=0)
-        pairs.append((part, swap(part, stages[-1])))
-    return pairs
-
-
-def gather_far(pairs, *earlier):
-    far = []
-    for first, second in pairs:
-        late = after(second, *earlier) if earlier else second
-        far += [swap(first, 0), swap(late, 0)]
-    return [piece for pair in pairs for piece in pair] + far
+    return arrived, sent, [swap(v, order[0]) for v, order in zip(outgoing, swap_orders())]
+
+
+GELU_SCALE = math.sqrt(2.0 / math.pi)
+
+
+def gelu_and_slope(values):
+    square = values * values
+    bent = jnp.tanh(GELU_SCALE * (values + 0.044715 * (values * square)))
+    half = 0.5 * (1.0 + bent)
+    slope = half + (0.5 * GELU_SCALE) * values * (1.0 - bent * bent) * (
+        1.0 + (3.0 * 0.044715) * square
+    )
+    return values * half, slope
+
+
+def exchange_kernel(sizes, *refs):
+    segments, quarter, own, bits = sizes
+    refs = list(refs)
+    pre_keep, pre_core, pre_first = refs[0], refs[1], refs[2:4]
+    back_keep, back_send = refs[4:6]
+    hidden, near, far = refs[6], refs[7:9], refs[9:11]
+    (acc, core_in, first_in, back, back_in, stage_out, stage_in, own_hidden, own_back) = refs[11:20]
+    local_sems, send_sems, recv_sems = refs[20:]
+    half = quarter // 2
+    row = lax.axis_index("row")
+    orders = [list(range(1, bits)), list(range(1, bits))[::-1]]
+    tokens = acc.shape[2]
+    strip = 32
+    started = []
+    counts = [0, 0]
+
+    def local(source, target):
+        copy = pltpu.make_async_copy(source, target, local_sems.at[counts[0]])
+        counts[0] += 1
+        copy.start()
+        return copy
+
+    def remote(source, target, bit):
+        partner = row ^ (1 << bit)
+        copy = pltpu.make_async_remote_copy(
+            src_ref=source,
+            dst_ref=target,
+            send_sem=send_sems.at[counts[1]],
+            recv_sem=recv_sems.at[counts[1]],
+            device_id={"row": partner},
+            device_id_type=pl.DeviceIdType.MESH,
+        )
+        counts[1] += 1
+        copy.start()
+        started.append(copy)
+        return copy
+
+    def over(count, step):
+        def blocks(index, carry):
+            for start in range(0, tokens, strip):
+                step(index, pl.ds(start, strip))
+            return carry
+
+        lax.fori_loop(0, count, blocks, 0)
+
+    loads = []
+    for n in range(2):
+        whole = pl.ds(n * quarter, half)
+        loads.append(
+            [
+                local(pre_keep.at[whole], acc.at[n]),
+                local(pre_core.at[whole], core_in.at[n]),
+                local(pre_first[n], first_in.at[n]),
+            ]
+        )
+    back_loads = [local(back_keep.at[pl.ds(n * quarter, quarter)], back.at[n]) for n in range(2)]
+
+    barrier = pltpu.get_barrier_semaphore()
+    for bit in range(bits):
+        pl.semaphore_signal(
+            barrier,
+            inc=1,
+            device_id={"row": row ^ (1 << bit)},
+            device_id_type=pl.DeviceIdType.MESH,
+        )
+    pl.semaphore_wait(barrier, bits)
+
+    core_swaps = []
+    for start in (half, 0):
+        for n in range(2):
+            core_swaps.append(
+                remote(
+                    back_send.at[pl.ds(n * quarter + start, half)],
+                    back_in.at[n, pl.ds(start, half)],
+                    0,
+                )
+            )
+
+    offset = [0]
+
+    def slot(count):
+        offset[0] += count
+        return offset[0] - count
+
+    def stage_send(n, bit, count, value):
+        base = slot(count)
+
+        def step(index, rows):
+            stage_out[base + index, rows] = value(index, rows).astype(jnp.bfloat16)
+
+        over(count, step)
+        copy = remote(stage_out.at[pl.ds(base, count)], stage_in.at[pl.ds(base, count)], bit)
+        return copy, base
+
+    def fold_front(n, count):
+        def step(index, rows):
+            acc[n, index, rows] = (
+                acc[n, index, rows]
+                + core_in[n, index, rows].astype(jnp.float32)
+                + first_in[n, index, rows].astype(jnp.float32)
+            )
+
+        over(count, step)
+
+    pre_flight = [None, None]
+    count = half // 2
+    for n in range(2):
+        for copy in loads[n]:
+            copy.wait()
+        pre_flight[n] = stage_send(
+            n,
+            orders[n][1],
+            count,
+            lambda i, r, n=n: acc[n, count + i, r]
+            + core_in[n, count + i, r].astype(jnp.float32)
+            + first_in[n, count + i, r].astype(jnp.float32),
+        )
+    for n in range(2):
+        fold_front(n, count)
+
+    back_flight = [None, None]
+    for n in range(2):
+        back_loads[n].wait()
+        core_swaps[n].wait_recv()
+        back_flight[n] = stage_send(
+            n,
+            orders[n][0],
+            half,
+            lambda i, r, n=n: back[n, half + i, r] + back_in[n, half + i, r].astype(jnp.float32),
+        )
+
+    def settle(ref, n, flight, count, later):
+        for bit in later:
+            copy, base = flight
+            copy.wait_recv()
+            lower = count // 2
+
+            def value(i, r):
+                return ref[n, lower + i, r] + stage_in[base + lower + i, r].astype(jnp.float32)
+
+            flight = stage_send(n, bit, lower, value)
+
+            def fold(i, r):
+                ref[n, i, r] = ref[n, i, r] + stage_in[base + i, r].astype(jnp.float32)
+
+            over(lower, fold)
+            count = lower
+        return flight
+
+    gathers = [None, None]
+    kept = [None, None]
+    for n in range(2):
+        flight, base = settle(acc, n, pre_flight[n], count, orders[n][2:])
+        flight.wait_recv()
+
+        def act(i, r):
+            value, slope = gelu_and_slope(
+                acc[n, i, r] + stage_in[base + i, r].astype(jnp.float32)
+            )
+            own_hidden[n, i, r] = value.astype(jnp.bfloat16)
+            acc[n, i, r] = slope
+
+        over(own, act)
+        start = n * quarter
+        kept[n] = local(own_hidden.at[n], hidden.at[pl.ds(start, own)])
+        gathers[n] = remote(
+            own_hidden.at[n], hidden.at[pl.ds(start + own, own)], orders[n][-1]
+        )
+
+    for n in range(2):
+        core_swaps[2 + n].wait_recv()
+
+        def fold(i, r):
+            back[n, i, r] = back[n, i, r] + back_in[n, i, r].astype(jnp.float32)
+
+        over(half, fold)
+
+    for n in range(2):
+        flight, base = back_flight[n]
+        back_flight[n] = settle(back, n, back_flight[n], half, orders[n][1:2])
+
+    for n in range(2):
+        start = n * quarter
+        size = own
+        kept[n].wait()
+        for bit in orders[n][::-1][1:]:
+            gathers[n].wait_recv()
+            size = size * 2
+            gathers[n] = remote(
+                hidden.at[pl.ds(start, size)], hidden.at[pl.ds(start + size, size)], bit
+            )
+    far_copies = []
+    for n in range(2):
+        start = n * quarter
+        far_copies.append(
+            remote(
+                hidden.at[pl.ds(start, half)], hidden.at[pl.ds(2 * quarter + start, half)], 0
+            )
+        )
+
+    spread = [None, None]
+    held = [None, None]
+    for n in range(2):
+        flight, base = settle(back, n, back_flight[n], half // 2, orders[n][2:])
+        flight.wait_recv()
+
+        def cotangent(i, r):
+            value = back[n, i, r] + stage_in[base + i, r].astype(jnp.float32)
+            own_back[n, i, r] = (value * acc[n, i, r]).astype(jnp.bfloat16)
+
+        over(own, cotangent)
+        held[n] = local(own_back.at[n], near[n].at[pl.ds(0, own)])
+        spread[n] = remote(own_back.at[n], near[n].at[pl.ds(own, own)], orders[n][-1])
+
+    for n in range(2):
+        size = own
+        held[n].wait()
+        for bit in orders[n][::-1][1:-1]:
+            spread[n].wait_recv()
+            size = size * 2
+            spread[n] = remote(near[n].at[pl.ds(0, size)], near[n].at[pl.ds(size, size)], bit)
+        spread[n].wait_recv()
+        far_copies.append(remote(near[n], far[n], 0))
+
+    for n in range(2):
+        gathers[n].wait_recv()
+        start = n * quarter + half
+        far_copies.append(
+            remote(
+                hidden.at[pl.ds(start, half)], hidden.at[pl.ds(2 * quarter + start, half)], 0
+            )
+        )
+    for copy in far_copies:
+        copy.wait_recv()
+    for copy in started:
+        copy.wait_send()
+
+
+def exchange(pre_keep, pre_core, pre_first, back_keep, back_send):
+    held, tokens, width = pre_keep.shape
+    segments = 2 * held
+    quarter = held // 2
+    half = quarter // 2
+    bits = int(math.log2(lax.axis_size("row")))
+    own = quarter >> (bits - 1)
+    staged = 2 * (half - own) + 2 * (quarter - own)
+    copies = 4 + 2 * (bits - 2) + 2 * (bits - 1) + 2 * (bits - 1) + 2 * (bits - 2) + 6
+    wide, narrow = jnp.float32, jnp.bfloat16
+
+    def hbm(count):
+        return jax.ShapeDtypeStruct((count, tokens, width), narrow)
+
+    return pl.pallas_call(
+        functools.partial(exchange_kernel, (segments, quarter, own, bits)),
+        in_specs=[pl.BlockSpec(memory_space=pl.ANY)] * 6,
+        out_specs=[pl.BlockSpec(memory_space=pl.ANY)] * 5,
+        out_shape=[hbm(segments)] + [hbm(half)] * 4,
+        scratch_shapes=[
+            pltpu.VMEM((2, half, tokens, width), wide),
+            pltpu.VMEM((2, half, tokens, width), narrow),
+            pltpu.VMEM((2, half, tokens, width), narrow),
+            pltpu.VMEM((2, quarter, tokens, width), wide),
+            pltpu.VMEM((2, quarter, tokens, width), narrow),
+            pltpu.VMEM((staged, tokens, width), narrow),
+            pltpu.VMEM((staged, tokens, width), narrow),
+            pltpu.VMEM((2, own, tokens, width), narrow),
+            pltpu.VMEM((2, own, tokens, width), narrow),
+            pltpu.SemaphoreType.DMA((12,)),
+            pltpu.SemaphoreType.DMA((copies,)),
+            pltpu.SemaphoreType.DMA((copies,)),
+        ],
+        compiler_params=pltpu.CompilerParams(
+            collective_id=1, has_side_effects=True, vmem_limit_bytes=VMEM_LIMIT
+        ),
+        cost_estimate=pl.CostEstimate(
+            flops=40 * segments * tokens * width,
+            bytes_accessed=30 * segments * tokens * width // 2,
+            transcendentals=2 * own * tokens * width,
+        ),
+    )(pre_keep, pre_core, *pre_first, back_keep, back_send)
+
+
+RELAY_ROWS = 16
+
+
+def relay_kernel(members, own_ref, all_ref, local_sem, send_sems, recv_sems):
+    share = own_ref.shape[0]
+    pieces = share // RELAY_ROWS
+    me = lax.axis_index("col")
+    hops = members - 1
+
+    def place(block, device, piece):
+        slot = (block - device + members) % members
+        return pl.ds(pl.multiple_of(slot * share + piece * RELAY_ROWS, RELAY_ROWS), RELAY_ROWS)
+
+    mine = pltpu.make_async_copy(own_ref, all_ref.at[pl.ds(0, share)], local_sem)
+    mine.start()
+    barrier = pltpu.get_barrier_semaphore()
+    for step in (1, -1):
+        inside = (me + step >= 0) & (me + step < members)
+
+        @pl.when(inside)
+        def _():
+            pl.semaphore_signal(
+                barrier,
+                inc=1,
+                device_id={"col": me + step},
+                device_id_type=pl.DeviceIdType.MESH,
+            )
+
+    pl.semaphore_wait(barrier, jnp.where((me > 0) & (me < members - 1), 2, 1))
+
+    def move(side, hop, piece):
+        step = 1 if side == 0 else -1
+        block = me - step * hop
+        target = jnp.clip(me + step, 0, members - 1)
+        block = jnp.clip(block, 0, members - 1)
+        if hop == 0:
+            source = own_ref.at[pl.ds(piece * RELAY_ROWS, RELAY_ROWS)]
+        else:
+            source = all_ref.at[place(block, me, piece)]
+        at = (side * hops + hop) * pieces + piece
+        return pltpu.make_async_remote_copy(
+            src_ref=source,
+            dst_ref=all_ref.at[place(block, target, piece)],
+            send_sem=send_sems.at[at],
+            recv_sem=recv_sems.at[at],
+            device_id={"col": target},
+            device_id_type=pl.DeviceIdType.MESH,
+        )
+
+    def exists(side, hop):
+        step = 1 if side == 0 else -1
+        block = me - step * hop
+        target = me + step
+        return (block >= 0) & (block < members) & (target >= 0) & (target < members)
+
+    def comes(side, hop):
+        step = 1 if side == 0 else -1
+        block = me - step * (hop + 1)
+        return (block >= 0) & (block < members)
+
+    for hop in range(members):
+        for piece in range(pieces):
+            for side in range(2):
+                if hop > 0:
+
+                    @pl.when(comes(side, hop - 1))
+                    def _():
+                        move(side, hop - 1, piece).wait_recv()
+
+                if hop < hops:
+
+                    @pl.when(exists(side, hop))
+                    def _():
+                        move(side, hop, piece).start()
+
+    for hop in range(hops):
+        for piece in range(pieces):
+            for side in range(2):
+
+                @pl.when(exists(side, hop))
+                def _():
+                    move(side, hop, piece).wait_send()
+
+    mine.wait()
+
+
+def relay_tokens(values):
+    members = lax.axis_size("col")
+    share, columns = values.shape
+    copies = 2 * (members - 1) * (share // RELAY_ROWS)
+    return pl.pallas_call(
+        functools.partial(relay_kernel, members),
+        in_specs=[pl.BlockSpec(memory_space=pl.ANY)],
+        out_specs=pl.BlockSpec(memory_space=pl.ANY),
+        out_shape=jax.ShapeDtypeStruct((members * share, columns), values.dtype),
+        scratch_shapes=[
+            pltpu.SemaphoreType.DMA,
+            pltpu.SemaphoreType.DMA((copies,)),
+            pltpu.SemaphoreType.DMA((copies,)),
+        ],
+        compiler_params=pltpu.CompilerParams(collective_id=2, has_side_effects=True),
+    )(values)
 
 
 def shift(values, distance):
@@ -319,35 +688,26 @@
     weights_one = first_blocks[0, 0]
     weights_two = second_blocks[0, 0]
 
-    inputs_all = gather_tokens(activations)
+    inputs_all = relay_tokens(activations)
     cotangent_all = gather_tokens(after(grad_out, inputs_all))
     pre_keep, pre_send = to_hidden(
         inputs_all, weights_one, model_one, target_one, col_tiles, False
     )
-    pre_terms, pre_sent, pre_arrived = scatter_begin(pre_keep, after(pre_send, cotangent_all))
+    pre_core, pre_sent, pre_first = scatter_begin(pre_keep, after(pre_send, cotangent_all))
     back_keep, back_send = to_hidden(
         after(cotangent_all, *pre_sent), weights_two, model_two, target_two, col_tiles, True
     )
-    pre_parts = scatter_end(pre_terms, pre_arrived)
-    back_terms, _, back_arrived = scatter_begin(
-        back_keep, after(back_send, *pre_arrived), *pre_parts
-    )
-    hidden_own, gelu_backs = [], []
-    for pre in pre_parts:
-        hidden_full, gelu_back = jax.vjp(gelu_tanh, pre)
-        hidden_own.append(hidden_full.astype(jnp.bfloat16))
-        gelu_backs.append(gelu_back)
-    hidden_near = gather_near(hidden_own)
-    back_parts = scatter_end(back_terms, after(back_arrived, *[pair[0] for pair in hidden_near]))
-    grad_pre_own = [
-        gelu_back(back)[0].astype(jnp.bfloat16) for gelu_back, back in zip(gelu_backs, back_parts)
-    ]
-    hidden_parts = gather_far(hidden_near)
-    grad_pre_near = gather_near(after(grad_pre_own, *hidden_near))
+    hidden, near_a, near_b, far_a, far_b = exchange(
+        pre_keep, pre_core, pre_first, back_keep, back_send
+    )
+    orders = swap_orders()
+    last_a, last_b = swap(near_a, orders[0][0]), swap(near_b, orders[1][0])
     grad_second, own_out, send_out = to_model(
-        cotangent_all, hidden_parts, weights_two, (model_two, hidden_two, live_two), members, False
-    )
-    grad_pre_parts = gather_far(grad_pre_near, own_out)
+        cotangent_all, [hidden], weights_two, (model_two, hidden_two, live_two), members, False
+    )
+    far_last_a = swap(after(last_a, own_out), 0)
+    far_last_b = swap(after(last_b, own_out), 0)
+    grad_pre_parts = [near_a, last_a, near_b, last_b, far_a, far_last_a, far_b, far_last_b]
     output = scatter_tokens(own_out, after(send_out, *grad_pre_parts))
     places_one = (model_one, hidden_one, live_one)
     own_in, send_in = to_model(

time: 309 us -> 274 us (0.89)
  waiting for transfers between devices: 138 us -> 14 us
  Pallas kernels: 106 us -> 226 us
  starting transfers between devices: 39.3 us -> 18.4 us
  other arithmetic: 19.1 us -> 11.1 us
    pallas_call x0 -> x2, Pallas kernels: none -> 120 us  [the longest x1 101 us: exchange(): pl.pallas_call(functools.partial(exchange_kernel, (segments, quarter, own...]
    ppermute x26 -> x7, waiting for transfers between devices: 117 us -> 11.5 us  [swap(): lax.ppermute(values, 'row', [(s, s ^ 1 << bit) for s in range(count)])]
    ppermute x12 -> x9, waiting for transfers between devices: 20.5 us -> 2.49 us  [shift(): lax.ppermute(values, 'col', [(s, (s + distance) % count) for s in range(c...]
    ppermute x26 -> x7, starting transfers between devices: 21.6 us -> 4.94 us  [swap(): lax.ppermute(values, 'row', [(s, s ^ 1 << bit) for s in range(count)])]
    convert_element_type x6 -> x0, other arithmetic: 7.98 us -> none  [the longest x2 4.35 us: body(): hidden_own.append(hidden_full.astype(jnp.bfloat16))]
    ppermute x12 -> x9, starting transfers between devices: 17.7 us -> 13.5 us  [shift(): lax.ppermute(values, 'col', [(s, (s + distance) % count) for s in range(c...]
  transfers between devices with their start and end apart: 38 -> 16, of which waited for: 21 -> 7; matrix products, arithmetic and copies ran while one was open for 5% -> 2% of each run, Pallas kernels for 35% -> 39%
where the time goes in v1:
time: 274 us; the launch traced here: 273 us
  Pallas kernels  226 us (82%)
  starting transfers between devices  18.4 us (7%)
  waiting for transfers between devices  14 us (5%)
  other arithmetic  11.1 us (4%)
    pallas_call x1, Pallas kernels, exchange(): pl.pallas_call(functools.partial(exchange_kernel, (segments, quarter, own...  101 us
    pallas_call x3, Pallas kernels, to_model(): pl.pallas_call(kernel, grid_spec=pltpu.PrefetchScalarGridSpec(num_scalar_...  62.2 us
    pallas_call x2, Pallas kernels, to_hidden(): pl.pallas_call(functools.partial(to_hidden_kernel, flipped), grid_spec=pl...  44.4 us
    pallas_call x1, Pallas kernels, relay_tokens(): pl.pallas_call(functools.partial(relay_kernel, members), in_specs=[pl.Blo...  19.2 us
    ppermute x9, starting transfers between devices, shift(): lax.ppermute(values, 'col', [(s, (s + distance) % count) for s in range(c...  13.5 us
    ppermute x7, waiting for transfers between devices, swap(): lax.ppermute(values, 'row', [(s, s ^ 1 << bit) for s in range(count)])  11.5 us
  transfers between devices with their start and end apart: 16, of which 7 were waited for; matrix products, arithmetic and copies ran while one was open for 2% of the time, Pallas kernels for 39%

profile of v1, /device:TPU:12, one launch (start us, length us, event | category | flops | bytes accessed | tf_op | source)
XLA Modules:
  0.0 273.0 jit_solution(14292208001750907319)
XLA Ops:
  0.6 19.2 %shard_map.93.panel.refs_3_ = bf16[256,2048]{1,0:T(8,128)(2,1)} custom-call(bf16[64,2048]{1,0:T(8,128)(2,1)} %own_ref.1), custom_call_target="tpu_custom_call" | custom-call | tf_op jit(solution)/shard_map/pallas_call | solution.py:636
  19.9 2.5 collective-permute-start
  22.4 1.0 collective-permute-start.1
  23.4 2.8 %collective-permute-start.2 = (bf16[64,2048]{1,0:T(8,128)(2,1)}, bf16[64,2048]{1,0:T(8,128)(2,1)S(1)}, u32[]{:S(2)}, u32[]{:S(2)}) collective-permute-start(bf16[64,2048]{1,0:T(8,128)(2,1)} %param.7), channel_id=1, source_target_pairs={{0,1},{1,2},{2,3},{3,0},{4,5},{5,6},{6,7},{7,4},{8,9},{9,10},{10,1... | collective-permute-start | bytes 786440 | tf_op jit(solution)/shard_map/ppermute | solution.py:652
  26.3 0.7 compare_reduce_fusion
  27.0 0.8 subtract_reduce_fusion
  27.8 0.6 broadcast_select_fusion.1
  28.4 22.2 %shard_map.94 = (f32[64,256,128]{2,1,0:T(8,128)}, bf16[64,256,128]{2,1,0:T(8,128)(2,1)}) custom-call(s32[384]{0:T(512)} %get-tuple-element.82.source.refs_0_, s32[384]{0:T(512)} %get-tuple-element.78.target, bf16[256,2048]{1,0:T(8,128)(2,1)} %shard_map.93.panel.refs_3_, bf16[384,128,128]{2,1,0:T(8,128)(2,1)} %bitcast.6), custom_call_target="tpu_custom_call" | custom-call | flops 12884901888 | bytes 25165824 | tf_op jit(solution)/shard_map/pallas_call | solution.py:65
  50.6 0.0 copy-done.5
  50.6 0.0 collective-permute-done
  50.7 0.0 collective-permute-done.1
  50.7 0.0 collective-permute-done.2
  50.8 0.0 copy-start.6
  50.8 1.0 copy-done.6
  51.8 0.0 collective-permute-start.3
  51.8 0.0 copy-done.7
  51.8 0.6 convert_element_type.36.refs_2_
  52.4 0.6 broadcast_select_fusion
  53.0 6.1 %collective-permute-done.3.refs_1_ = bf16[64,256,128]{2,1,0:T(8,128)(2,1)S(1)} collective-permute-done((bf16[64,256,128]{2,1,0:T(8,128)(2,1)}, bf16[64,256,128]{2,1,0:T(8,128)(2,1)S(1)}, u32[]{:S(2)}, u32[]{:S(2)}) %collective-permute-start.3) | collective-permute-done | bytes 4194336 | tf_op jit(solution)/shard_map/ppermute | solution.py:208
  59.1 5.4 %add_convert_fusion = (bf16[16,256,128]{2,1,0:T(8,128)(2,1)S(1)}, bf16[16,256,128]{2,1,0:T(8,128)(2,1)}) fusion(f32[64,256,128]{2,1,0:T(8,128)} %get-tuple-element.39.refs_0_, bf16[64,256,128]{2,1,0:T(8,128)(2,1)S(1)} %collective-permute-done.3.refs_1_), kind=kLoop, calls=%fused_computation | loop fusion | flops 3145728 | bytes 8388608 | tf_op jit(solution)/shard_map/convert_element_type | solution.py:246
  64.5 0.0 copy-done
  64.5 1.7 collective-permute-start.4
  66.2 0.3 collective-permute-start.5
  66.5 22.2 %shard_map.95 = (f32[64,256,128]{2,1,0:T(8,128)}, bf16[64,256,128]{2,1,0:T(8,128)(2,1)}) custom-call(s32[384]{0:T(512)} %get-tuple-element.83.source.refs_0_, s32[384]{0:T(512)} %get-tuple-element.76.target, bf16[256,2048]{1,0:T(8,128)(2,1)} %copy-done.6, bf16[384,128,128]{2,1,0:T(8,128)(2,1)} %bitcast.4), custom_call_target="tpu_custom_call" | custom-call | flops 12884901888 | bytes 25165824 | tf_op jit(solution)/shard_map/pallas_call | solution.py:65
  88.7 1.2 collective-permute-done.4.refs_2_
  89.9 1.2 collective-permute-done.5.refs_3_
  91.1 0.0 copy-done.1
  91.1 1.0 copy-done.2
  92.1 100.7 %shard_map.96 = (bf16[128,256,128]{2,1,0:T(8,128)(2,1)}, bf16[16,256,128]{2,1,0:T(8,128)(2,1)}, bf16[16,256,128]{2,1,0:T(8,128)(2,1)}, bf16[16,256,128]{2,1,0:T(8,128)(2,1)}, bf16[16,256,128]{2,1,0:T(8,128)(2,1)}) custom-call(f32[64,256,128]{2,1,0:T(8,128)} %get-tuple-element.39.refs_0_, bf16[64,256,128]{2,1,0:T(8,128)(2,1)} %copy-done, ...), custom_call_target="tpu_custom_call" | custom-call | flops 167772160 | bytes 62914560 | tf_op jit(solution)/shard_map/pallas_call | solution.py:516
  192.8 1.2 collective-permute-start.7
  194.1 1.1 collective-permute-start.6
  195.2 25.1 %shard_map.97 = (bf16[384,128,128]{2,1,0:T(8,128)(2,1)}, f32[64,2048]{1,0:T(8,128)}, bf16[64,2048]{1,0:T(8,128)(2,1)}, bf16[64,2048]{1,0:T(8,128)(2,1)}, bf16[64,2048]{1,0:T(8,128)(2,1)}) custom-call(s32[384]{0:T(512)} %get-tuple-element.83.source.refs_0_, s32[384]{0:T(512)} %get-tuple-element.77.refs_1_, s32[384]{0:T(512)} %convert_element_type.36.refs_2_, ...), custom_call_target="tpu_custom_call" | custom-call | flops 25769803776 | bytes 33554432 | tf_op jit(solution)/shard_map/pallas_call | solution.py:187
  220.3 0.0 collective-permute-done.7.refs_7_
  220.3 0.0 copy-start.8
  220.3 0.1 collective-permute-start.9
  220.4 0.0 collective-permute-done.6.refs_5_
  220.4 0.0 copy-start.9
  220.4 0.5 collective-permute-start.8
  220.9 0.6 convert_element_type.44.refs_2_
  221.5 1.5 collective-permute-done.9.refs_11_
  223.0 1.5 collective-permute-done.8.refs_9_
  224.5 0.0 collective-permute-start.10
  224.5 1.6 collective-permute-start.11
  226.1 1.2 collective-permute-start.12
  227.2 0.0 copy-done.11
  227.2 0.0 copy-done.8
  227.2 0.0 copy-done.9
  227.2 0.0 copy-done.10
  227.2 0.0 copy-start.3
  227.3 18.7 %shard_map.98 = (f32[64,2048]{1,0:T(8,128)}, bf16[64,2048]{1,0:T(8,128)(2,1)}, bf16[64,2048]{1,0:T(8,128)(2,1)}, bf16[64,2048]{1,0:T(8,128)(2,1)}) custom-call(s32[384]{0:T(512)} %get-tuple-element.82.source.refs_0_, s32[384]{0:T(512)} %get-tuple-element.79.refs_1_, s32[384]{0:T(512)} %convert_element_type.44.refs_2_, bf16[384,128,128]{2,1,0:T(8,128)(2,1)} %bitcast.7, ...), custom_call_target="tpu_custom_call" | custom-call | flops 12884901888 | bytes 33554432 | tf_op jit(solution)/shard_map/pallas_call | solution.py:187
  246.0 0.9 collective-permute-start.13
  246.9 3.2 %collective-permute-start.14 = (bf16[64,2048]{1,0:T(8,128)(2,1)}, bf16[64,2048]{1,0:T(8,128)(2,1)S(1)}, u32[]{:S(2)}, u32[]{:S(2)}) collective-permute-start(bf16[64,2048]{1,0:T(8,128)(2,1)} %get-tuple-element.61), channel_id=1, source_target_pairs={{0,2},{1,3},{2,0},{3,1},{4,6},{5,7},{6,4},{7,5},{8,10},{9,11},{10,... | collective-permute-start | bytes 786440 | tf_op jit(solution)/shard_map/ppermute | solution.py:652
  250.1 0.0 collective-permute-done.10
  250.1 0.2 collective-permute-start.15
  250.3 0.0 collective-permute-done.11
  250.3 0.0 collective-permute-done.12
  250.3 0.0 copy-done.3
  250.3 0.9 convert_add_fusion.1
  251.2 18.4 %shard_map.99 = bf16[384,128,128]{2,1,0:T(8,128)(2,1)} custom-call(s32[384]{0:T(512)} %get-tuple-element.82.source.refs_0_, s32[384]{0:T(512)} %get-tuple-element.79.refs_1_, s32[384]{0:T(512)} %convert_element_type.44.refs_2_, bf16[256,2048]{1,0:T(8,128)(2,1)} %shard_map.93.panel.refs_3_, bf16[16,256,128]{2,1,0:T(8,128)(2,1)} %get-tuple-element.63.refs_4_, ...), custom_call_target="tpu_custom_call" | custom-call | flops 12884901888 | bytes 33554432 | tf_op jit(solution)/shard_map/pallas_call | solution.py:187
  269.6 0.0 collective-permute-done.13
  269.6 0.7 collective-permute-done.14
  270.3 1.8 collective-permute-done.15
  272.1 0.0 copy-done.4
  272.1 0.9 convert_add_fusion
  (13 shorter events, 0.1 us)
Async XLA Ops:
  19.9 30.8 %collective-permute-start = (bf16[64,2048]{1,0:T(8,128)(2,1)}, bf16[64,2048]{1,0:T(8,128)(2,1)S(1)}, u32[]{:S(2)}, u32[]{:S(2)}) collective-permute-start(bf16[64,2048]{1,0:T(8,128)(2,1)} %param.7), channel_id=1, source_target_pairs={{0,3},{1,0},{2,1},{3,2},{4,7},{5,4},{6,5},{7,6},{8,11},{9,8},{10,9... | collective-permute-start | bytes 786440 | tf_op jit(solution)/shard_map/ppermute | solution.py:652
  22.4 28.3 %collective-permute-start.1 = (bf16[64,2048]{1,0:T(8,128)(2,1)}, bf16[64,2048]{1,0:T(8,128)(2,1)S(1)}, u32[]{:S(2)}, u32[]{:S(2)}) collective-permute-start(bf16[64,2048]{1,0:T(8,128)(2,1)} %param.7), channel_id=1, source_target_pairs={{0,2},{1,3},{2,0},{3,1},{4,6},{5,7},{6,4},{7,5},{8,10},{9,11},{10,... | collective-permute-start | bytes 786440 | tf_op jit(solution)/shard_map/ppermute | solution.py:652
  23.4 27.3 %collective-permute-start.2 = (bf16[64,2048]{1,0:T(8,128)(2,1)}, bf16[64,2048]{1,0:T(8,128)(2,1)S(1)}, u32[]{:S(2)}, u32[]{:S(2)}) collective-permute-start(bf16[64,2048]{1,0:T(8,128)(2,1)} %param.7), channel_id=1, source_target_pairs={{0,1},{1,2},{2,3},{3,0},{4,5},{5,6},{6,7},{7,4},{8,9},{9,10},{10,1... | collective-permute-start | bytes 786440 | tf_op jit(solution)/shard_map/ppermute | solution.py:652
  28.4 22.2 %copy-start.5 = (bf16[64,2048]{1,0:T(8,128)(2,1)S(1)}, bf16[64,2048]{1,0:T(8,128)(2,1)}, u32[]{:S(2)}) copy-start(bf16[64,2048]{1,0:T(8,128)(2,1)} %param.7) | copy-start | bytes 786436
  28.4 23.4 %copy-start.7 = (s32[1,1,384,2]{2,3,1,0:T(2,128)S(1)}, s32[1,1,384,2]{2,3,1,0:T(2,128)}, u32[]{:S(2)}) copy-start(s32[1,1,384,2]{2,3,1,0:T(2,128)} %param.11) | copy-start | bytes 9220
  50.8 1.0 copy-start.6
  51.8 7.4 %collective-permute-start.3 = (bf16[64,256,128]{2,1,0:T(8,128)(2,1)}, bf16[64,256,128]{2,1,0:T(8,128)(2,1)S(1)}, u32[]{:S(2)}, u32[]{:S(2)}) collective-permute-start(bf16[64,256,128]{2,1,0:T(8,128)(2,1)} %get-tuple-element.41), channel_id=1, source_target_pairs={{0,4},{4,0},{8,12},{12,8},{16,20},{20,16},{24,28},{28,24},{1,5},{5... | collective-permute-start | bytes 12582920 | tf_op jit(solution)/shard_map/ppermute | solution.py:208
  59.1 5.4 %copy-start = (bf16[64,256,128]{2,1,0:T(8,128)(2,1)}, bf16[64,256,128]{2,1,0:T(8,128)(2,1)S(1)}, u32[]{:S(2)}) copy-start(bf16[64,256,128]{2,1,0:T(8,128)(2,1)S(1)} %collective-permute-done.3.refs_1_) | copy-start | bytes 12582916
  64.5 25.4 %collective-permute-start.4 = (bf16[16,256,128]{2,1,0:T(8,128)(2,1)}, bf16[16,256,128]{2,1,0:T(8,128)(2,1)S(1)}, u32[]{:S(2)}, u32[]{:S(2)}) collective-permute-start(bf16[16,256,128]{2,1,0:T(8,128)(2,1)} %get-tuple-element.81), channel_id=1, source_target_pairs={{0,8},{4,12},{8,0},{12,4},{16,24},{20,28},{24,16},{28,20},{1,9},{5... | collective-permute-start | bytes 3145736 | tf_op jit(solution)/shard_map/ppermute | solution.py:208
  66.2 24.9 %collective-permute-start.5 = (bf16[16,256,128]{2,1,0:T(8,128)(2,1)S(1)}, bf16[16,256,128]{2,1,0:T(8,128)(2,1)S(1)}, u32[]{:S(2)}, u32[]{:S(2)}) collective-permute-start(bf16[16,256,128]{2,1,0:T(8,128)(2,1)S(1)} %get-tuple-element.80), channel_id=1, source_target_pairs={{0,16},{4,20},{8,24},{12,28},{16,0},{20,4},{24,8},{28,12},{1,17},{... | collective-permute-start | bytes 3145736 | tf_op jit(solution)/shard_map/ppermute | solution.py:208
  89.9 1.2 copy-start.1
  91.1 1.0 copy-start.2
  192.8 27.5 %collective-permute-start.7 = (bf16[16,256,128]{2,1,0:T(8,128)(2,1)}, bf16[16,256,128]{2,1,0:T(8,128)(2,1)S(1)}, u32[]{:S(2)}, u32[]{:S(2)}) collective-permute-start(bf16[16,256,128]{2,1,0:T(8,128)(2,1)} %get-tuple-element.65.refs_6_), channel_id=1, source_target_pairs={{0,16},{4,20},{8,24},{12,28},{16,0},{20,4},{24,8},{28,12},{1,17},{... | collective-permute-start | bytes 3145736 | tf_op jit(solution)/shard_map/ppermute | solution.py:208
  194.1 26.3 %collective-permute-start.6 = (bf16[16,256,128]{2,1,0:T(8,128)(2,1)}, bf16[16,256,128]{2,1,0:T(8,128)(2,1)S(1)}, u32[]{:S(2)}, u32[]{:S(2)}) collective-permute-start(bf16[16,256,128]{2,1,0:T(8,128)(2,1)} %get-tuple-element.63.refs_4_), channel_id=1, source_target_pairs={{0,8},{4,12},{8,0},{12,4},{16,24},{20,28},{24,16},{28,20},{1,9},{5... | collective-permute-start | bytes 3145736 | tf_op jit(solution)/shard_map/ppermute | solution.py:208
  220.3 7.0 %copy-start.8 = (bf16[16,256,128]{2,1,0:T(8,128)(2,1)}, bf16[16,256,128]{2,1,0:T(8,128)(2,1)S(1)}, u32[]{:S(2)}) copy-start(bf16[16,256,128]{2,1,0:T(8,128)(2,1)S(1)} %collective-permute-done.7.refs_7_) | copy-start | bytes 3145732
  220.3 2.7 collective-permute-start.9
  220.4 6.9 %copy-start.9 = (bf16[16,256,128]{2,1,0:T(8,128)(2,1)}, bf16[16,256,128]{2,1,0:T(8,128)(2,1)S(1)}, u32[]{:S(2)}) copy-start(bf16[16,256,128]{2,1,0:T(8,128)(2,1)S(1)} %collective-permute-done.6.refs_5_) | copy-start | bytes 3145732
  220.4 4.1 %collective-permute-start.8 = (bf16[16,256,128]{2,1,0:T(8,128)(2,1)S(1)}, bf16[16,256,128]{2,1,0:T(8,128)(2,1)S(1)}, u32[]{:S(2)}, u32[]{:S(2)}) collective-permute-start(bf16[16,256,128]{2,1,0:T(8,128)(2,1)S(1)} %collective-permute-done.6.refs_5_), channel_id=1, source_target_pairs={{0,4},{4,0},{8,12},{12,8},{16,20},{20,16},{24,28},{28,24},{1,5},{5... | collective-permute-start | bytes 3145736 | tf_op jit(solution)/shard_map/ppermute | solution.py:208
  223.0 4.2 %copy-start.10 = (bf16[16,256,128]{2,1,0:T(8,128)(2,1)}, bf16[16,256,128]{2,1,0:T(8,128)(2,1)S(1)}, u32[]{:S(2)}) copy-start(bf16[16,256,128]{2,1,0:T(8,128)(2,1)S(1)} %collective-permute-done.9.refs_11_) | copy-start | bytes 3145732
  224.5 2.7 copy-start.11
  224.5 25.6 %collective-permute-start.10 = (bf16[64,2048]{1,0:T(8,128)(2,1)}, bf16[64,2048]{1,0:T(8,128)(2,1)S(1)}, u32[]{:S(2)}, u32[]{:S(2)}) collective-permute-start(bf16[64,2048]{1,0:T(8,128)(2,1)} %get-tuple-element.56), channel_id=1, source_target_pairs={{0,1},{1,2},{2,3},{3,0},{4,5},{5,6},{6,7},{7,4},{8,9},{9,10},{10,1... | collective-permute-start | bytes 786440 | tf_op jit(solution)/shard_map/ppermute | solution.py:652
  224.5 25.8 %collective-permute-start.11 = (bf16[64,2048]{1,0:T(8,128)(2,1)}, bf16[64,2048]{1,0:T(8,128)(2,1)S(1)}, u32[]{:S(2)}, u32[]{:S(2)}) collective-permute-start(bf16[64,2048]{1,0:T(8,128)(2,1)} %get-tuple-element.57), channel_id=1, source_target_pairs={{0,2},{1,3},{2,0},{3,1},{4,6},{5,7},{6,4},{7,5},{8,10},{9,11},{10,... | collective-permute-start | bytes 786440 | tf_op jit(solution)/shard_map/ppermute | solution.py:652
  226.1 24.2 %collective-permute-start.12 = (bf16[64,2048]{1,0:T(8,128)(2,1)}, bf16[64,2048]{1,0:T(8,128)(2,1)S(1)}, u32[]{:S(2)}, u32[]{:S(2)}) collective-permute-start(bf16[64,2048]{1,0:T(8,128)(2,1)} %get-tuple-element.58), channel_id=1, source_target_pairs={{0,3},{1,0},{2,1},{3,2},{4,7},{5,4},{6,5},{7,6},{8,11},{9,8},{10,9... | collective-permute-start | bytes 786440 | tf_op jit(solution)/shard_map/ppermute | solution.py:652
  227.2 23.1 %copy-start.3 = (f32[64,2048]{1,0:T(8,128)S(1)}, f32[64,2048]{1,0:T(8,128)}, u32[]{:S(2)}) copy-start(f32[64,2048]{1,0:T(8,128)} %get-tuple-element.46) | copy-start | bytes 1572868
  246.0 23.7 %collective-permute-start.13 = (bf16[64,2048]{1,0:T(8,128)(2,1)}, bf16[64,2048]{1,0:T(8,128)(2,1)S(1)}, u32[]{:S(2)}, u32[]{:S(2)}) collective-permute-start(bf16[64,2048]{1,0:T(8,128)(2,1)} %get-tuple-element.60), channel_id=1, source_target_pairs={{0,1},{1,2},{2,3},{3,0},{4,5},{5,6},{6,7},{7,4},{8,9},{9,10},{10,1... | collective-permute-start | bytes 786440 | tf_op jit(solution)/shard_map/ppermute | solution.py:652
  246.9 23.4 %collective-permute-start.14 = (bf16[64,2048]{1,0:T(8,128)(2,1)}, bf16[64,2048]{1,0:T(8,128)(2,1)S(1)}, u32[]{:S(2)}, u32[]{:S(2)}) collective-permute-start(bf16[64,2048]{1,0:T(8,128)(2,1)} %get-tuple-element.61), channel_id=1, source_target_pairs={{0,2},{1,3},{2,0},{3,1},{4,6},{5,7},{6,4},{7,5},{8,10},{9,11},{10,... | collective-permute-start | bytes 786440 | tf_op jit(solution)/shard_map/ppermute | solution.py:652
  250.1 22.0 %collective-permute-start.15 = (bf16[64,2048]{1,0:T(8,128)(2,1)}, bf16[64,2048]{1,0:T(8,128)(2,1)S(1)}, u32[]{:S(2)}, u32[]{:S(2)}) collective-permute-start(bf16[64,2048]{1,0:T(8,128)(2,1)} %get-tuple-element.62), channel_id=1, source_target_pairs={{0,3},{1,0},{2,1},{3,2},{4,7},{5,4},{6,5},{7,6},{8,11},{9,8},{10,9... | collective-permute-start | bytes 786440 | tf_op jit(solution)/shard_map/ppermute | solution.py:652
  251.2 20.9 %copy-start.4 = (f32[64,2048]{1,0:T(8,128)S(1)}, f32[64,2048]{1,0:T(8,128)}, u32[]{:S(2)}) copy-start(f32[64,2048]{1,0:T(8,128)} %get-tuple-element.59) | copy-start | bytes 1572868

commit v2 on v1

--- a/solution.py
+++ b/solution.py
@@ -238,16 +238,6 @@
     return total
 
 
-def scatter_begin(keep, send, *earlier):
-    arrived = swap(send, 0)
-    quarter = keep.shape[0] // 2
-    half = quarter // 2
-    parts = [[(keep, n * quarter), (arrived, n * quarter)] for n in range(2)]
-    sent = [added(terms, half, half).astype(jnp.bfloat16) for terms in parts]
-    outgoing = after(sent, *earlier) if earlier else sent
-    return arrived, sent, [swap(v, order[0]) for v, order in zip(outgoing, swap_orders())]
-
-
 GELU_SCALE = math.sqrt(2.0 / math.pi)
 
 
@@ -261,18 +251,27 @@
     return values * half, slope
 
 
+GROUP = 32
+AHEAD = 3
+
+
 def exchange_kernel(sizes, *refs):
-    segments, quarter, own, bits = sizes
+    quarter, own, bits, members = sizes
     refs = list(refs)
-    pre_keep, pre_core, pre_first = refs[0], refs[1], refs[2:4]
-    back_keep, back_send = refs[4:6]
-    hidden, near, far = refs[6], refs[7:9], refs[9:11]
-    (acc, core_in, first_in, back, back_in, stage_out, stage_in, own_hidden, own_back) = refs[11:20]
-    local_sems, send_sems, recv_sems = refs[20:]
+    source_at, carries, ends, filled = refs[0:4]
+    pre_keep, pre_send, cotangent, weights = refs[4:8]
+    hidden, near, far, cotangent_out = refs[8], refs[9:11], refs[11:13], refs[13]
+    (acc, core_in, back, back_in, stage_out, stage_in, own_hidden, own_back) = refs[14:22]
+    (panel, tiles, blocks, running, sums) = refs[22:27]
+    local_sems, block_sems, send_sems, recv_sems = refs[27:]
     half = quarter // 2
     row = lax.axis_index("row")
+    col = lax.axis_index("col")
     orders = [list(range(1, bits)), list(range(1, bits))[::-1]]
-    tokens = acc.shape[2]
+    tokens, width = acc.shape[2:]
+    share = tokens // members
+    slots = weights.shape[0]
+    groups = slots // GROUP
     strip = 32
     started = []
     counts = [0, 0]
@@ -283,14 +282,13 @@
         copy.start()
         return copy
 
-    def remote(source, target, bit):
-        partner = row ^ (1 << bit)
+    def remote_to(source, target, device):
         copy = pltpu.make_async_remote_copy(
             src_ref=source,
             dst_ref=target,
             send_sem=send_sems.at[counts[1]],
             recv_sem=recv_sems.at[counts[1]],
-            device_id={"row": partner},
+            device_id=device,
             device_id_type=pl.DeviceIdType.MESH,
         )
         counts[1] += 1
@@ -298,25 +296,27 @@
         started.append(copy)
         return copy
 
+    def remote(source, target, bit):
+        return remote_to(source, target, {"row": row ^ (1 << bit)})
+
     def over(count, step):
-        def blocks(index, carry):
+        def each(index, carry):
             for start in range(0, tokens, strip):
                 step(index, pl.ds(start, strip))
             return carry
 
-        lax.fori_loop(0, count, blocks, 0)
-
-    loads = []
-    for n in range(2):
-        whole = pl.ds(n * quarter, half)
-        loads.append(
-            [
-                local(pre_keep.at[whole], acc.at[n]),
-                local(pre_core.at[whole], core_in.at[n]),
-                local(pre_first[n], first_in.at[n]),
-            ]
+        lax.fori_loop(0, count, each, 0)
+
+    def fetch_group(group):
+        place = lax.rem(group, AHEAD)
+        return pltpu.make_async_copy(
+            weights.at[pl.ds(group * GROUP, GROUP)], blocks.at[place], block_sems.at[place]
         )
-    back_loads = [local(back_keep.at[pl.ds(n * quarter, quarter)], back.at[n]) for n in range(2)]
+
+    loads = [local(pre_keep.at[pl.ds(n * quarter + half, half)], acc.at[n]) for n in range(2)]
+    own_tokens = local(cotangent, panel.at[pl.ds(0, share)])
+    for group in range(min(AHEAD, groups)):
+        fetch_group(group).start()
 
     barrier = pltpu.get_barrier_semaphore()
     for bit in range(bits):
@@ -326,209 +326,327 @@
             device_id={"row": row ^ (1 << bit)},
             device_id_type=pl.DeviceIdType.MESH,
         )
-    pl.semaphore_wait(barrier, bits)
-
-    core_swaps = []
-    for start in (half, 0):
+    for distance in range(1, members):
+        pl.semaphore_signal(
+            barrier,
+            inc=1,
+            device_id={"col": lax.rem(col + distance, members)},
+            device_id_type=pl.DeviceIdType.MESH,
+        )
+    pl.semaphore_wait(barrier, bits + members - 1)
+
+    low = half // 2
+    spans = ((half + low, low), (half, low), (0, half))
+
+    def swap_core(n, span, source, target):
+        return remote(source, target.at[n, pl.ds(*span)], 0)
+
+    pre_core = [[], []]
+    for span in spans:
         for n in range(2):
-            core_swaps.append(
+            source = pre_send.at[pl.ds(n * quarter + span[0], span[1])]
+            pre_core[n].append(swap_core(n, span, source, core_in))
+    arrivals = []
+    for distance in range(1, members):
+        slot = pl.ds((members - distance) * share, share)
+        device = {"col": lax.rem(col + distance, members)}
+        arrivals.append(remote_to(cotangent, panel.at[slot], device))
+
+    pre_stages = []
+    out_places = [0]
+    in_places = [0]
+
+    def stage_send(n, bit, count, value, ready):
+        base, there = out_places[0], in_places[0]
+        out_places[0] += count
+        in_places[0] += count
+        cut = count // 2
+        copies = []
+        for number, (start, size) in enumerate(((cut, count - cut), (0, cut))):
+            ready[number]()
+
+            def step(index, rows):
+                stage_out[base + start + index, rows] = value(start + index, rows).astype(
+                    jnp.bfloat16
+                )
+
+            over(size, step)
+            copies.append(
                 remote(
-                    back_send.at[pl.ds(n * quarter + start, half)],
-                    back_in.at[n, pl.ds(start, half)],
-                    0,
+                    stage_out.at[pl.ds(base + start, size)],
+                    stage_in.at[pl.ds(there + start, size)],
+                    bit,
                 )
             )
-
-    offset = [0]
-
-    def slot(count):
-        offset[0] += count
-        return offset[0] - count
-
-    def stage_send(n, bit, count, value):
-        base = slot(count)
-
-        def step(index, rows):
-            stage_out[base + index, rows] = value(index, rows).astype(jnp.bfloat16)
+        pre_stages.append((copies, there))
+        return copies, there
+
+    def nothing():
+        return None
+
+    def arrived_at(base):
+        return lambda i, r: stage_in[base + i, r].astype(jnp.float32)
+
+    def pass_on(ref, n, flight, count, bit):
+        copies, base = flight
+        lower = count // 2
+        copies[0].wait_recv()
+        term = arrived_at(base)
+        return stage_send(
+            n,
+            bit,
+            lower,
+            lambda i, r: ref[n, lower + i, r] + term(lower + i, r),
+            (nothing, nothing),
+        )
+
+    def fold(ref, n, count, term):
+        def step(i, r):
+            ref[n, i, r] = ref[n, i, r] + term(i, r)
 
         over(count, step)
-        copy = remote(stage_out.at[pl.ds(base, count)], stage_in.at[pl.ds(base, count)], bit)
-        return copy, base
-
-    def fold_front(n, count):
-        def step(index, rows):
-            acc[n, index, rows] = (
-                acc[n, index, rows]
-                + core_in[n, index, rows].astype(jnp.float32)
-                + first_in[n, index, rows].astype(jnp.float32)
-            )
-
-        over(count, step)
+
+    def fold_rest(ref, n, flight, count):
+        copies, base = flight
+        copies[1].wait_recv()
+        fold(ref, n, count // 2, arrived_at(base))
+
+    def product(group, carry):
+        fetch_group(group).wait()
+        place = lax.rem(group, AHEAD)
+        total = running[...]
+        for slot in range(GROUP):
+            k = group * GROUP + slot
+            term = contract(tiles[source_at[k]], blocks[place, slot], 1, 1)
+            total = total * carries[k] + term
+            sums[k] = total.astype(jnp.bfloat16)
+        running[...] = total
+
+        @pl.when(group + AHEAD < groups)
+        def _():
+            fetch_group(group + AHEAD).start()
+
+        return carry
+
+    def summed(position, rows):
+        return sums[ends[position], rows].astype(jnp.float32) * filled[position]
+
+    def spread(target, n, stages, source, start, size, at, landed, number):
+        for later in range(number, len(stages)):
+            place = at + start + (own << later)
+            copy = remote(source, target.at[pl.ds(place, size)], stages[later])
+            landed[later].append((start + (own << later), size, copy))
+
+    def forward(target, n, stages, at, landed, number):
+        for start, size, copy in landed[number]:
+            copy.wait_recv()
+            piece = target.at[pl.ds(at + start, size)]
+            spread(target, n, stages, piece, start, size, at, landed, number + 1)
+
+    def cross(source, target, at, start, size):
+        far_copies.append(remote(source, target.at[pl.ds(at + start, size)], 0))
+
+    far_copies = []
+    to_hidden_stages = [order[::-1] for order in orders]
+    to_near_stages = [order[::-1][:-1] for order in orders]
+    hidden_landed = [[[] for _ in stages] for stages in to_hidden_stages]
+    near_landed = [[[] for _ in stages] for stages in to_near_stages]
+    cut = own // 2
+    own_spans = ((cut, own - cut), (0, cut))
 
     pre_flight = [None, None]
-    count = half // 2
     for n in range(2):
-        for copy in loads[n]:
-            copy.wait()
+        loads[n].wait()
         pre_flight[n] = stage_send(
             n,
-            orders[n][1],
-            count,
-            lambda i, r, n=n: acc[n, count + i, r]
-            + core_in[n, count + i, r].astype(jnp.float32)
-            + first_in[n, count + i, r].astype(jnp.float32),
+            orders[n][0],
+            half,
+            lambda i, r, n=n: acc[n, i, r] + core_in[n, half + i, r].astype(jnp.float32),
+            (pre_core[n][0].wait_recv, pre_core[n][1].wait_recv),
         )
+        loads[n] = local(pre_keep.at[pl.ds(n * quarter, half)], acc.at[n])
     for n in range(2):
-        fold_front(n, count)
-
+        loads[n].wait()
+        pre_core[n][2].wait_recv()
+        fold(acc, n, half, lambda i, r: core_in[n, i, r].astype(jnp.float32))
+    running[...] = jnp.zeros(running.shape, jnp.float32)
+
+    count = half
+    marks = [0, groups // 3, 2 * groups // 3, groups]
+    for number, _ in enumerate(orders[0][1:]):
+        flights = [
+            pass_on(acc, n, pre_flight[n], count, orders[n][1 + number]) for n in range(2)
+        ]
+        if number == 0:
+            own_tokens.wait()
+            for copy in arrivals:
+                copy.wait_recv()
+            given = local(panel, cotangent_out)
+            for tile in range(tiles.shape[0]):
+                tiles[tile] = panel[:, tile * width : (tile + 1) * width]
+            lax.fori_loop(marks[0], marks[1], product, 0)
+        for n in range(2):
+            fold_rest(acc, n, pre_flight[n], count)
+        pre_flight = flights
+        count = count // 2
+    lax.fori_loop(marks[1], marks[2], product, 0)
+
+    kept = []
+    for number, (start, size) in enumerate(own_spans):
+        for n in range(2):
+            copies, base = pre_flight[n]
+            copies[number].wait_recv()
+
+            def act(index, r):
+                i = start + index
+                value, slope = gelu_and_slope(
+                    acc[n, i, r] + stage_in[base + i, r].astype(jnp.float32)
+                )
+                own_hidden[n, i, r] = value.astype(jnp.bfloat16)
+                acc[n, i, r] = slope
+
+            over(size, act)
+            piece = own_hidden.at[n, pl.ds(start, size)]
+            at = n * quarter
+            spread(
+                hidden, n, to_hidden_stages[n], piece, start, size, at, hidden_landed[n], 0
+            )
+            cross(piece, hidden, 2 * quarter + at, start, size)
+            kept.append(local(piece, hidden.at[pl.ds(at + start, size)]))
+        if number == 0:
+            lax.fori_loop(marks[2], marks[3], product, 0)
+
+    for copies, _ in pre_stages:
+        for copy in copies:
+            copy.wait_send()
+            started[:] = [other for other in started if other is not copy]
+    out_places[0] = 0
+    back_core = [[], []]
+    for first, size in spans:
+        for n in range(2):
+
+            def step(i, r):
+                value = summed(2 * quarter + n * quarter + first + i, r)
+                core_in[n, first + i, r] = value.astype(jnp.bfloat16)
+
+            over(size, step)
+            source = core_in.at[n, pl.ds(first, size)]
+            back_core[n].append(swap_core(n, (first, size), source, back_in))
     back_flight = [None, None]
     for n in range(2):
-        back_loads[n].wait()
-        core_swaps[n].wait_recv()
         back_flight[n] = stage_send(
             n,
             orders[n][0],
             half,
-            lambda i, r, n=n: back[n, half + i, r] + back_in[n, half + i, r].astype(jnp.float32),
+            lambda i, r, n=n: summed(n * quarter + half + i, r)
+            + back_in[n, half + i, r].astype(jnp.float32),
+            (back_core[n][0].wait_recv, back_core[n][1].wait_recv),
         )
-
-    def settle(ref, n, flight, count, later):
-        for bit in later:
-            copy, base = flight
-            copy.wait_recv()
-            lower = count // 2
-
-            def value(i, r):
-                return ref[n, lower + i, r] + stage_in[base + lower + i, r].astype(jnp.float32)
-
-            flight = stage_send(n, bit, lower, value)
-
-            def fold(i, r):
-                ref[n, i, r] = ref[n, i, r] + stage_in[base + i, r].astype(jnp.float32)
-
-            over(lower, fold)
-            count = lower
-        return flight
-
-    gathers = [None, None]
-    kept = [None, None]
     for n in range(2):
-        flight, base = settle(acc, n, pre_flight[n], count, orders[n][2:])
-        flight.wait_recv()
-
-        def act(i, r):
-            value, slope = gelu_and_slope(
-                acc[n, i, r] + stage_in[base + i, r].astype(jnp.float32)
-            )
-            own_hidden[n, i, r] = value.astype(jnp.bfloat16)
-            acc[n, i, r] = slope
-
-        over(own, act)
-        start = n * quarter
-        kept[n] = local(own_hidden.at[n], hidden.at[pl.ds(start, own)])
-        gathers[n] = remote(
-            own_hidden.at[n], hidden.at[pl.ds(start + own, own)], orders[n][-1]
-        )
-
+        forward(hidden, n, to_hidden_stages[n], n * quarter, hidden_landed[n], 0)
     for n in range(2):
-        core_swaps[2 + n].wait_recv()
-
-        def fold(i, r):
-            back[n, i, r] = back[n, i, r] + back_in[n, i, r].astype(jnp.float32)
-
-        over(half, fold)
+        back_core[n][2].wait_recv()
+
+        def begin(i, r):
+            back[n, i, r] = summed(n * quarter + i, r) + back_in[
+                n, i, r
+            ].astype(jnp.float32)
+
+        over(half, begin)
+
+    def cross_landed(target, other, n, at, there, landed, number):
+        for start, size, copy in landed[number]:
+            cross(target.at[pl.ds(at + start, size)], other, there, start, size)
 
     for n in range(2):
-        flight, base = back_flight[n]
-        back_flight[n] = settle(back, n, back_flight[n], half, orders[n][1:2])
-
-    for n in range(2):
-        start = n * quarter
-        size = own
-        kept[n].wait()
-        for bit in orders[n][::-1][1:]:
-            gathers[n].wait_recv()
-            size = size * 2
-            gathers[n] = remote(
-                hidden.at[pl.ds(start, size)], hidden.at[pl.ds(start + size, size)], bit
-            )
-    far_copies = []
-    for n in range(2):
-        start = n * quarter
-        far_copies.append(
-            remote(
-                hidden.at[pl.ds(start, half)], hidden.at[pl.ds(2 * quarter + start, half)], 0
-            )
-        )
-
-    spread = [None, None]
-    held = [None, None]
-    for n in range(2):
-        flight, base = settle(back, n, back_flight[n], half // 2, orders[n][2:])
-        flight.wait_recv()
-
-        def cotangent(i, r):
-            value = back[n, i, r] + stage_in[base + i, r].astype(jnp.float32)
-            own_back[n, i, r] = (value * acc[n, i, r]).astype(jnp.bfloat16)
-
-        over(own, cotangent)
-        held[n] = local(own_back.at[n], near[n].at[pl.ds(0, own)])
-        spread[n] = remote(own_back.at[n], near[n].at[pl.ds(own, own)], orders[n][-1])
-
-    for n in range(2):
-        size = own
-        held[n].wait()
-        for bit in orders[n][::-1][1:-1]:
-            spread[n].wait_recv()
-            size = size * 2
-            spread[n] = remote(near[n].at[pl.ds(0, size)], near[n].at[pl.ds(size, size)], bit)
-        spread[n].wait_recv()
-        far_copies.append(remote(near[n], far[n], 0))
-
-    for n in range(2):
-        gathers[n].wait_recv()
-        start = n * quarter + half
-        far_copies.append(
-            remote(
-                hidden.at[pl.ds(start, half)], hidden.at[pl.ds(2 * quarter + start, half)], 0
-            )
-        )
+        at = n * quarter
+        cross_landed(hidden, hidden, n, at, 2 * quarter + at, hidden_landed[n], 0)
+
+    count = half
+    for number, _ in enumerate(orders[0][1:]):
+        flights = [
+            pass_on(back, n, back_flight[n], count, orders[n][1 + number]) for n in range(2)
+        ]
+        for n in range(2):
+            fold_rest(back, n, back_flight[n], count)
+        back_flight = flights
+        count = count // 2
+
+    for number, (start, size) in enumerate(own_spans):
+        for n in range(2):
+            copies, base = back_flight[n]
+            copies[number].wait_recv()
+
+            def slope_times(index, r):
+                i = start + index
+                value = back[n, i, r] + stage_in[base + i, r].astype(jnp.float32)
+                own_back[n, i, r] = (value * acc[n, i, r]).astype(jnp.bfloat16)
+
+            over(size, slope_times)
+            piece = own_back.at[n, pl.ds(start, size)]
+            spread(near[n], n, to_near_stages[n], piece, start, size, 0, near_landed[n], 0)
+            cross(piece, far[n], 0, start, size)
+            kept.append(local(piece, near[n].at[pl.ds(start, size)]))
+
+    for number in range(1, len(to_hidden_stages[0])):
+        for n in range(2):
+            at = n * quarter
+            forward(hidden, n, to_hidden_stages[n], at, hidden_landed[n], number)
+            cross_landed(hidden, hidden, n, at, 2 * quarter + at, hidden_landed[n], number)
+    for number in range(len(to_near_stages[0])):
+        for n in range(2):
+            forward(near[n], n, to_near_stages[n], 0, near_landed[n], number)
+            cross_landed(near[n], far[n], n, 0, 0, near_landed[n], number)
+    given.wait()
+    for copy in kept:
+        copy.wait()
     for copy in far_copies:
         copy.wait_recv()
     for copy in started:
         copy.wait_send()
 
 
-def exchange(pre_keep, pre_core, pre_first, back_keep, back_send):
+def exchange(pre_keep, pre_send, cotangent, weights, source_at, carries, ends, filled):
     held, tokens, width = pre_keep.shape
+    columns = cotangent.shape[1]
+    slots = weights.shape[0]
     segments = 2 * held
     quarter = held // 2
     half = quarter // 2
     bits = int(math.log2(lax.axis_size("row")))
+    members = lax.axis_size("col")
     own = quarter >> (bits - 1)
-    staged = 2 * (half - own) + 2 * (quarter - own)
-    copies = 4 + 2 * (bits - 2) + 2 * (bits - 1) + 2 * (bits - 1) + 2 * (bits - 2) + 6
+    staged = 2 * (quarter - own)
+    copies = members - 1 + 12 + 8 * (bits - 1) + 16 * (quarter // own)
     wide, narrow = jnp.float32, jnp.bfloat16
 
     def hbm(count):
         return jax.ShapeDtypeStruct((count, tokens, width), narrow)
 
     return pl.pallas_call(
-        functools.partial(exchange_kernel, (segments, quarter, own, bits)),
-        in_specs=[pl.BlockSpec(memory_space=pl.ANY)] * 6,
-        out_specs=[pl.BlockSpec(memory_space=pl.ANY)] * 5,
-        out_shape=[hbm(segments)] + [hbm(half)] * 4,
+        functools.partial(exchange_kernel, (quarter, own, bits, members)),
+        in_specs=[pl.BlockSpec(memory_space=pltpu.SMEM)] * 4
+        + [pl.BlockSpec(memory_space=pl.ANY)] * 4,
+        out_specs=[pl.BlockSpec(memory_space=pl.ANY)] * 6,
+        out_shape=[hbm(segments)]
+        + [hbm(half)] * 4
+        + [jax.ShapeDtypeStruct((tokens, columns), narrow)],
         scratch_shapes=[
             pltpu.VMEM((2, half, tokens, width), wide),
-            pltpu.VMEM((2, half, tokens, width), narrow),
-            pltpu.VMEM((2, half, tokens, width), narrow),
-            pltpu.VMEM((2, quarter, tokens, width), wide),
+            pltpu.VMEM((2, quarter, tokens, width), narrow),
+            pltpu.VMEM((2, half, tokens, width), wide),
             pltpu.VMEM((2, quarter, tokens, width), narrow),
             pltpu.VMEM((staged, tokens, width), narrow),
-            pltpu.VMEM((staged, tokens, width), narrow),
+            pltpu.VMEM((2 * staged, tokens, width), narrow),
             pltpu.VMEM((2, own, tokens, width), narrow),
             pltpu.VMEM((2, own, tokens, width), narrow),
-            pltpu.SemaphoreType.DMA((12,)),
+            pltpu.VMEM((tokens, columns), narrow),
+            pltpu.VMEM((columns // width, tokens, width), narrow),
+            pltpu.VMEM((AHEAD, GROUP, width, width), narrow),
+            pltpu.VMEM((tokens, width), wide),
+            pltpu.VMEM((slots, tokens, width), narrow),
+            pltpu.SemaphoreType.DMA((16,)),
+            pltpu.SemaphoreType.DMA((AHEAD,)),
             pltpu.SemaphoreType.DMA((copies,)),
             pltpu.SemaphoreType.DMA((copies,)),
         ],
@@ -536,11 +654,11 @@
             collective_id=1, has_side_effects=True, vmem_limit_bytes=VMEM_LIMIT
         ),
         cost_estimate=pl.CostEstimate(
-            flops=40 * segments * tokens * width,
+            flops=8 * slots * tokens * width * width,
             bytes_accessed=30 * segments * tokens * width // 2,
             transcendentals=2 * own * tokens * width,
         ),
-    )(pre_keep, pre_core, *pre_first, back_keep, back_send)
+    )(source_at, carries, ends, filled, pre_keep, pre_send, cotangent, weights)
 
 
 RELAY_ROWS = 16
@@ -689,16 +807,20 @@
     weights_two = second_blocks[0, 0]
 
     inputs_all = relay_tokens(activations)
-    cotangent_all = gather_tokens(after(grad_out, inputs_all))
     pre_keep, pre_send = to_hidden(
         inputs_all, weights_one, model_one, target_one, col_tiles, False
     )
-    pre_core, pre_sent, pre_first = scatter_begin(pre_keep, after(pre_send, cotangent_all))
-    back_keep, back_send = to_hidden(
-        after(cotangent_all, *pre_sent), weights_two, model_two, target_two, col_tiles, True
-    )
-    hidden, near_a, near_b, far_a, far_b = exchange(
-        pre_keep, pre_core, pre_first, back_keep, back_send
+    same = (target_two[1:] == target_two[:-1]).astype(jnp.float32)
+    carries = jnp.concatenate([jnp.zeros((1,), jnp.float32), same])
+    numbers = jnp.arange(target_two.shape[0], dtype=jnp.int32)
+    places = jnp.arange(col_tiles, dtype=jnp.int32)
+    lasts = jnp.max(
+        jnp.where(target_two[None, :] == places[:, None], numbers[None, :], -1), axis=1
+    )
+    ends = jnp.maximum(lasts, 0)
+    filled = (lasts >= 0).astype(jnp.float32)
+    hidden, near_a, near_b, far_a, far_b, cotangent_all = exchange(
+        pre_keep, pre_send, grad_out, weights_two, model_two, carries, ends, filled
     )
     orders = swap_orders()
     last_a, last_b = swap(near_a, orders[0][0]), swap(near_b, orders[1][0])

time: 274 us -> 264 us (0.964)
  starting transfers between devices: 18.4 us -> 11.1 us
  Pallas kernels: 226 us -> 229 us
    pallas_call x1, Pallas kernels: 101 us -> 125 us  [exchange(): pl.pallas_call(functools.partial(exchange_kernel, (quarter, own, bits, me...]
    pallas_call x2 -> x1, Pallas kernels: 44.4 us -> 22.1 us  [to_hidden(): pl.pallas_call(functools.partial(to_hidden_kernel, flipped), grid_spec=pl...]
    ppermute x9 -> x6, waiting for transfers between devices: 2.49 us -> 11.3 us  [shift(): lax.ppermute(values, 'col', [(s, (s + distance) % count) for s in range(c...]
    ppermute x7 -> x4, waiting for transfers between devices: 11.5 us -> 3 us  [swap(): lax.ppermute(values, 'row', [(s, s ^ 1 << bit) for s in range(count)])]
    ppermute x9 -> x6, starting transfers between devices: 13.5 us -> 7.46 us  [shift(): lax.ppermute(values, 'col', [(s, (s + distance) % count) for s in range(c...]
    convert_element_type x1, other arithmetic: 5.38 us -> 0.59 us  [body(): filled = (lasts >= 0).astype(jnp.float32)]
  transfers between devices with their start and end apart: 16 -> 10, of which waited for: 7 -> 3; matrix products, arithmetic and copies ran while one was open for 2% -> 1% of each run, Pallas kernels for 39% -> 24%
where the time goes in v2:
time: 264 us; the launch traced here: 263 us
  Pallas kernels  229 us (87%)
  waiting for transfers between devices  14.3 us (5%)
  starting transfers between devices  11.1 us (4%)
  other arithmetic  8.43 us (3%)
    pallas_call x1, Pallas kernels, exchange(): pl.pallas_call(functools.partial(exchange_kernel, (quarter, own, bits, me...  125 us
    pallas_call x3, Pallas kernels, to_model(): pl.pallas_call(kernel, grid_spec=pltpu.PrefetchScalarGridSpec(num_scalar_...  62.2 us
    pallas_call x1, Pallas kernels, to_hidden(): pl.pallas_call(functools.partial(to_hidden_kernel, flipped), grid_spec=pl...  22.1 us
    pallas_call x1, Pallas kernels, relay_tokens(): pl.pallas_call(functools.partial(relay_kernel, members), in_specs=[pl.Blo...  19.2 us
    ppermute x6, waiting for transfers between devices, shift(): lax.ppermute(values, 'col', [(s, (s + distance) % count) for s in range(c...  11.3 us
    ppermute x6, starting transfers between devices, shift(): lax.ppermute(values, 'col', [(s, (s + distance) % count) for s in range(c...  7.46 us
  transfers between devices with their start and end apart: 10, of which 3 were waited for; matrix products, arithmetic and copies ran while one was open for 1% of the time, Pallas kernels for 24%

profile of v2, /device:TPU:12, one launch (start us, length us, event | category | flops | bytes accessed | tf_op | source)
XLA Modules:
  0.0 263.2 jit_solution(15686179786046304202)
XLA Ops:
  0.6 0.7 compare_reduce_fusion
  1.4 0.7 compare_reduce_fusion.1
  2.1 0.8 subtract_reduce_fusion
  2.9 0.6 broadcast_select_fusion.1
  3.5 0.1 select_reduce_fusion
  3.6 0.1 slice_compare_fusion
  3.7 0.6 compare_convert_fusion.refs_3_
  4.2 0.6 broadcast_maximum_fusion.refs_2_
  4.8 19.2 %shard_map.93.panel.refs_3_ = bf16[256,2048]{1,0:T(8,128)(2,1)} custom-call(bf16[64,2048]{1,0:T(8,128)(2,1)} %own_ref.1), custom_call_target="tpu_custom_call" | custom-call | tf_op jit(solution)/shard_map/pallas_call | solution.py:754
  24.0 0.7 add_convert_fusion.refs_1_
  24.7 0.6 broadcast_select_fusion
  25.3 22.1 %shard_map.94 = (f32[64,256,128]{2,1,0:T(8,128)}, bf16[64,256,128]{2,1,0:T(8,128)(2,1)}) custom-call(s32[384]{0:T(512)} %get-tuple-element.72.source.refs_0_, s32[384]{0:T(512)} %get-tuple-element.68.target, bf16[256,2048]{1,0:T(8,128)(2,1)} %shard_map.93.panel.refs_3_, bf16[384,128,128]{2,1,0:T(8,128)(2,1)} %bitcast.6), custom_call_target="tpu_custom_call" | custom-call | flops 12884901888 | bytes 25165824 | tf_op jit(solution)/shard_map/pallas_call | solution.py:65
  47.4 125.1 %shard_map.95 = (bf16[128,256,128]{2,1,0:T(8,128)(2,1)}, bf16[16,256,128]{2,1,0:T(8,128)(2,1)}, bf16[16,256,128]{2,1,0:T(8,128)(2,1)}, bf16[16,256,128]{2,1,0:T(...) custom-call(s32[384]{0:T(512)} %get-tuple-element.73.refs_0_, f32[384]{0:T(512)} %add_convert_fusion.refs_1_, ...), custom_call_target="tpu_custom_call" | custom-call | flops 12884901888 | bytes 62914560 | tf_op jit(solution)/shard_map/pallas_call | solution.py:626
  172.5 1.7 collective-permute-start
  174.2 1.4 collective-permute-start.1
  175.5 0.5 convert_element_type.28.refs_2_
  176.1 25.1 %shard_map.96 = (bf16[384,128,128]{2,1,0:T(8,128)(2,1)}, f32[64,2048]{1,0:T(8,128)}, bf16[64,2048]{1,0:T(8,128)(2,1)}, bf16[64,2048]{1,0:T(8,128)(2,1)}, bf16[64,2048]{1,0:T(8,128)(2,1)}) custom-call(s32[384]{0:T(512)} %get-tuple-element.73.refs_0_, s32[384]{0:T(512)} %get-tuple-element.71.refs_1_, s32[384]{0:T(512)} %convert_element_type.28.refs_2_, ...), custom_call_target="tpu_custom_call" | custom-call | flops 25769803776 | bytes 33554432 | tf_op jit(solution)/shard_map/pallas_call | solution.py:187
  201.2 0.0 collective-permute-done.1.refs_7_
  201.2 0.0 copy-start.3
  201.2 0.0 collective-permute-done.refs_5_
  201.2 0.0 copy-start.2
  201.2 0.1 collective-permute-start.2
  201.3 0.5 collective-permute-start.3
  201.8 0.6 convert_element_type.33.refs_2_
  202.4 1.5 collective-permute-done.2.refs_9_
  203.9 0.0 copy-start.4
  203.9 1.5 collective-permute-done.3.refs_11_
  205.4 0.0 copy-start.5
  205.4 0.6 collective-permute-start.4
  206.1 2.9 %collective-permute-start.5 = (bf16[64,2048]{1,0:T(8,128)(2,1)}, bf16[64,2048]{1,0:T(8,128)(2,1)S(1)}, u32[]{:S(2)}, u32[]{:S(2)}) collective-permute-start(bf16[64,2048]{1,0:T(8,128)(2,1)} %get-tuple-element.49), channel_id=1, source_target_pairs={{0,2},{1,3},{2,0},{3,1},{4,6},{5,7},{6,4},{7,5},{8,10},{9,11},{10,... | collective-permute-start | bytes 786440 | tf_op jit(solution)/shard_map/ppermute | solution.py:770
  209.0 0.2 collective-permute-start.6
  209.3 0.0 copy-done.5
  209.3 0.0 copy-done.3
  209.3 0.0 copy-done.2
  209.3 0.0 copy-done.4
  209.3 0.0 copy-start
  209.3 18.7 %shard_map.97 = (f32[64,2048]{1,0:T(8,128)}, bf16[64,2048]{1,0:T(8,128)(2,1)}, bf16[64,2048]{1,0:T(8,128)(2,1)}, bf16[64,2048]{1,0:T(8,128)(2,1)}) custom-call(s32[384]{0:T(512)} %get-tuple-element.72.source.refs_0_, s32[384]{0:T(512)} %get-tuple-element.69.refs_1_, s32[384]{0:T(512)} %convert_element_type.33.refs_2_, bf16[384,128,128]{2,1,0:T(8,128)(2,1)} %bitcast.7, ...), custom_call_target="tpu_custom_call" | custom-call | flops 12884901888 | bytes 33554432 | tf_op jit(solution)/shard_map/pallas_call | solution.py:187
  228.0 1.8 collective-permute-start.7
  229.8 1.8 collective-permute-start.8
  231.6 0.0 collective-permute-done.4
  231.6 0.0 collective-permute-start.9
  231.6 0.0 collective-permute-done.5
  231.6 11.3 %collective-permute-done.6 = bf16[64,2048]{1,0:T(8,128)(2,1)S(1)} collective-permute-done((bf16[64,2048]{1,0:T(8,128)(2,1)}, bf16[64,2048]{1,0:T(8,128)(2,1)S(1)}, u32[]{:S(2)}, u32[]{:S(2)}) %collective-permute-start.6) | collective-permute-done | bytes 262176 | tf_op jit(solution)/shard_map/ppermute | solution.py:770
  243.0 0.0 copy-done
  243.0 0.9 convert_add_fusion.1
  243.9 0.0 copy-start.1
  243.9 18.4 %shard_map.98 = bf16[384,128,128]{2,1,0:T(8,128)(2,1)} custom-call(s32[384]{0:T(512)} %get-tuple-element.72.source.refs_0_, s32[384]{0:T(512)} %get-tuple-element.69.refs_1_, s32[384]{0:T(512)} %convert_element_type.33.refs_2_, bf16[256,2048]{1,0:T(8,128)(2,1)} %shard_map.93.panel.refs_3_, bf16[16,256,128]{2,1,0:T(8,128)(2,1)} %get-tuple-element.55.refs_4_, ...), custom_call_target="tpu_custom_call" | custom-call | flops 12884901888 | bytes 33554432 | tf_op jit(solution)/shard_map/pallas_call | solution.py:187
  262.3 0.0 collective-permute-done.7
  262.3 0.0 collective-permute-done.8
  262.3 0.0 collective-permute-done.9
  262.3 0.0 copy-done.1
  262.3 0.9 convert_add_fusion
Async XLA Ops:
  172.5 28.7 %collective-permute-start = (bf16[16,256,128]{2,1,0:T(8,128)(2,1)}, bf16[16,256,128]{2,1,0:T(8,128)(2,1)S(1)}, u32[]{:S(2)}, u32[]{:S(2)}) collective-permute-start(bf16[16,256,128]{2,1,0:T(8,128)(2,1)} %get-tuple-element.55.refs_4_), channel_id=1, source_target_pairs={{0,8},{4,12},{8,0},{12,4},{16,24},{20,28},{24,16},{28,20},{1,9},{5... | collective-permute-start | bytes 3145736 | tf_op jit(solution)/shard_map/ppermute | solution.py:208
  174.2 27.0 %collective-permute-start.1 = (bf16[16,256,128]{2,1,0:T(8,128)(2,1)}, bf16[16,256,128]{2,1,0:T(8,128)(2,1)S(1)}, u32[]{:S(2)}, u32[]{:S(2)}) collective-permute-start(bf16[16,256,128]{2,1,0:T(8,128)(2,1)} %get-tuple-element.57.refs_6_), channel_id=1, source_target_pairs={{0,16},{4,20},{8,24},{12,28},{16,0},{20,4},{24,8},{28,12},{1,17},{... | collective-permute-start | bytes 3145736 | tf_op jit(solution)/shard_map/ppermute | solution.py:208
  201.2 8.1 %copy-start.3 = (bf16[16,256,128]{2,1,0:T(8,128)(2,1)}, bf16[16,256,128]{2,1,0:T(8,128)(2,1)S(1)}, u32[]{:S(2)}) copy-start(bf16[16,256,128]{2,1,0:T(8,128)(2,1)S(1)} %collective-permute-done.1.refs_7_) | copy-start | bytes 3145732
  201.2 8.1 %copy-start.2 = (bf16[16,256,128]{2,1,0:T(8,128)(2,1)}, bf16[16,256,128]{2,1,0:T(8,128)(2,1)S(1)}, u32[]{:S(2)}) copy-start(bf16[16,256,128]{2,1,0:T(8,128)(2,1)S(1)} %collective-permute-done.refs_5_) | copy-start | bytes 3145732
  201.2 2.7 %collective-permute-start.2 = (bf16[16,256,128]{2,1,0:T(8,128)(2,1)S(1)}, bf16[16,256,128]{2,1,0:T(8,128)(2,1)S(1)}, u32[]{:S(2)}, u32[]{:S(2)}) collective-permute-start(bf16[16,256,128]{2,1,0:T(8,128)(2,1)S(1)} %collective-permute-done.refs_5_), channel_id=1, source_target_pairs={{0,4},{4,0},{8,12},{12,8},{16,20},{20,16},{24,28},{28,24},{1,5},{5... | collective-permute-start | bytes 3145736 | tf_op jit(solution)/shard_map/ppermute | solution.py:208
  201.3 4.1 %collective-permute-start.3 = (bf16[16,256,128]{2,1,0:T(8,128)(2,1)S(1)}, bf16[16,256,128]{2,1,0:T(8,128)(2,1)S(1)}, u32[]{:S(2)}, u32[]{:S(2)}) collective-permute-start(bf16[16,256,128]{2,1,0:T(8,128)(2,1)S(1)} %collective-permute-done.1.refs_7_), channel_id=1, source_target_pairs={{0,4},{4,0},{8,12},{12,8},{16,20},{20,16},{24,28},{28,24},{1,5},{5... | collective-permute-start | bytes 3145736 | tf_op jit(solution)/shard_map/ppermute | solution.py:208
  203.9 5.3 %copy-start.4 = (bf16[16,256,128]{2,1,0:T(8,128)(2,1)}, bf16[16,256,128]{2,1,0:T(8,128)(2,1)S(1)}, u32[]{:S(2)}) copy-start(bf16[16,256,128]{2,1,0:T(8,128)(2,1)S(1)} %collective-permute-done.2.refs_9_) | copy-start | bytes 3145732
  205.4 3.8 %copy-start.5 = (bf16[16,256,128]{2,1,0:T(8,128)(2,1)}, bf16[16,256,128]{2,1,0:T(8,128)(2,1)S(1)}, u32[]{:S(2)}) copy-start(bf16[16,256,128]{2,1,0:T(8,128)(2,1)S(1)} %collective-permute-done.3.refs_11_) | copy-start | bytes 3145732
  205.4 26.2 %collective-permute-start.4 = (bf16[64,2048]{1,0:T(8,128)(2,1)}, bf16[64,2048]{1,0:T(8,128)(2,1)S(1)}, u32[]{:S(2)}, u32[]{:S(2)}) collective-permute-start(bf16[64,2048]{1,0:T(8,128)(2,1)} %get-tuple-element.48), channel_id=1, source_target_pairs={{0,1},{1,2},{2,3},{3,0},{4,5},{5,6},{6,7},{7,4},{8,9},{9,10},{10,1... | collective-permute-start | bytes 786440 | tf_op jit(solution)/shard_map/ppermute | solution.py:770
  206.1 25.6 %collective-permute-start.5 = (bf16[64,2048]{1,0:T(8,128)(2,1)}, bf16[64,2048]{1,0:T(8,128)(2,1)S(1)}, u32[]{:S(2)}, u32[]{:S(2)}) collective-permute-start(bf16[64,2048]{1,0:T(8,128)(2,1)} %get-tuple-element.49), channel_id=1, source_target_pairs={{0,2},{1,3},{2,0},{3,1},{4,6},{5,7},{6,4},{7,5},{8,10},{9,11},{10,... | collective-permute-start | bytes 786440 | tf_op jit(solution)/shard_map/ppermute | solution.py:770
  209.0 33.9 %collective-permute-start.6 = (bf16[64,2048]{1,0:T(8,128)(2,1)}, bf16[64,2048]{1,0:T(8,128)(2,1)S(1)}, u32[]{:S(2)}, u32[]{:S(2)}) collective-permute-start(bf16[64,2048]{1,0:T(8,128)(2,1)} %get-tuple-element.50), channel_id=1, source_target_pairs={{0,3},{1,0},{2,1},{3,2},{4,7},{5,4},{6,5},{7,6},{8,11},{9,8},{10,9... | collective-permute-start | bytes 786440 | tf_op jit(solution)/shard_map/ppermute | solution.py:770
  209.3 33.7 %copy-start = (f32[64,2048]{1,0:T(8,128)S(1)}, f32[64,2048]{1,0:T(8,128)}, u32[]{:S(2)}) copy-start(f32[64,2048]{1,0:T(8,128)} %get-tuple-element.38) | copy-start | bytes 1572868
  228.0 34.3 %collective-permute-start.7 = (bf16[64,2048]{1,0:T(8,128)(2,1)}, bf16[64,2048]{1,0:T(8,128)(2,1)S(1)}, u32[]{:S(2)}, u32[]{:S(2)}) collective-permute-start(bf16[64,2048]{1,0:T(8,128)(2,1)} %get-tuple-element.52), channel_id=1, source_target_pairs={{0,1},{1,2},{2,3},{3,0},{4,5},{5,6},{6,7},{7,4},{8,9},{9,10},{10,1... | collective-permute-start | bytes 786440 | tf_op jit(solution)/shard_map/ppermute | solution.py:770
  229.8 32.5 %collective-permute-start.8 = (bf16[64,2048]{1,0:T(8,128)(2,1)}, bf16[64,2048]{1,0:T(8,128)(2,1)S(1)}, u32[]{:S(2)}, u32[]{:S(2)}) collective-permute-start(bf16[64,2048]{1,0:T(8,128)(2,1)} %get-tuple-element.53), channel_id=1, source_target_pairs={{0,2},{1,3},{2,0},{3,1},{4,6},{5,7},{6,4},{7,5},{8,10},{9,11},{10,... | collective-permute-start | bytes 786440 | tf_op jit(solution)/shard_map/ppermute | solution.py:770
  231.6 30.7 %collective-permute-start.9 = (bf16[64,2048]{1,0:T(8,128)(2,1)}, bf16[64,2048]{1,0:T(8,128)(2,1)S(1)}, u32[]{:S(2)}, u32[]{:S(2)}) collective-permute-start(bf16[64,2048]{1,0:T(8,128)(2,1)} %get-tuple-element.54), channel_id=1, source_target_pairs={{0,3},{1,0},{2,1},{3,2},{4,7},{5,4},{6,5},{7,6},{8,11},{9,8},{10,9... | collective-permute-start | bytes 786440 | tf_op jit(solution)/shard_map/ppermute | solution.py:770
  243.9 18.5 %copy-start.1 = (f32[64,2048]{1,0:T(8,128)S(1)}, f32[64,2048]{1,0:T(8,128)}, u32[]{:S(2)}) copy-start(f32[64,2048]{1,0:T(8,128)} %get-tuple-element.51) | copy-start | bytes 1572868

commit v3 on v2

--- a/solution.py
+++ b/solution.py
@@ -99,13 +99,16 @@
         copy.wait()
 
 
-def to_model_kernel(transposed, pieces, with_sums, with_grads, model_at, hidden_at, live, *refs):
+def to_model_kernel(transposed, pieces, with_sums, with_grads, carried, model_at, hidden_at, live, *refs):
     refs = list(refs)
     panel = refs.pop(0) if with_grads else None
     weights = refs.pop(0) if with_sums else None
     hidden_parts = [refs.pop(0) for _ in range(pieces)]
+    carried_in = refs.pop(0) if carried else None
     grads = refs.pop(0) if with_grads else None
-    own, send, totals = [refs.pop(0) for _ in range(3)] if with_sums else (None, None, None)
+    own, send = [refs.pop(0) for _ in range(2)] if with_sums else (None, None)
+    carried_out = refs.pop(0) if carried else None
+    totals = refs.pop(0) if with_sums else None
     hidden, sems = refs
     step = pl.program_id(0)
     width = hidden.shape[-1]
@@ -115,6 +118,9 @@
         if with_sums:
             totals[...] = jnp.zeros(totals.shape, jnp.float32)
         fetch(hidden_parts, hidden, sems)
+
+    if carried:
+        carried_out[...] = carried_in[...]
 
     for slot in range(CHUNK):
         k = step * CHUNK + slot
@@ -146,7 +152,15 @@
 
 
 def to_model(
-    panel, hidden_parts, weights, places, members, transposed, with_sums=True, with_grads=True
+    panel,
+    hidden_parts,
+    weights,
+    places,
+    members,
+    transposed,
+    with_sums=True,
+    with_grads=True,
+    carried=None,
 ):
     tokens, columns = panel.shape
     slots, width, _ = weights.shape
@@ -175,21 +189,30 @@
         pltpu.VMEM((hidden_count, tokens, width), jnp.bfloat16),
         pltpu.SemaphoreType.DMA((pieces,)),
     ]
+    extra, extra_specs = [], []
+    if carried is not None:
+        extra = [carried]
+        carried_spec = pl.BlockSpec(
+            (CHUNK // 2, 2 * width, width), lambda s, a, b, c: (s, 0, 0)
+        )
+        extra_specs.append(carried_spec)
+        out_specs.append(carried_spec)
+        out_shape.append(jax.ShapeDtypeStruct(carried.shape, carried.dtype))
 
     def kernel(*refs):
         flat = list(refs)
         if with_sums:
-            start = 3 + len(operands) + pieces + (1 if with_grads else 0) + 1
+            start = 3 + len(operands) + pieces + len(extra) + (1 if with_grads else 0) + 1
             if not isinstance(flat[start], (list, tuple)):
                 flat[start : start + members - 1] = [flat[start : start + members - 1]]
-        to_model_kernel(transposed, pieces, with_sums, with_grads, *flat)
+        to_model_kernel(transposed, pieces, with_sums, with_grads, carried is not None, *flat)
 
     return pl.pallas_call(
         kernel,
         grid_spec=pltpu.PrefetchScalarGridSpec(
             num_scalar_prefetch=3,
             grid=(slots // CHUNK,),
-            in_specs=in_specs + [pl.BlockSpec(memory_space=pl.ANY)] * pieces,
+            in_specs=in_specs + [pl.BlockSpec(memory_space=pl.ANY)] * pieces + extra_specs,
             out_specs=out_specs,
             scratch_shapes=scratch,
         ),
@@ -200,7 +223,7 @@
             bytes_accessed=4 * weights.size + 2 * hidden_count * tokens * width,
             transcendentals=0,
         ),
-    )(*places, *operands, *hidden_parts)
+    )(*places, *operands, *hidden_parts, *extra)
 
 
 def swap(values, bit):
@@ -252,23 +275,29 @@
 
 
 GROUP = 32
-AHEAD = 3
+AHEAD = 2
+EXCHANGE_LIMIT = 62 * 1024 * 1024
 
 
 def exchange_kernel(sizes, *refs):
     quarter, own, bits, members = sizes
     refs = list(refs)
     source_at, carries, ends, filled = refs[0:4]
-    pre_keep, pre_send, cotangent, weights = refs[4:8]
-    hidden, near, far, cotangent_out = refs[8], refs[9:11], refs[11:13], refs[13]
-    (acc, core_in, back, back_in, stage_out, stage_in, own_hidden, own_back) = refs[14:22]
-    (panel, tiles, blocks, running, sums) = refs[22:27]
-    local_sems, block_sems, send_sems, recv_sems = refs[27:]
+    hidden_at, alive, sorted_at, block_at, chain, part_ends, part_filled = refs[4:11]
+    pre_keep, pre_send, cotangent, weights = refs[11:15]
+    hidden, spread_back, grads, output = refs[15:19]
+    (parts, hold, back_all, stage_out, stage_in, own_hidden, own_back) = refs[19:26]
+    (panel, tiles, blocks, running, sums, slopes, out, landing, chosen) = refs[26:35]
+    local_sems, block_sems, grad_sems, send_sems, recv_sems = refs[35:]
     half = quarter // 2
     row = lax.axis_index("row")
     col = lax.axis_index("col")
     orders = [list(range(1, bits)), list(range(1, bits))[::-1]]
-    tokens, width = acc.shape[2:]
+    tokens, width = parts.shape[1:]
+    acc = [parts.at[pl.ds(n * half, half)] for n in range(2)]
+    back = [back_all.at[n] for n in range(2)]
+    core_in = [hold.at[pl.ds(n * quarter, quarter)] for n in range(2)]
+    back_in = [hold.at[pl.ds((2 + n) * quarter, quarter)] for n in range(2)]
     share = tokens // members
     slots = weights.shape[0]
     groups = slots // GROUP
@@ -313,7 +342,7 @@
             weights.at[pl.ds(group * GROUP, GROUP)], blocks.at[place], block_sems.at[place]
         )
 
-    loads = [local(pre_keep.at[pl.ds(n * quarter + half, half)], acc.at[n]) for n in range(2)]
+    loads = [local(pre_keep.at[pl.ds(n * quarter + half, half)], acc[n]) for n in range(2)]
     own_tokens = local(cotangent, panel.at[pl.ds(0, share)])
     for group in range(min(AHEAD, groups)):
         fetch_group(group).start()
@@ -339,7 +368,7 @@
     spans = ((half + low, low), (half, low), (0, half))
 
     def swap_core(n, span, source, target):
-        return remote(source, target.at[n, pl.ds(*span)], 0)
+        return remote(source, target[n].at[pl.ds(*span)], 0)
 
     pre_core = [[], []]
     for span in spans:
@@ -396,13 +425,13 @@
             n,
             bit,
             lower,
-            lambda i, r: ref[n, lower + i, r] + term(lower + i, r),
+            lambda i, r: ref[n][lower + i, r] + term(lower + i, r),
             (nothing, nothing),
         )
 
     def fold(ref, n, count, term):
         def step(i, r):
-            ref[n, i, r] = ref[n, i, r] + term(i, r)
+            ref[n][i, r] = ref[n][i, r] + term(i, r)
 
         over(count, step)
 
@@ -446,11 +475,18 @@
     def cross(source, target, at, start, size):
         far_copies.append(remote(source, target.at[pl.ds(at + start, size)], 0))
 
+    def move_on(target, landed, number):
+        for n in range(2):
+            at = n * quarter
+            forward(target, n, to_hidden_stages[n], at, landed[n], number)
+            for start, size, _ in landed[n][number]:
+                piece = target.at[pl.ds(at + start, size)]
+                cross(piece, target, 2 * quarter + at, start, size)
+
     far_copies = []
     to_hidden_stages = [order[::-1] for order in orders]
-    to_near_stages = [order[::-1][:-1] for order in orders]
     hidden_landed = [[[] for _ in stages] for stages in to_hidden_stages]
-    near_landed = [[[] for _ in stages] for stages in to_near_stages]
+    back_landed = [[[] for _ in stages] for stages in to_hidden_stages]
     cut = own // 2
     own_spans = ((cut, own - cut), (0, cut))
 
@@ -461,14 +497,14 @@
             n,
             orders[n][0],
             half,
-            lambda i, r, n=n: acc[n, i, r] + core_in[n, half + i, r].astype(jnp.float32),
+            lambda i, r, n=n: acc[n][i, r] + core_in[n][half + i, r].astype(jnp.float32),
             (pre_core[n][0].wait_recv, pre_core[n][1].wait_recv),
         )
-        loads[n] = local(pre_keep.at[pl.ds(n * quarter, half)], acc.at[n])
+        loads[n] = local(pre_keep.at[pl.ds(n * quarter, half)], acc[n])
     for n in range(2):
         loads[n].wait()
         pre_core[n][2].wait_recv()
-        fold(acc, n, half, lambda i, r: core_in[n, i, r].astype(jnp.float32))
+        fold(acc, n, half, lambda i, r: core_in[n][i, r].astype(jnp.float32))
     running[...] = jnp.zeros(running.shape, jnp.float32)
 
     count = half
@@ -481,7 +517,6 @@
             own_tokens.wait()
             for copy in arrivals:
                 copy.wait_recv()
-            given = local(panel, cotangent_out)
             for tile in range(tiles.shape[0]):
                 tiles[tile] = panel[:, tile * width : (tile + 1) * width]
             lax.fori_loop(marks[0], marks[1], product, 0)
@@ -500,10 +535,10 @@
             def act(index, r):
                 i = start + index
                 value, slope = gelu_and_slope(
-                    acc[n, i, r] + stage_in[base + i, r].astype(jnp.float32)
+                    acc[n][i, r] + stage_in[base + i, r].astype(jnp.float32)
                 )
                 own_hidden[n, i, r] = value.astype(jnp.bfloat16)
-                acc[n, i, r] = slope
+                slopes[n, i, r] = slope
 
             over(size, act)
             piece = own_hidden.at[n, pl.ds(start, size)]
@@ -527,50 +562,106 @@
 
             def step(i, r):
                 value = summed(2 * quarter + n * quarter + first + i, r)
-                core_in[n, first + i, r] = value.astype(jnp.bfloat16)
+                core_in[n][first + i, r] = value.astype(jnp.bfloat16)
 
             over(size, step)
-            source = core_in.at[n, pl.ds(first, size)]
+            source = core_in[n].at[pl.ds(first, size)]
             back_core[n].append(swap_core(n, (first, size), source, back_in))
     back_flight = [None, None]
+    move_on(hidden, hidden_landed, 0)
     for n in range(2):
         back_flight[n] = stage_send(
             n,
             orders[n][0],
             half,
             lambda i, r, n=n: summed(n * quarter + half + i, r)
-            + back_in[n, half + i, r].astype(jnp.float32),
+            + back_in[n][half + i, r].astype(jnp.float32),
             (back_core[n][0].wait_recv, back_core[n][1].wait_recv),
         )
     for n in range(2):
-        forward(hidden, n, to_hidden_stages[n], n * quarter, hidden_landed[n], 0)
-    for n in range(2):
         back_core[n][2].wait_recv()
 
         def begin(i, r):
-            back[n, i, r] = summed(n * quarter + i, r) + back_in[
-                n, i, r
-            ].astype(jnp.float32)
+            back[n][i, r] = summed(n * quarter + i, r) + back_in[n][i, r].astype(jnp.float32)
 
         over(half, begin)
-
-    def cross_landed(target, other, n, at, there, landed, number):
-        for start, size, copy in landed[number]:
-            cross(target.at[pl.ds(at + start, size)], other, there, start, size)
-
-    for n in range(2):
-        at = n * quarter
-        cross_landed(hidden, hidden, n, at, 2 * quarter + at, hidden_landed[n], 0)
+    for copies in back_core:
+        for copy in copies:
+            copy.wait_send()
+            started[:] = [other for other in started if other is not copy]
+
+    for number in range(1, len(to_hidden_stages[0])):
+        move_on(hidden, hidden_landed, number)
+    for copy in kept:
+        copy.wait()
+    kept.clear()
+    for copy in far_copies:
+        copy.wait_recv()
+    far_copies.clear()
+    filled_in = [
+        local(hidden.at[pl.ds(n * quarter, quarter)], hold.at[pl.ds(n * quarter, quarter)])
+        for n in range(4)
+    ]
+
+    out[...] = jnp.zeros(out.shape, jnp.float32)
+    pairs = GROUP // 2
+
+    def grad_copy(group):
+        here = pl.ds(group * pairs, pairs)
+        return pltpu.make_async_copy(sums.at[here], grads.at[here], grad_sems.at[group])
+
+    def forward_product(group, carry):
+        fetch_group(group).wait()
+        place = lax.rem(group, AHEAD)
+        for slot in range(GROUP):
+            k = group * GROUP + slot
+            grad = contract(hold[hidden_at[k]], tiles[source_at[k]], 0, 0) * alive[k]
+            rows = pl.ds(slot % 2 * width, width)
+            sums[group * pairs + slot // 2, rows] = grad.astype(jnp.bfloat16)
+        grad_copy(group).start()
+        for slot in range(GROUP):
+            chosen[slot] = blocks[place, slot]
+        total = None
+        for slot in range(GROUP):
+            source = hold[sorted_at[group, slot]]
+            term = contract(source, chosen[block_at[group, slot]], 1, 0)
+            total = term if slot == 0 else total * chain[group, slot] + term
+            parts[slot] = total
+
+        def flush(tile, inner):
+            end, factor = part_ends[group, tile], part_filled[group, tile]
+            for start in range(0, tokens, strip):
+                rows = pl.ds(start, strip)
+                out[tile, rows] = out[tile, rows] + parts[end, rows] * factor
+            return inner
+
+        lax.fori_loop(0, out.shape[0], flush, 0)
+
+        @pl.when(group + AHEAD < groups)
+        def _():
+            fetch_group(group + AHEAD).start()
+
+        return carry
+
+    for group in range(min(AHEAD, groups)):
+        fetch_group(group).start()
+    for copy in filled_in:
+        copy.wait()
+    steps = [0, groups // 6, groups // 2, 2 * groups // 3, 3 * groups // 4, groups]
+    lax.fori_loop(steps[0], steps[1], forward_product, 0)
 
     count = half
     for number, _ in enumerate(orders[0][1:]):
         flights = [
             pass_on(back, n, back_flight[n], count, orders[n][1 + number]) for n in range(2)
         ]
+        if number == 0:
+            lax.fori_loop(steps[1], steps[2], forward_product, 0)
         for n in range(2):
             fold_rest(back, n, back_flight[n], count)
         back_flight = flights
         count = count // 2
+    lax.fori_loop(steps[2], steps[3], forward_product, 0)
 
     for number, (start, size) in enumerate(own_spans):
         for n in range(2):
@@ -579,36 +670,57 @@
 
             def slope_times(index, r):
                 i = start + index
-                value = back[n, i, r] + stage_in[base + i, r].astype(jnp.float32)
-                own_back[n, i, r] = (value * acc[n, i, r]).astype(jnp.bfloat16)
+                value = back[n][i, r] + stage_in[base + i, r].astype(jnp.float32)
+                own_back[n, i, r] = (value * slopes[n, i, r]).astype(jnp.bfloat16)
 
             over(size, slope_times)
             piece = own_back.at[n, pl.ds(start, size)]
-            spread(near[n], n, to_near_stages[n], piece, start, size, 0, near_landed[n], 0)
-            cross(piece, far[n], 0, start, size)
-            kept.append(local(piece, near[n].at[pl.ds(start, size)]))
-
-    for number in range(1, len(to_hidden_stages[0])):
-        for n in range(2):
             at = n * quarter
-            forward(hidden, n, to_hidden_stages[n], at, hidden_landed[n], number)
-            cross_landed(hidden, hidden, n, at, 2 * quarter + at, hidden_landed[n], number)
-    for number in range(len(to_near_stages[0])):
-        for n in range(2):
-            forward(near[n], n, to_near_stages[n], 0, near_landed[n], number)
-            cross_landed(near[n], far[n], n, 0, 0, near_landed[n], number)
-    given.wait()
+            spread(
+                spread_back, n, to_hidden_stages[n], piece, start, size, at, back_landed[n], 0
+            )
+            cross(piece, spread_back, 2 * quarter + at, start, size)
+            kept.append(local(piece, spread_back.at[pl.ds(at + start, size)]))
+        if number == 0:
+            lax.fori_loop(steps[3], steps[4], forward_product, 0)
+    lax.fori_loop(steps[4], steps[5], forward_product, 0)
+
+    for tile in range(out.shape[0]):
+        panel[:, tile * width : (tile + 1) * width] = out[tile].astype(jnp.bfloat16)
+    shares = []
+    for distance in range(1, members):
+        device = {"col": lax.rem(col + distance, members)}
+        source = panel.at[pl.ds(distance * share, share)]
+        slot = pl.ds((distance - 1) * share, share)
+        shares.append(remote_to(source, landing.at[slot], device))
+    for number in range(len(to_hidden_stages[0])):
+        move_on(spread_back, back_landed, number)
+    for copy in shares:
+        copy.wait_recv()
+    for tile in range(out.shape[0]):
+        columns = slice(tile * width, (tile + 1) * width)
+        total = out[tile, 0:share]
+        for number in range(members - 1):
+            rows = slice(number * share, (number + 1) * share)
+            total = total + landing[rows, columns].astype(jnp.float32)
+        output[:, columns] = total
     for copy in kept:
         copy.wait()
     for copy in far_copies:
         copy.wait_recv()
+
+    def grads_done(group, carry):
+        grad_copy(group).wait()
+        return carry
+
+    lax.fori_loop(0, groups, grads_done, 0)
     for copy in started:
         copy.wait_send()
 
 
-def exchange(pre_keep, pre_send, cotangent, weights, source_at, carries, ends, filled):
+def exchange(pre_keep, pre_send, cotangent, weights, scalars):
     held, tokens, width = pre_keep.shape
-    columns = cotangent.shape[1]
+    share, columns = cotangent.shape
     slots = weights.shape[0]
     segments = 2 * held
     quarter = held // 2
@@ -617,48 +729,82 @@
     members = lax.axis_size("col")
     own = quarter >> (bits - 1)
     staged = 2 * (quarter - own)
-    copies = members - 1 + 12 + 8 * (bits - 1) + 16 * (quarter // own)
+    copies = 2 * (members - 1) + 12 + 8 * (bits - 1) + 16 * (quarter // own)
     wide, narrow = jnp.float32, jnp.bfloat16
-
-    def hbm(count):
-        return jax.ShapeDtypeStruct((count, tokens, width), narrow)
-
+    pair_shape = (slots // 2, 2 * width, width)
+    tiles = columns // width
+    out_shape = [jax.ShapeDtypeStruct((segments, tokens, width), narrow)] * 2
+    out_shape += [
+        jax.ShapeDtypeStruct(pair_shape, narrow),
+        jax.ShapeDtypeStruct((share, columns), wide),
+    ]
     return pl.pallas_call(
         functools.partial(exchange_kernel, (quarter, own, bits, members)),
-        in_specs=[pl.BlockSpec(memory_space=pltpu.SMEM)] * 4
+        in_specs=[pl.BlockSpec(memory_space=pltpu.SMEM)] * len(scalars)
         + [pl.BlockSpec(memory_space=pl.ANY)] * 4,
-        out_specs=[pl.BlockSpec(memory_space=pl.ANY)] * 6,
-        out_shape=[hbm(segments)]
-        + [hbm(half)] * 4
-        + [jax.ShapeDtypeStruct((tokens, columns), narrow)],
+        out_specs=[pl.BlockSpec(memory_space=pl.ANY)] * 3
+        + [pl.BlockSpec(memory_space=pltpu.VMEM)],
+        out_shape=out_shape,
         scratch_shapes=[
+            pltpu.VMEM((max(2 * half, GROUP), tokens, width), wide),
+            pltpu.VMEM((4 * quarter, tokens, width), narrow),
             pltpu.VMEM((2, half, tokens, width), wide),
-            pltpu.VMEM((2, quarter, tokens, width), narrow),
-            pltpu.VMEM((2, half, tokens, width), wide),
-            pltpu.VMEM((2, quarter, tokens, width), narrow),
             pltpu.VMEM((staged, tokens, width), narrow),
             pltpu.VMEM((2 * staged, tokens, width), narrow),
             pltpu.VMEM((2, own, tokens, width), narrow),
             pltpu.VMEM((2, own, tokens, width), narrow),
             pltpu.VMEM((tokens, columns), narrow),
-            pltpu.VMEM((columns // width, tokens, width), narrow),
+            pltpu.VMEM((tiles, tokens, width), narrow),
             pltpu.VMEM((AHEAD, GROUP, width, width), narrow),
             pltpu.VMEM((tokens, width), wide),
             pltpu.VMEM((slots, tokens, width), narrow),
-            pltpu.SemaphoreType.DMA((16,)),
+            pltpu.VMEM((2, own, tokens, width), wide),
+            pltpu.VMEM((tiles, tokens, width), wide),
+            pltpu.VMEM((tokens - share, columns), narrow),
+            pltpu.VMEM((GROUP, width, width), narrow),
+            pltpu.SemaphoreType.DMA((24,)),
             pltpu.SemaphoreType.DMA((AHEAD,)),
+            pltpu.SemaphoreType.DMA((slots // GROUP,)),
             pltpu.SemaphoreType.DMA((copies,)),
             pltpu.SemaphoreType.DMA((copies,)),
         ],
         compiler_params=pltpu.CompilerParams(
-            collective_id=1, has_side_effects=True, vmem_limit_bytes=VMEM_LIMIT
+            collective_id=1, has_side_effects=True, vmem_limit_bytes=EXCHANGE_LIMIT
         ),
         cost_estimate=pl.CostEstimate(
-            flops=8 * slots * tokens * width * width,
+            flops=24 * slots * tokens * width * width,
             bytes_accessed=30 * segments * tokens * width // 2,
             transcendentals=2 * own * tokens * width,
         ),
-    )(source_at, carries, ends, filled, pre_keep, pre_send, cotangent, weights)
+    )(*scalars, pre_keep, pre_send, cotangent, weights)
+
+
+def group_order(model, hidden, live, tiles):
+    slots = model.shape[0]
+    key = jnp.where(live > 0, model, tiles).reshape(-1, GROUP)
+    place = jnp.arange(GROUP, dtype=jnp.int32)
+    first = (key[:, None, :] < key[:, :, None]) | (
+        (key[:, None, :] == key[:, :, None]) & (place[None, :] < place[:, None])
+    )
+    rank = jnp.sum(first.astype(jnp.int32), axis=2)
+    chosen = rank[:, None, :] == place[None, :, None]
+
+    def pick(values):
+        return jnp.sum(jnp.where(chosen, values[:, None, :], 0), axis=2)
+
+    spot = jnp.broadcast_to(place[None, :], key.shape)
+    ordered = pick(key)
+    chain = jnp.concatenate(
+        [jnp.zeros_like(ordered[:, :1]), (ordered[:, 1:] == ordered[:, :-1]).astype(jnp.int32)],
+        axis=1,
+    ).astype(jnp.float32)
+    targets = jnp.arange(tiles, dtype=jnp.int32)
+    lasts = jnp.max(
+        jnp.where(ordered[:, None, :] == targets[None, :, None], spot[:, None, :], -1), axis=2
+    )
+    ordered_fields = [pick(hidden.reshape(-1, GROUP)), pick(spot), chain, jnp.maximum(lasts, 0)]
+    ordered_fields.append((lasts >= 0).astype(jnp.float32))
+    return ordered_fields
 
 
 RELAY_ROWS = 16
@@ -819,20 +965,15 @@
     )
     ends = jnp.maximum(lasts, 0)
     filled = (lasts >= 0).astype(jnp.float32)
-    hidden, near_a, near_b, far_a, far_b, cotangent_all = exchange(
-        pre_keep, pre_send, grad_out, weights_two, model_two, carries, ends, filled
-    )
-    orders = swap_orders()
-    last_a, last_b = swap(near_a, orders[0][0]), swap(near_b, orders[1][0])
-    grad_second, own_out, send_out = to_model(
-        cotangent_all, [hidden], weights_two, (model_two, hidden_two, live_two), members, False
-    )
-    far_last_a = swap(after(last_a, own_out), 0)
-    far_last_b = swap(after(last_b, own_out), 0)
-    grad_pre_parts = [near_a, last_a, near_b, last_b, far_a, far_last_a, far_b, far_last_b]
-    output = scatter_tokens(own_out, after(send_out, *grad_pre_parts))
+    alive_two = live_two.astype(jnp.float32)
+    scalars = [model_two, carries, ends, filled, hidden_two, alive_two]
+    scalars += group_order(model_two, hidden_two, live_two, grad_out.shape[1] // width)
+    _, grad_pre, grads_two, output = exchange(
+        pre_keep, pre_send, grad_out, weights_two, scalars
+    )
+    grad_pre_parts = [grad_pre]
     places_one = (model_one, hidden_one, live_one)
-    own_in, send_in = to_model(
+    own_in, send_in, grad_second = to_model(
         inputs_all,
         grad_pre_parts,
         weights_one,
@@ -840,7 +981,9 @@
         members,
         True,
         with_grads=False,
-    )
+        carried=grads_two,
+    )
+    grad_second = grad_second.reshape(second_blocks.shape[2:])
     grad_input = scatter_tokens(own_in, send_in)
     (grad_first,) = to_model(
         inputs_all,

time: 264 us -> 257 us (0.973)
  waiting for transfers between devices: 14.3 us -> 4.68 us
  starting transfers between devices: 11.1 us -> 3.88 us
  Pallas kernels: 229 us -> 234 us
  other arithmetic: 8.43 us -> 11.4 us
    pallas_call x1, Pallas kernels: 125 us -> 150 us  [exchange(): pl.pallas_call(functools.partial(exchange_kernel, (quarter, own, bits, me...]
    pallas_call x3 -> x2, Pallas kernels: 62.2 us -> 42.7 us  [to_model(): pl.pallas_call(kernel, grid_spec=pltpu.PrefetchScalarGridSpec(num_scalar_...]
    ppermute x6 -> x3, waiting for transfers between devices: 11.3 us -> 4.68 us  [shift(): lax.ppermute(values, 'col', [(s, (s + distance) % count) for s in range(c...]
    ppermute x4 -> x0, starting transfers between devices: 3.65 us -> none  [swap(): lax.ppermute(values, 'row', [(s, s ^ 1 << bit) for s in range(count)])]
    ppermute x6 -> x3, starting transfers between devices: 7.46 us -> 3.88 us  [shift(): lax.ppermute(values, 'col', [(s, (s + distance) % count) for s in range(c...]
    ppermute x4 -> x0, waiting for transfers between devices: 3 us -> none  [swap(): lax.ppermute(values, 'row', [(s, s ^ 1 << bit) for s in range(count)])]
  transfers between devices with their start and end apart: 10 -> 3, of which waited for: 3 -> 2; matrix products, arithmetic and copies ran while one was open for 1% -> 0% of each run, Pallas kernels for 24% -> 7%
where the time goes in v3:
time: 257 us; the launch traced here: 256 us
  Pallas kernels  234 us (91%)
  other arithmetic  11.4 us (4%)
  waiting for transfers between devices  4.68 us (2%)
  starting transfers between devices  3.88 us (2%)
    pallas_call x1, Pallas kernels, exchange(): pl.pallas_call(functools.partial(exchange_kernel, (quarter, own, bits, me...  150 us
    pallas_call x2, Pallas kernels, to_model(): pl.pallas_call(kernel, grid_spec=pltpu.PrefetchScalarGridSpec(num_scalar_...  42.7 us
    pallas_call x1, Pallas kernels, to_hidden(): pl.pallas_call(functools.partial(to_hidden_kernel, flipped), grid_spec=pl...  22.1 us
    pallas_call x1, Pallas kernels, relay_tokens(): pl.pallas_call(functools.partial(relay_kernel, members), in_specs=[pl.Blo...  19.2 us
  transfers between devices with their start and end apart: 3, of which 2 were waited for; matrix products, arithmetic and copies ran while one was open for 0% of the time, Pallas kernels for 7%

profile of v3, /device:TPU:12, one launch (start us, length us, event | category | flops | bytes accessed | tf_op | source)
XLA Modules:
  0.0 255.8 jit_solution(356490586917475652)
XLA Ops:
  0.7 0.7 compare_reduce_fusion
  1.4 0.7 compare_reduce_fusion.1
  2.1 0.8 subtract_reduce_fusion
  2.9 0.1 sub.60
  3.0 0.1 sub.61
  3.0 0.1 ge.39
  3.1 0.4 convert_reduce_fusion
  3.5 1.3 select_reduce_fusion
  4.8 0.3 select_reduce_fusion.4
  5.1 0.6 broadcast_maximum_fusion.refs_9_
  5.7 0.6 compare_convert_fusion.refs_10_
  6.3 0.1 slice_compare_fusion
  6.4 0.6 broadcast_select_fusion.1
  7.0 0.1 select_reduce_fusion.3
  7.1 0.6 broadcast_maximum_fusion.1.refs_2_
  7.7 0.6 compare_convert_fusion.1.refs_3_
  8.2 0.1 slice_compare_fusion.1
  8.3 0.6 convert_convert_fusion.1.refs_5_
  8.9 19.2 %shard_map.93.panel.refs_3_ = bf16[256,2048]{1,0:T(8,128)(2,1)} custom-call(bf16[64,2048]{1,0:T(8,128)(2,1)} %own_ref.1), custom_call_target="tpu_custom_call" | custom-call | tf_op jit(solution)/shard_map/pallas_call | solution.py:900
  28.1 0.7 convert_convert_fusion.refs_8_
  28.8 0.6 convert_element_type.49.refs_2_
  29.3 0.6 broadcast_select_fusion
  29.9 0.7 add_convert_fusion.refs_1_
  30.6 22.1 %shard_map.94 = (f32[64,256,128]{2,1,0:T(8,128)}, bf16[64,256,128]{2,1,0:T(8,128)(2,1)}) custom-call(s32[384]{0:T(512)} %get-tuple-element.39.source.refs_0_, s32[384]{0:T(512)} %get-tuple-element.33.target, bf16[256,2048]{1,0:T(8,128)(2,1)} %shard_map.93.panel.refs_3_, bf16[384,128,128]{2,1,0:T(8,128)(2,1)} %bitcast.5), custom_call_target="tpu_custom_call" | custom-call | flops 12884901888 | bytes 25165824 | tf_op jit(solution)/shard_map/pallas_call | solution.py:65
  52.7 150.2 %shard_map.95 = (bf16[128,256,128]{2,1,0:T(8,128)(2,1)}, bf16[128,256,128]{2,1,0:T(8,128)(2,1)}, bf16[192,256,128]{2,1,0:T(8,128)(2,1)}, f32[64,2048]{1,0:T(8,128)}) custom-call(s32[384]{0:T(512)} %get-tuple-element.40.refs_0_, f32[384]{0:T(512)} %add_convert_fusion.refs_1_, s32[128]{0:T(128)} %broadcast_maximum_fusion.1.refs_2_, ...), custom_call_target="tpu_custom_call" | custom-call | flops 38654705664 | bytes 62914560 | tf_op jit(solution)/shard_map/pallas_call | solution.py:741
  202.9 24.7 %shard_map.96 = (f32[64,2048]{1,0:T(8,128)}, bf16[64,2048]{1,0:T(8,128)(2,1)}, bf16[64,2048]{1,0:T(8,128)(2,1)}, bf16[64,2048]{1,0:T(8,128)(2,1)}, bf16[192,256,128]{2,1,0:T(8,128)(2,1)}) custom-call(s32[384]{0:T(512)} %get-tuple-element.39.source.refs_0_, s32[384]{0:T(512)} %get-tuple-element.34.refs_1_, s32[384]{0:T(512)} %convert_element_type.49.refs_2_, ...), custom_call_target="tpu_custom_call" | custom-call | flops 12884901888 | bytes 33554432 | tf_op jit(solution)/shard_map/pallas_call | solution.py:210
  227.6 0.6 collective-permute-start
  228.2 3.2 %collective-permute-start.1 = (bf16[64,2048]{1,0:T(8,128)(2,1)}, bf16[64,2048]{1,0:T(8,128)(2,1)S(1)}, u32[]{:S(2)}, u32[]{:S(2)}) collective-permute-start(bf16[64,2048]{1,0:T(8,128)(2,1)} %get-tuple-element.22), channel_id=1, source_target_pairs={{0,2},{1,3},{2,0},{3,1},{4,6},{5,7},{6,4},{7,5},{8,10},{9,11},{10,... | collective-permute-start | bytes 786440 | tf_op jit(solution)/shard_map/ppermute | solution.py:916
  231.4 0.0 collective-permute-start.2
  231.4 0.0 copy-start
  231.4 0.0 copy-start.1
  231.4 18.0 %shard_map.97 = bf16[384,128,128]{2,1,0:T(8,128)(2,1)} custom-call(s32[384]{0:T(512)} %get-tuple-element.39.source.refs_0_, s32[384]{0:T(512)} %get-tuple-element.34.refs_1_, s32[384]{0:T(512)} %convert_element_type.49.refs_2_, bf16[256,2048]{1,0:T(8,128)(2,1)} %shard_map.93.panel.refs_3_, bf16[128,256,128]{2,1,0:T(8,128)(2,1)} %get-tuple-element.24.refs_4_), custom_call_target="tpu_custom_call" | custom-call | flops 12884901888 | bytes 33554432 | tf_op jit(solution)/shard_map/pallas_call | solution.py:210
  249.4 0.0 collective-permute-done
  249.4 1.6 collective-permute-done.1
  251.1 3.0 %collective-permute-done.2 = bf16[64,2048]{1,0:T(8,128)(2,1)S(1)} collective-permute-done((bf16[64,2048]{1,0:T(8,128)(2,1)}, bf16[64,2048]{1,0:T(8,128)(2,1)S(1)}, u32[]{:S(2)}, u32[]{:S(2)}) %collective-permute-start.2) | collective-permute-done | bytes 262176 | tf_op jit(solution)/shard_map/ppermute | solution.py:916
  254.1 0.0 copy-done
  254.1 0.9 convert_add_fusion
  255.0 0.0 copy-done.1
  255.0 0.8 copy.11
  (2 shorter events, 0.0 us)
Async XLA Ops:
  227.6 21.9 %collective-permute-start = (bf16[64,2048]{1,0:T(8,128)(2,1)}, bf16[64,2048]{1,0:T(8,128)(2,1)S(1)}, u32[]{:S(2)}, u32[]{:S(2)}) collective-permute-start(bf16[64,2048]{1,0:T(8,128)(2,1)} %get-tuple-element.21), channel_id=1, source_target_pairs={{0,1},{1,2},{2,3},{3,0},{4,5},{5,6},{6,7},{7,4},{8,9},{9,10},{10,1... | collective-permute-start | bytes 786440 | tf_op jit(solution)/shard_map/ppermute | solution.py:916
  228.2 22.9 %collective-permute-start.1 = (bf16[64,2048]{1,0:T(8,128)(2,1)}, bf16[64,2048]{1,0:T(8,128)(2,1)S(1)}, u32[]{:S(2)}, u32[]{:S(2)}) collective-permute-start(bf16[64,2048]{1,0:T(8,128)(2,1)} %get-tuple-element.22), channel_id=1, source_target_pairs={{0,2},{1,3},{2,0},{3,1},{4,6},{5,7},{6,4},{7,5},{8,10},{9,11},{10,... | collective-permute-start | bytes 786440 | tf_op jit(solution)/shard_map/ppermute | solution.py:916
  231.4 22.7 %collective-permute-start.2 = (bf16[64,2048]{1,0:T(8,128)(2,1)}, bf16[64,2048]{1,0:T(8,128)(2,1)S(1)}, u32[]{:S(2)}, u32[]{:S(2)}) collective-permute-start(bf16[64,2048]{1,0:T(8,128)(2,1)} %get-tuple-element.23), channel_id=1, source_target_pairs={{0,3},{1,0},{2,1},{3,2},{4,7},{5,4},{6,5},{7,6},{8,11},{9,8},{10,9... | collective-permute-start | bytes 786440 | tf_op jit(solution)/shard_map/ppermute | solution.py:916
  231.4 22.7 %copy-start = (f32[64,2048]{1,0:T(8,128)S(1)}, f32[64,2048]{1,0:T(8,128)}, u32[]{:S(2)}) copy-start(f32[64,2048]{1,0:T(8,128)} %get-tuple-element.20) | copy-start | bytes 1572868
  231.4 23.6 %copy-start.1 = (f32[64,2048]{1,0:T(8,128)S(1)}, f32[64,2048]{1,0:T(8,128)}, u32[]{:S(2)}) copy-start(f32[64,2048]{1,0:T(8,128)} %get-tuple-element.47) | copy-start | bytes 1572868

commit v4 on v3

--- a/solution.py
+++ b/solution.py
@@ -9,7 +9,7 @@
 from jax.sharding import PartitionSpec as P
 
 FF = 65536
-CHUNK = 32
+CHUNK = 64
 VMEM_LIMIT = 58 * 1024 * 1024
 
 
@@ -27,52 +27,87 @@
     return ref[:, pl.ds(pl.multiple_of(index * width, width), width)]
 
 
-def to_hidden_kernel(flipped, source, target, panel, weights, keep, send, totals):
-    step = pl.program_id(0)
+OUT_PIECES = 4
+
+
+def longest_run(slots):
+    return next(run for run in (48, 40, 32, 16, 8, 4, 2, 1) if slots % run == 0)
+
+
+def to_hidden_kernel(source, target, panel, weights, keep, send, totals, blocks, rounded, *sems):
+    block_sems, keep_sems, send_sems = sems
+    slots, width, _ = weights.shape
     segments = totals.shape[0] - 1
     half = segments // 2
-    width = weights.shape[-1]
-
-    @pl.when(step == 0)
-    def _():
-        def clear(index, carry):
-            totals[index] = jnp.zeros(totals.shape[1:], jnp.float32)
+    run = longest_run(slots)
+    piece = half // OUT_PIECES
+
+    def load(number):
+        here = pl.ds(number * run, run)
+        return pltpu.make_async_copy(weights.at[here], blocks.at[here], block_sems.at[number])
+
+    def store(values, number, base, out, out_sems):
+        return pltpu.make_async_copy(
+            values.at[pl.ds(base + number * piece, piece)],
+            out.at[pl.ds(number * piece, piece)],
+            out_sems.at[number],
+        )
+
+    for number in range(slots // run):
+        load(number).start()
+
+    def clear(index, carry):
+        totals[index] = jnp.zeros(totals.shape[1:], jnp.float32)
+        return carry
+
+    lax.fori_loop(0, segments, clear, 0)
+
+    def add(number, carry):
+        load(number).wait()
+        for slot in range(run):
+            k = number * run + slot
+            totals[target[k]] += contract(lanes(panel, source[k], width), blocks[k], 1, 0)
+        return carry
+
+    lax.fori_loop(0, slots // run, add, 0)
+    for number in range(OUT_PIECES):
+        store(totals, number, 0, keep, keep_sems).start()
+    for number in range(OUT_PIECES):
+
+        def turn(index, carry):
+            at = number * piece + index
+            rounded[at] = totals[half + at].astype(jnp.bfloat16)
             return carry
 
-        lax.fori_loop(0, segments, clear, 0)
-
-    for slot in range(CHUNK):
-        k = step * CHUNK + slot
-        term = contract(
-            lanes(panel, source[k], width), weights[slot], 1, 1 if flipped else 0
-        )
-        totals[target[k]] += term
-
-    @pl.when(step == pl.num_programs(0) - 1)
-    def _():
-        def write(index, carry):
-            keep[index] = totals[index]
-            send[index] = totals[half + index].astype(jnp.bfloat16)
-            return carry
-
-        lax.fori_loop(0, half, write, 0)
-
-
-def to_hidden(panel, weights, source, target, segments, flipped):
+        lax.fori_loop(0, piece, turn, 0)
+        store(rounded, number, 0, send, send_sems).start()
+    for number in range(OUT_PIECES):
+        store(totals, number, 0, keep, keep_sems).wait()
+        store(rounded, number, 0, send, send_sems).wait()
+
+
+def to_hidden(panel, weights, source, target, segments):
     tokens = panel.shape[0]
     slots, width, _ = weights.shape
     half = segments // 2
     return pl.pallas_call(
-        functools.partial(to_hidden_kernel, flipped),
+        to_hidden_kernel,
         grid_spec=pltpu.PrefetchScalarGridSpec(
             num_scalar_prefetch=2,
-            grid=(slots // CHUNK,),
+            grid=(1,),
             in_specs=[
                 pl.BlockSpec(panel.shape, lambda s, a, b: (0, 0)),
-                pl.BlockSpec((CHUNK, width, width), lambda s, a, b: (s, 0, 0)),
+                pl.BlockSpec(memory_space=pl.ANY),
             ],
-            out_specs=[pl.BlockSpec((half, tokens, width), lambda s, a, b: (0, 0, 0))] * 2,
-            scratch_shapes=[pltpu.VMEM((segments + 1, tokens, width), jnp.float32)],
+            out_specs=[pl.BlockSpec(memory_space=pl.ANY)] * 2,
+            scratch_shapes=[
+                pltpu.VMEM((segments + 1, tokens, width), jnp.float32),
+                pltpu.VMEM((slots, width, width), jnp.bfloat16),
+                pltpu.VMEM((half, tokens, width), jnp.bfloat16),
+                pltpu.SemaphoreType.DMA((slots // longest_run(slots),)),
+                pltpu.SemaphoreType.DMA((OUT_PIECES,)),
+                pltpu.SemaphoreType.DMA((OUT_PIECES,)),
+            ],
         ),
         out_shape=[
             jax.ShapeDtypeStruct((half, tokens, width), jnp.float32),
@@ -99,7 +134,7 @@
         copy.wait()
 
 
-def to_model_kernel(transposed, pieces, with_sums, with_grads, carried, model_at, hidden_at, live, *refs):
+def to_model_kernel(transposed, pieces, with_sums, with_grads, carried, chunk, model_at, hidden_at, live, *refs):
     refs = list(refs)
     panel = refs.pop(0) if with_grads else None
     weights = refs.pop(0) if with_sums else None
@@ -122,8 +157,8 @@
     if carried:
         carried_out[...] = carried_in[...]
 
-    for slot in range(CHUNK):
-        k = step * CHUNK + slot
+    for slot in range(chunk):
+        k = step * chunk + slot
         model = model_at[k]
         values = hidden[hidden_at[k]]
         is_live = live[k] > 0
@@ -166,9 +201,10 @@
     slots, width, _ = weights.shape
     segments = columns // width
     share = tokens // members
+    chunk = next(count for count in (CHUNK, CHUNK // 2, 1) if slots % count == 0)
     hidden_count = sum(part.shape[0] for part in hidden_parts)
     pieces = len(hidden_parts)
-    chunk_spec = pl.BlockSpec((CHUNK, width, width), lambda s, a, b, c: (s, 0, 0))
+    chunk_spec = pl.BlockSpec((chunk, width, width), lambda s, a, b, c: (s, 0, 0))
     share_spec = pl.BlockSpec((share, columns), lambda s, a, b, c: (0, 0))
     operands, in_specs, out_specs, out_shape, scratch = [], [], [], [], []
     if with_grads:
@@ -193,7 +229,7 @@
     if carried is not None:
         extra = [carried]
         carried_spec = pl.BlockSpec(
-            (CHUNK // 2, 2 * width, width), lambda s, a, b, c: (s, 0, 0)
+            (chunk // 2, 2 * width, width), lambda s, a, b, c: (s, 0, 0)
         )
         extra_specs.append(carried_spec)
         out_specs.append(carried_spec)
@@ -205,13 +241,13 @@
             start = 3 + len(operands) + pieces + len(extra) + (1 if with_grads else 0) + 1
             if not isinstance(flat[start], (list, tuple)):
                 flat[start : start + members - 1] = [flat[start : start + members - 1]]
-        to_model_kernel(transposed, pieces, with_sums, with_grads, carried is not None, *flat)
+        to_model_kernel(transposed, pieces, with_sums, with_grads, carried is not None, chunk, *flat)
 
     return pl.pallas_call(
         kernel,
         grid_spec=pltpu.PrefetchScalarGridSpec(
             num_scalar_prefetch=3,
-            grid=(slots // CHUNK,),
+            grid=(slots // chunk,),
             in_specs=in_specs + [pl.BlockSpec(memory_space=pl.ANY)] * pieces + extra_specs,
             out_specs=out_specs,
             scratch_shapes=scratch,
@@ -952,10 +988,7 @@
     weights_one = first_blocks[0, 0]
     weights_two = second_blocks[0, 0]
 
-    inputs_all = relay_tokens(activations)
-    pre_keep, pre_send = to_hidden(
-        inputs_all, weights_one, model_one, target_one, col_tiles, False
-    )
+    inputs_all = gather_tokens(activations)
     same = (target_two[1:] == target_two[:-1]).astype(jnp.float32)
     carries = jnp.concatenate([jnp.zeros((1,), jnp.float32), same])
     numbers = jnp.arange(target_two.shape[0], dtype=jnp.int32)
@@ -968,12 +1001,14 @@
     alive_two = live_two.astype(jnp.float32)
     scalars = [model_two, carries, ends, filled, hidden_two, alive_two]
     scalars += group_order(model_two, hidden_two, live_two, grad_out.shape[1] // width)
+    source_one, target_one, scalars = lax.optimization_barrier((model_one, target_one, scalars))
+    pre_keep, pre_send = to_hidden(inputs_all, weights_one, source_one, target_one, col_tiles)
     _, grad_pre, grads_two, output = exchange(
         pre_keep, pre_send, grad_out, weights_two, scalars
     )
     grad_pre_parts = [grad_pre]
     places_one = (model_one, hidden_one, live_one)
-    own_in, send_in, grad_second = to_model(
+    own_in, send_in = to_model(
         inputs_all,
         grad_pre_parts,
         weights_one,
@@ -981,11 +1016,9 @@
         members,
         True,
         with_grads=False,
-        carried=grads_two,
     )
-    grad_second = grad_second.reshape(second_blocks.shape[2:])
     grad_input = scatter_tokens(own_in, send_in)
-    (grad_first,) = to_model(
+    grad_first, grad_second = to_model(
         inputs_all,
         after(grad_pre_parts, own_in, output),
         weights_one,
@@ -993,7 +1026,9 @@
         members,
         True,
         with_sums=False,
+        carried=grads_two,
     )
+    grad_second = grad_second.reshape(second_blocks.shape[2:])
     return (output, grad_input, grad_first[None, None], grad_second[None, None])
 
 

time: 257 us -> 243 us (0.946)
  Pallas kernels: 234 us -> 206 us
  waiting for transfers between devices: 4.68 us -> 10.3 us
  starting transfers between devices: 3.88 us -> 8.54 us
    pallas_call x2 -> x1, Pallas kernels: 41.3 us -> 18.5 us  [to_hidden(): pl.pallas_call(to_hidden_kernel, grid_spec=pltpu.PrefetchScalarGridSpec(n...]
    ppermute x3 -> x6, waiting for transfers between devices: 4.68 us -> 10.3 us  [shift(): lax.ppermute(values, 'col', [(s, (s + distance) % count) for s in range(c...]
    pallas_call x2, Pallas kernels: 42.7 us -> 37.3 us  [to_model(): pl.pallas_call(kernel, grid_spec=pltpu.PrefetchScalarGridSpec(num_scalar_...]
    ppermute x3 -> x6, starting transfers between devices: 3.88 us -> 8.54 us  [shift(): lax.ppermute(values, 'col', [(s, (s + distance) % count) for s in range(c...]
  transfers between devices with their start and end apart: 3 -> 6, of which waited for: 2 -> 3; matrix products, arithmetic and copies ran while one was open for 0% -> 5% of each run, Pallas kernels for 7% -> 9%
where the time goes in v4:
time: 243 us; the launch traced here: 240 us
  Pallas kernels  206 us (85%)
  other arithmetic  11.4 us (5%)
  waiting for transfers between devices  10.3 us (4%)
  starting transfers between devices  8.54 us (4%)
  local copies, waits for them, and re-layouts  3.1 us (1%)
    pallas_call x1, Pallas kernels, exchange(): pl.pallas_call(functools.partial(exchange_kernel, (quarter, own, bits, me...  150 us
    pallas_call x2, Pallas kernels, to_model(): pl.pallas_call(kernel, grid_spec=pltpu.PrefetchScalarGridSpec(num_scalar_...  37.3 us
    pallas_call x1, Pallas kernels, to_hidden(): pl.pallas_call(to_hidden_kernel, grid_spec=pltpu.PrefetchScalarGridSpec(n...  18.5 us
    ppermute x6, waiting for transfers between devices, shift(): lax.ppermute(values, 'col', [(s, (s + distance) % count) for s in range(c...  10.3 us
    ppermute x6, starting transfers between devices, shift(): lax.ppermute(values, 'col', [(s, (s + distance) % count) for s in range(c...  8.54 us
  transfers between devices with their start and end apart: 6, of which 3 were waited for; matrix products, arithmetic and copies ran while one was open for 5% of the time, Pallas kernels for 9%

profile of v4, /device:TPU:12, one launch (start us, length us, event | category | flops | bytes accessed | tf_op | source)
XLA Modules:
  0.0 240.4 jit_solution(14508184411120671504)
XLA Ops:
  0.6 2.7 %collective-permute-start.1 = (bf16[64,2048]{1,0:T(8,128)(2,1)}, bf16[64,2048]{1,0:T(8,128)(2,1)S(1)}, u32[]{:S(2)}, u32[]{:S(2)}) collective-permute-start(bf16[64,2048]{1,0:T(8,128)(2,1)} %param.6), channel_id=1, source_target_pairs={{0,2},{1,3},{2,0},{3,1},{4,6},{5,7},{6,4},{7,5},{8,10},{9,11},{10,... | collective-permute-start | bytes 786440 | tf_op jit(solution)/shard_map/ppermute | solution.py:952
  3.3 0.4 collective-permute-start
  3.7 1.6 collective-permute-start.2
  5.3 0.7 compare_reduce_fusion
  6.0 0.1 ge.41
  6.1 0.6 convert_convert_fusion.1.refs_5_
  6.7 0.7 compare_reduce_fusion.1
  7.4 0.8 subtract_reduce_fusion
  8.2 0.6 broadcast_select_fusion
  8.8 0.1 select_reduce_fusion.3
  8.9 0.1 slice_compare_fusion.1
  9.0 0.1 sub.64
  9.1 0.1 sub.65
  9.2 0.4 convert_reduce_fusion
  9.5 1.3 select_reduce_fusion
  10.8 0.1 slice_compare_fusion
  10.9 0.3 select_reduce_fusion.4
  11.2 0.6 compare_convert_fusion.refs_10_
  11.8 0.6 broadcast_maximum_fusion.refs_9_
  12.4 1.0 constant_dynamic-update-slice_fusion.3
  13.4 0.6 compare_convert_fusion.1.refs_3_
  14.0 0.6 broadcast_select_fusion.1
  14.5 0.6 broadcast_maximum_fusion.1.refs_2_
  15.1 0.7 convert_convert_fusion.refs_8_
  15.8 0.7 add_convert_fusion.refs_1_
  16.5 0.6 convert_element_type.49.refs_2_
  17.0 8.7 %collective-permute-done = bf16[64,2048]{1,0:T(8,128)(2,1)S(1)} collective-permute-done((bf16[64,2048]{1,0:T(8,128)(2,1)}, bf16[64,2048]{1,0:T(8,128)(2,1)S(1)}, u32[]{:S(2)}, u32[]{:S(2)}) %collective-permute-start) | collective-permute-done | bytes 262176 | tf_op jit(solution)/shard_map/ppermute | solution.py:952
  25.8 0.0 collective-permute-done.1
  25.8 0.2 collective-permute-done.2
  26.0 0.0 copy-start.2
  26.0 1.0 copy-done.2
  27.0 18.5 %shard_map.93 = (f32[64,256,128]{2,1,0:T(8,128)}, bf16[64,256,128]{2,1,0:T(8,128)(2,1)}) custom-call(s32[384]{0:T(512)} %get-tuple-element.40.source.refs_0_, s32[384]{0:T(512)} %get-tuple-element.41.target, bf16[256,2048]{1,0:T(8,128)(2,1)} %copy-done.2, bf16[384,128,128]{2,1,0:T(8,128)(2,1)} %bitcast.5), custom_call_target="tpu_custom_call" | custom-call | flops 12884901888 | bytes 25165824 | tf_op jit(solution)/shard_map/pallas_call | solution.py:93
  45.6 150.5 %shard_map.94 = (bf16[128,256,128]{2,1,0:T(8,128)(2,1)}, bf16[128,256,128]{2,1,0:T(8,128)(2,1)}, bf16[192,256,128]{2,1,0:T(8,128)(2,1)}, f32[64,2048]{1,0:T(8,128)}) custom-call(s32[384]{0:T(512)} %get-tuple-element.29.refs_0_, f32[384]{0:T(512)} %add_convert_fusion.refs_1_, s32[128]{0:T(128)} %broadcast_maximum_fusion.1.refs_2_, ...), custom_call_target="tpu_custom_call" | custom-call | flops 38654705664 | bytes 62914560 | tf_op jit(solution)/shard_map/pallas_call | solution.py:777
  196.1 15.7 %shard_map.95 = (f32[64,2048]{1,0:T(8,128)}, bf16[64,2048]{1,0:T(8,128)(2,1)}, bf16[64,2048]{1,0:T(8,128)(2,1)}, bf16[64,2048]{1,0:T(8,128)(2,1)}) custom-call(s32[384]{0:T(512)} %get-tuple-element.40.source.refs_0_, s32[384]{0:T(512)} %get-tuple-element.64.refs_1_, s32[384]{0:T(512)} %convert_element_type.49.refs_2_, bf16[384,128,128]{2,1,0:T(8,128)(2,1)} %bitcast.6, ...), custom_call_target="tpu_custom_call" | custom-call | flops 12884901888 | bytes 33554432 | tf_op jit(solution)/shard_map/pallas_call | solution.py:246
  211.8 0.1 collective-permute-start.3
  211.9 3.8 %collective-permute-start.4 = (bf16[64,2048]{1,0:T(8,128)(2,1)}, bf16[64,2048]{1,0:T(8,128)(2,1)S(1)}, u32[]{:S(2)}, u32[]{:S(2)}) collective-permute-start(bf16[64,2048]{1,0:T(8,128)(2,1)} %get-tuple-element.48), channel_id=1, source_target_pairs={{0,2},{1,3},{2,0},{3,1},{4,6},{5,7},{6,4},{7,5},{8,10},{9,11},{10,... | collective-permute-start | bytes 786440 | tf_op jit(solution)/shard_map/ppermute | solution.py:952
  215.7 0.0 collective-permute-start.5
  215.7 0.0 copy-start
  215.7 0.0 copy-start.1
  215.7 21.5 %shard_map.96 = (bf16[384,128,128]{2,1,0:T(8,128)(2,1)}, bf16[192,256,128]{2,1,0:T(8,128)(2,1)}) custom-call(s32[384]{0:T(512)} %get-tuple-element.40.source.refs_0_, s32[384]{0:T(512)} %get-tuple-element.64.refs_1_, s32[384]{0:T(512)} %convert_element_type.49.refs_2_, bf16[256,2048]{1,0:T(8,128)(2,1)} %copy-done.2, ...), custom_call_target="tpu_custom_call" | custom-call | flops 12884901888 | bytes 33554432 | tf_op jit(solution)/shard_map/pallas_call | solution.py:246
  237.2 0.0 collective-permute-done.3
  237.2 0.0 collective-permute-done.4
  237.3 1.4 collective-permute-done.5
  238.7 0.0 copy-done
  238.7 0.9 convert_add_fusion
  239.6 0.0 copy-done.1
  239.6 0.8 copy.14
  (5 shorter events, 0.1 us)
Async XLA Ops:
  0.6 25.1 %collective-permute-start.1 = (bf16[64,2048]{1,0:T(8,128)(2,1)}, bf16[64,2048]{1,0:T(8,128)(2,1)S(1)}, u32[]{:S(2)}, u32[]{:S(2)}) collective-permute-start(bf16[64,2048]{1,0:T(8,128)(2,1)} %param.6), channel_id=1, source_target_pairs={{0,2},{1,3},{2,0},{3,1},{4,6},{5,7},{6,4},{7,5},{8,10},{9,11},{10,... | collective-permute-start | bytes 786440 | tf_op jit(solution)/shard_map/ppermute | solution.py:952
  3.3 22.4 %collective-permute-start = (bf16[64,2048]{1,0:T(8,128)(2,1)}, bf16[64,2048]{1,0:T(8,128)(2,1)S(1)}, u32[]{:S(2)}, u32[]{:S(2)}) collective-permute-start(bf16[64,2048]{1,0:T(8,128)(2,1)} %param.6), channel_id=1, source_target_pairs={{0,3},{1,0},{2,1},{3,2},{4,7},{5,4},{6,5},{7,6},{8,11},{9,8},{10,9... | collective-permute-start | bytes 786440 | tf_op jit(solution)/shard_map/ppermute | solution.py:952
  3.7 22.2 %collective-permute-start.2 = (bf16[64,2048]{1,0:T(8,128)(2,1)}, bf16[64,2048]{1,0:T(8,128)(2,1)S(1)}, u32[]{:S(2)}, u32[]{:S(2)}) collective-permute-start(bf16[64,2048]{1,0:T(8,128)(2,1)} %param.6), channel_id=1, source_target_pairs={{0,1},{1,2},{2,3},{3,0},{4,5},{5,6},{6,7},{7,4},{8,9},{9,10},{10,1... | collective-permute-start | bytes 786440 | tf_op jit(solution)/shard_map/ppermute | solution.py:952
  26.0 1.0 copy-start.2
  211.8 25.4 %collective-permute-start.3 = (bf16[64,2048]{1,0:T(8,128)(2,1)}, bf16[64,2048]{1,0:T(8,128)(2,1)S(1)}, u32[]{:S(2)}, u32[]{:S(2)}) collective-permute-start(bf16[64,2048]{1,0:T(8,128)(2,1)} %get-tuple-element.47), channel_id=1, source_target_pairs={{0,1},{1,2},{2,3},{3,0},{4,5},{5,6},{6,7},{7,4},{8,9},{9,10},{10,1... | collective-permute-start | bytes 786440 | tf_op jit(solution)/shard_map/ppermute | solution.py:952
  211.9 25.4 %collective-permute-start.4 = (bf16[64,2048]{1,0:T(8,128)(2,1)}, bf16[64,2048]{1,0:T(8,128)(2,1)S(1)}, u32[]{:S(2)}, u32[]{:S(2)}) collective-permute-start(bf16[64,2048]{1,0:T(8,128)(2,1)} %get-tuple-element.48), channel_id=1, source_target_pairs={{0,2},{1,3},{2,0},{3,1},{4,6},{5,7},{6,4},{7,5},{8,10},{9,11},{10,... | collective-permute-start | bytes 786440 | tf_op jit(solution)/shard_map/ppermute | solution.py:952
  215.7 23.0 %collective-permute-start.5 = (bf16[64,2048]{1,0:T(8,128)(2,1)}, bf16[64,2048]{1,0:T(8,128)(2,1)S(1)}, u32[]{:S(2)}, u32[]{:S(2)}) collective-permute-start(bf16[64,2048]{1,0:T(8,128)(2,1)} %get-tuple-element.49), channel_id=1, source_target_pairs={{0,3},{1,0},{2,1},{3,2},{4,7},{5,4},{6,5},{7,6},{8,11},{9,8},{10,9... | collective-permute-start | bytes 786440 | tf_op jit(solution)/shard_map/ppermute | solution.py:952
  215.7 23.0 %copy-start = (f32[64,2048]{1,0:T(8,128)S(1)}, f32[64,2048]{1,0:T(8,128)}, u32[]{:S(2)}) copy-start(f32[64,2048]{1,0:T(8,128)} %get-tuple-element.46) | copy-start | bytes 1572868
  215.7 23.9 %copy-start.1 = (f32[64,2048]{1,0:T(8,128)S(1)}, f32[64,2048]{1,0:T(8,128)}, u32[]{:S(2)}) copy-start(f32[64,2048]{1,0:T(8,128)} %get-tuple-element.75) | copy-start | bytes 1572868

commit v5 on v4

--- a/solution.py
+++ b/solution.py
@@ -9,7 +9,7 @@
 from jax.sharding import PartitionSpec as P
 
 FF = 65536
-CHUNK = 64
+CHUNK = 96
 VMEM_LIMIT = 58 * 1024 * 1024
 
 
@@ -122,14 +122,20 @@
     )(source, target, panel, weights)
 
 
+FETCHES = 4
+
+
 def fetch(parts, hidden, sems):
     copies = []
     start = 0
-    for number, part in enumerate(parts):
-        count = part.shape[0]
-        copies.append(pltpu.make_async_copy(part, hidden.at[pl.ds(start, count)], sems.at[number]))
-        copies[-1].start()
-        start += count
+    for part in parts:
+        count = part.shape[0] // FETCHES
+        for number in range(FETCHES):
+            source = part.at[pl.ds(number * count, count)]
+            target = hidden.at[pl.ds(start, count)]
+            copies.append(pltpu.make_async_copy(source, target, sems.at[len(copies)]))
+            copies[-1].start()
+            start += count
     for copy in copies:
         copy.wait()
 
@@ -201,7 +207,7 @@
     slots, width, _ = weights.shape
     segments = columns // width
     share = tokens // members
-    chunk = next(count for count in (CHUNK, CHUNK // 2, 1) if slots % count == 0)
+    chunk = next(count for count in (CHUNK, 64, 32, 16, 1) if slots % count == 0)
     hidden_count = sum(part.shape[0] for part in hidden_parts)
     pieces = len(hidden_parts)
     chunk_spec = pl.BlockSpec((chunk, width, width), lambda s, a, b, c: (s, 0, 0))
@@ -223,7 +229,7 @@
         scratch.append(pltpu.VMEM((segments + 1, tokens, width), jnp.float32))
     scratch += [
         pltpu.VMEM((hidden_count, tokens, width), jnp.bfloat16),
-        pltpu.SemaphoreType.DMA((pieces,)),
+        pltpu.SemaphoreType.DMA((pieces * FETCHES,)),
     ]
     extra, extra_specs = [], []
     if carried is not None:
@@ -843,110 +849,6 @@
     return ordered_fields
 
 
-RELAY_ROWS = 16
-
-
-def relay_kernel(members, own_ref, all_ref, local_sem, send_sems, recv_sems):
-    share = own_ref.shape[0]
-    pieces = share // RELAY_ROWS
-    me = lax.axis_index("col")
-    hops = members - 1
-
-    def place(block, device, piece):
-        slot = (block - device + members) % members
-        return pl.ds(pl.multiple_of(slot * share + piece * RELAY_ROWS, RELAY_ROWS), RELAY_ROWS)
-
-    mine = pltpu.make_async_copy(own_ref, all_ref.at[pl.ds(0, share)], local_sem)
-    mine.start()
-    barrier = pltpu.get_barrier_semaphore()
-    for step in (1, -1):
-        inside = (me + step >= 0) & (me + step < members)
-
-        @pl.when(inside)
-        def _():
-            pl.semaphore_signal(
-                barrier,
-                inc=1,
-                device_id={"col": me + step},
-                device_id_type=pl.DeviceIdType.MESH,
-            )
-
-    pl.semaphore_wait(barrier, jnp.where((me > 0) & (me < members - 1), 2, 1))
-
-    def move(side, hop, piece):
-        step = 1 if side == 0 else -1
-        block = me - step * hop
-        target = jnp.clip(me + step, 0, members - 1)
-        block = jnp.clip(block, 0, members - 1)
-        if hop == 0:
-            source = own_ref.at[pl.ds(piece * RELAY_ROWS, RELAY_ROWS)]
-        else:
-            source = all_ref.at[place(block, me, piece)]
-        at = (side * hops + hop) * pieces + piece
-        return pltpu.make_async_remote_copy(
-            src_ref=source,
-            dst_ref=all_ref.at[place(block, target, piece)],
-            send_sem=send_sems.at[at],
-            recv_sem=recv_sems.at[at],
-            device_id={"col": target},
-            device_id_type=pl.DeviceIdType.MESH,
-        )
-
-    def exists(side, hop):
-        step = 1 if side == 0 else -1
-        block = me - step * hop
-        target = me + step
-        return (block >= 0) & (block < members) & (target >= 0) & (target < members)
-
-    def comes(side, hop):
-        step = 1 if side == 0 else -1
-        block = me - step * (hop + 1)
-        return (block >= 0) & (block < members)
-
-    for hop in range(members):
-        for piece in range(pieces):
-            for side in range(2):
-                if hop > 0:
-
-                    @pl.when(comes(side, hop - 1))
-                    def _():
-                        move(side, hop - 1, piece).wait_recv()
-
-                if hop < hops:
-
-                    @pl.when(exists(side, hop))
-                    def _():
-                        move(side, hop, piece).start()
-
-    for hop in range(hops):
-        for piece in range(pieces):
-            for side in range(2):
-
-                @pl.when(exists(side, hop))
-                def _():
-                    move(side, hop, piece).wait_send()
-
-    mine.wait()
-
-
-def relay_tokens(values):
-    members = lax.axis_size("col")
-    share, columns = values.shape
-    copies = 2 * (members - 1) * (share // RELAY_ROWS)
-    return pl.pallas_call(
-        functools.partial(relay_kernel, members),
-        in_specs=[pl.BlockSpec(memory_space=pl.ANY)],
-        out_specs=pl.BlockSpec(memory_space=pl.ANY),
-        out_shape=jax.ShapeDtypeStruct((members * share, columns), values.dtype),
-        scratch_shapes=[
-            pltpu.SemaphoreType.DMA,
-            pltpu.SemaphoreType.DMA((copies,)),
-            pltpu.SemaphoreType.DMA((copies,)),
-        ],
-        compiler_params=pltpu.CompilerParams(collective_id=2, has_side_effects=True),
-    )(values)
-
-
 def shift(values, distance):
     count = lax.axis_size("col")
     return lax.ppermute(values, "col", [(s, (s + distance) % count) for s in range(count)])

time: 243 us -> 242 us (level)
  no operation moved by 1% of the time
where the time goes in v5:
time: 242 us; the launch traced here: 240 us
  Pallas kernels  205 us (85%)
  other arithmetic  11.4 us (5%)
  waiting for transfers between devices  10.5 us (4%)
  starting transfers between devices  8.54 us (4%)
  local copies, waits for them, and re-layouts  3.1 us (1%)
    pallas_call x1, Pallas kernels, exchange(): pl.pallas_call(functools.partial(exchange_kernel, (quarter, own, bits, me...  150 us
    pallas_call x2, Pallas kernels, to_model(): pl.pallas_call(kernel, grid_spec=pltpu.PrefetchScalarGridSpec(num_scalar_...  36.5 us
    pallas_call x1, Pallas kernels, to_hidden(): pl.pallas_call(to_hidden_kernel, grid_spec=pltpu.PrefetchScalarGridSpec(n...  18.5 us
    ppermute x6, waiting for transfers between devices, shift(): lax.ppermute(values, 'col', [(s, (s + distance) % count) for s in range(c...  10.5 us
    ppermute x6, starting transfers between devices, shift(): lax.ppermute(values, 'col', [(s, (s + distance) % count) for s in range(c...  8.54 us
  transfers between devices with their start and end apart: 6, of which 3 were waited for; matrix products, arithmetic and copies ran while one was open for 5% of the time, Pallas kernels for 9%

profile of v5, /device:TPU:12, one launch (start us, length us, event | category | flops | bytes accessed | tf_op | source)
XLA Modules:
  0.0 239.8 jit_solution(14354546093653574469)
XLA Ops:
  0.6 2.7 %collective-permute-start.1 = (bf16[64,2048]{1,0:T(8,128)(2,1)}, bf16[64,2048]{1,0:T(8,128)(2,1)S(1)}, u32[]{:S(2)}, u32[]{:S(2)}) collective-permute-start(bf16[64,2048]{1,0:T(8,128)(2,1)} %param.6), channel_id=1, source_target_pairs={{0,2},{1,3},{2,0},{3,1},{4,6},{5,7},{6,4},{7,5},{8,10},{9,11},{10,... | collective-permute-start | bytes 786440 | tf_op jit(solution)/shard_map/ppermute | solution.py:854
  3.3 0.4 collective-permute-start
  3.7 1.6 collective-permute-start.2
  5.3 0.7 compare_reduce_fusion
  6.0 0.1 ge.41
  6.1 0.6 convert_convert_fusion.1.refs_5_
  6.7 0.7 compare_reduce_fusion.1
  7.4 0.8 subtract_reduce_fusion
  8.2 0.6 broadcast_select_fusion
  8.8 0.1 select_reduce_fusion.3
  8.9 0.1 slice_compare_fusion.1
  9.0 0.1 sub.64
  9.1 0.1 sub.65
  9.2 0.4 convert_reduce_fusion
  9.5 1.3 select_reduce_fusion
  10.8 0.1 slice_compare_fusion
  10.9 0.3 select_reduce_fusion.4
  11.2 0.6 compare_convert_fusion.refs_10_
  11.8 0.6 broadcast_maximum_fusion.refs_9_
  12.4 1.0 constant_dynamic-update-slice_fusion.3
  13.4 0.6 compare_convert_fusion.1.refs_3_
  14.0 0.6 broadcast_select_fusion.1
  14.5 0.6 broadcast_maximum_fusion.1.refs_2_
  15.1 0.7 convert_convert_fusion.refs_8_
  15.8 0.7 add_convert_fusion.refs_1_
  16.5 0.6 convert_element_type.49.refs_2_
  17.0 8.7 %collective-permute-done = bf16[64,2048]{1,0:T(8,128)(2,1)S(1)} collective-permute-done((bf16[64,2048]{1,0:T(8,128)(2,1)}, bf16[64,2048]{1,0:T(8,128)(2,1)S(1)}, u32[]{:S(2)}, u32[]{:S(2)}) %collective-permute-start) | collective-permute-done | bytes 262176 | tf_op jit(solution)/shard_map/ppermute | solution.py:854
  25.8 0.0 collective-permute-done.1
  25.8 0.2 collective-permute-done.2
  26.0 0.0 copy-start.2
  26.0 1.0 copy-done.2
  27.0 18.5 %shard_map.93 = (f32[64,256,128]{2,1,0:T(8,128)}, bf16[64,256,128]{2,1,0:T(8,128)(2,1)}) custom-call(s32[384]{0:T(512)} %get-tuple-element.40.source.refs_0_, s32[384]{0:T(512)} %get-tuple-element.41.target, bf16[256,2048]{1,0:T(8,128)(2,1)} %copy-done.2, bf16[384,128,128]{2,1,0:T(8,128)(2,1)} %bitcast.5), custom_call_target="tpu_custom_call" | custom-call | flops 12884901888 | bytes 25165824 | tf_op jit(solution)/shard_map/pallas_call | solution.py:93
  45.6 150.5 %shard_map.94 = (bf16[128,256,128]{2,1,0:T(8,128)(2,1)}, bf16[128,256,128]{2,1,0:T(8,128)(2,1)}, bf16[192,256,128]{2,1,0:T(8,128)(2,1)}, f32[64,2048]{1,0:T(8,128)}) custom-call(s32[384]{0:T(512)} %get-tuple-element.29.refs_0_, f32[384]{0:T(512)} %add_convert_fusion.refs_1_, s32[128]{0:T(128)} %broadcast_maximum_fusion.1.refs_2_, ...), custom_call_target="tpu_custom_call" | custom-call | flops 38654705664 | bytes 62914560 | tf_op jit(solution)/shard_map/pallas_call | solution.py:783
  196.1 15.2 %shard_map.95 = (f32[64,2048]{1,0:T(8,128)}, bf16[64,2048]{1,0:T(8,128)(2,1)}, bf16[64,2048]{1,0:T(8,128)(2,1)}, bf16[64,2048]{1,0:T(8,128)(2,1)}) custom-call(s32[384]{0:T(512)} %get-tuple-element.40.source.refs_0_, s32[384]{0:T(512)} %get-tuple-element.64.refs_1_, s32[384]{0:T(512)} %convert_element_type.49.refs_2_, bf16[384,128,128]{2,1,0:T(8,128)(2,1)} %bitcast.6, ...), custom_call_target="tpu_custom_call" | custom-call | flops 12884901888 | bytes 33554432 | tf_op jit(solution)/shard_map/pallas_call | solution.py:252
  211.3 0.1 collective-permute-start.3
  211.3 3.8 %collective-permute-start.4 = (bf16[64,2048]{1,0:T(8,128)(2,1)}, bf16[64,2048]{1,0:T(8,128)(2,1)S(1)}, u32[]{:S(2)}, u32[]{:S(2)}) collective-permute-start(bf16[64,2048]{1,0:T(8,128)(2,1)} %get-tuple-element.48), channel_id=1, source_target_pairs={{0,2},{1,3},{2,0},{3,1},{4,6},{5,7},{6,4},{7,5},{8,10},{9,11},{10,... | collective-permute-start | bytes 786440 | tf_op jit(solution)/shard_map/ppermute | solution.py:854
  215.1 0.0 collective-permute-start.5
  215.1 0.0 copy-start
  215.1 0.0 copy-start.1
  215.1 21.3 %shard_map.96 = (bf16[384,128,128]{2,1,0:T(8,128)(2,1)}, bf16[192,256,128]{2,1,0:T(8,128)(2,1)}) custom-call(s32[384]{0:T(512)} %get-tuple-element.40.source.refs_0_, s32[384]{0:T(512)} %get-tuple-element.64.refs_1_, s32[384]{0:T(512)} %convert_element_type.49.refs_2_, bf16[256,2048]{1,0:T(8,128)(2,1)} %copy-done.2, ...), custom_call_target="tpu_custom_call" | custom-call | flops 12884901888 | bytes 33554432 | tf_op jit(solution)/shard_map/pallas_call | solution.py:252
  236.4 0.0 collective-permute-done.3
  236.4 0.0 collective-permute-done.4
  236.4 1.7 collective-permute-done.5
  238.1 0.0 copy-done
  238.1 0.9 convert_add_fusion
  239.0 0.0 copy-done.1
  239.0 0.8 copy.14
  (5 shorter events, 0.1 us)
Async XLA Ops:
  0.6 25.1 %collective-permute-start.1 = (bf16[64,2048]{1,0:T(8,128)(2,1)}, bf16[64,2048]{1,0:T(8,128)(2,1)S(1)}, u32[]{:S(2)}, u32[]{:S(2)}) collective-permute-start(bf16[64,2048]{1,0:T(8,128)(2,1)} %param.6), channel_id=1, source_target_pairs={{0,2},{1,3},{2,0},{3,1},{4,6},{5,7},{6,4},{7,5},{8,10},{9,11},{10,... | collective-permute-start | bytes 786440 | tf_op jit(solution)/shard_map/ppermute | solution.py:854
  3.3 22.4 %collective-permute-start = (bf16[64,2048]{1,0:T(8,128)(2,1)}, bf16[64,2048]{1,0:T(8,128)(2,1)S(1)}, u32[]{:S(2)}, u32[]{:S(2)}) collective-permute-start(bf16[64,2048]{1,0:T(8,128)(2,1)} %param.6), channel_id=1, source_target_pairs={{0,3},{1,0},{2,1},{3,2},{4,7},{5,4},{6,5},{7,6},{8,11},{9,8},{10,9... | collective-permute-start | bytes 786440 | tf_op jit(solution)/shard_map/ppermute | solution.py:854
  3.7 22.2 %collective-permute-start.2 = (bf16[64,2048]{1,0:T(8,128)(2,1)}, bf16[64,2048]{1,0:T(8,128)(2,1)S(1)}, u32[]{:S(2)}, u32[]{:S(2)}) collective-permute-start(bf16[64,2048]{1,0:T(8,128)(2,1)} %param.6), channel_id=1, source_target_pairs={{0,1},{1,2},{2,3},{3,0},{4,5},{5,6},{6,7},{7,4},{8,9},{9,10},{10,1... | collective-permute-start | bytes 786440 | tf_op jit(solution)/shard_map/ppermute | solution.py:854
  26.0 1.0 copy-start.2
  211.3 25.2 %collective-permute-start.3 = (bf16[64,2048]{1,0:T(8,128)(2,1)}, bf16[64,2048]{1,0:T(8,128)(2,1)S(1)}, u32[]{:S(2)}, u32[]{:S(2)}) collective-permute-start(bf16[64,2048]{1,0:T(8,128)(2,1)} %get-tuple-element.47), channel_id=1, source_target_pairs={{0,1},{1,2},{2,3},{3,0},{4,5},{5,6},{6,7},{7,4},{8,9},{9,10},{10,1... | collective-permute-start | bytes 786440 | tf_op jit(solution)/shard_map/ppermute | solution.py:854
  211.3 25.1 %collective-permute-start.4 = (bf16[64,2048]{1,0:T(8,128)(2,1)}, bf16[64,2048]{1,0:T(8,128)(2,1)S(1)}, u32[]{:S(2)}, u32[]{:S(2)}) collective-permute-start(bf16[64,2048]{1,0:T(8,128)(2,1)} %get-tuple-element.48), channel_id=1, source_target_pairs={{0,2},{1,3},{2,0},{3,1},{4,6},{5,7},{6,4},{7,5},{8,10},{9,11},{10,... | collective-permute-start | bytes 786440 | tf_op jit(solution)/shard_map/ppermute | solution.py:854
  215.1 23.0 %collective-permute-start.5 = (bf16[64,2048]{1,0:T(8,128)(2,1)}, bf16[64,2048]{1,0:T(8,128)(2,1)S(1)}, u32[]{:S(2)}, u32[]{:S(2)}) collective-permute-start(bf16[64,2048]{1,0:T(8,128)(2,1)} %get-tuple-element.49), channel_id=1, source_target_pairs={{0,3},{1,0},{2,1},{3,2},{4,7},{5,4},{6,5},{7,6},{8,11},{9,8},{10,9... | collective-permute-start | bytes 786440 | tf_op jit(solution)/shard_map/ppermute | solution.py:854
  215.1 23.0 %copy-start = (f32[64,2048]{1,0:T(8,128)S(1)}, f32[64,2048]{1,0:T(8,128)}, u32[]{:S(2)}) copy-start(f32[64,2048]{1,0:T(8,128)} %get-tuple-element.46) | copy-start | bytes 1572868
  215.1 23.9 %copy-start.1 = (f32[64,2048]{1,0:T(8,128)S(1)}, f32[64,2048]{1,0:T(8,128)}, u32[]{:S(2)}) copy-start(f32[64,2048]{1,0:T(8,128)} %get-tuple-element.75) | copy-start | bytes 1572868
